TPU v7x, 256 devices: a whole 4x4x8 slice. The times are simulated.
256 devices in a mesh: dp: 8 (over x, core), head: 32 (over y, z).
Axes of the slice: x: 4, y: 4, z: 8, core: 2. Of those that a mesh axis runs over, the one named last changes fastest.
Arguments:
- q_latent: bfloat16 [512, 1536], P('dp'), may hold values from -6 to 6
- w_qnope: bfloat16 [1536, 16384], P('dp', 'head'), may hold values from -0.15625 to 0.15625
- w_qrope: bfloat16 [1536, 8192], P('dp', 'head'), may hold values from -0.15625 to 0.15625
- w_uk: bfloat16 [128, 128, 512], P('head'), may hold values from -0.5 to 0.5
- w_uv: bfloat16 [128, 512, 128], P('head'), may hold values from -0.25 to 0.25
- w_out: bfloat16 [128, 128, 7168], P('head', 'dp'), may hold values from -0.09375 to 0.09375
- cache_latent: bfloat16 [16384, 128, 512], P(('dp', 'head')), may hold values from -210 to 210
- cache_rope: bfloat16 [16384, 64, 128], P(('dp', 'head')), may hold values from -6 to 6
- new_latent: bfloat16 [512, 512], P(('dp', 'head')), may hold values from -6 to 6
- new_rope: bfloat16 [512, 64], P(('dp', 'head')), may hold values from -6 to 6
- lengths: int32 [512], P('dp'), may hold values from 1 to 4096, as said below
- page_table: int32 [512, 32], P(('dp', 'head')), may hold values from 0 to 63, as said below
Outputs:
- mixed: bfloat16 [512, 7168], P('dp', 'head')
Inputs may be any that keep to these rules, and one draw needn't show every extreme that they name: `lengths`: each row of one device has at most 4096 cached tokens; some row holds exactly 4096. `page_table`: the entries of the 2 rows of one device together name each of its 64 pool pages once.
All inputs are finite; a program needn't handle non-finite values.
Results may differ from a plain program's by a relative error of at most 0.022.
Values may be sent and summed in bfloat16 or wider, within the bound.
No kernel may reach another device: no remote copies, remote signals or barrier semaphores. Data moves between devices by JAX's collectives and lax.ppermute only.
A program may use at most 128 MiB of HBM per device.

v0:
```python
import jax
import jax.numpy as jnp
from jax import lax
from jax.sharding import PartitionSpec as P

BLOCK_PAGES = 4


def rotate(x, pos):
    half = x.shape[-1] // 2
    freq = 10000.0 ** (-2.0 * jnp.arange(half, dtype=jnp.float32) / (2 * half))
    angle = pos.astype(jnp.float32)[:, None, None] * freq
    first = x[..., :half]
    second = x[..., half:]
    return jnp.concatenate(
        [
            first * jnp.cos(angle) - second * jnp.sin(angle),
            second * jnp.cos(angle) + first * jnp.sin(angle),
        ],
        axis=-1,
    )


def body(
    q_latent,
    w_qnope,
    w_qrope,
    w_uk,
    w_uv,
    w_out,
    cache_latent,
    cache_rope,
    new_latent,
    new_rope,
    lengths,
    page_table,
):
    rows_group = q_latent.shape[0]
    head_local = w_uk.shape[0]
    nope_dim = w_uk.shape[1]
    latent_dim = w_uk.shape[2]
    rope_dim = cache_rope.shape[1]
    page_size = cache_latent.shape[1]
    own_rows = page_table.shape[0]
    page_slots = page_table.shape[1]
    head_count = lax.axis_size("head")
    all_heads = head_local * head_count
    scale = 1.0 / (nope_dim + rope_dim) ** 0.5
    q_nope = jnp.dot(
        q_latent,
        lax.all_gather(w_qnope, "dp", axis=0, tiled=True),
        preferred_element_type=jnp.float32,
    )
    q_pe = jnp.dot(
        q_latent,
        lax.all_gather(w_qrope, "dp", axis=0, tiled=True),
        preferred_element_type=jnp.float32,
    )
    q_nope = q_nope.astype(jnp.bfloat16).reshape(rows_group, head_local, nope_dim)
    q_abs = jnp.einsum("rhn,hnl->rhl", q_nope, w_uk, preferred_element_type=jnp.float32).astype(
        jnp.bfloat16
    )
    q_abs = q_abs.reshape(rows_group, head_local * latent_dim)
    q_rot = rotate(q_pe.reshape(rows_group, head_local, rope_dim), lengths).astype(jnp.bfloat16)
    q_rot = q_rot.reshape(rows_group, head_local * rope_dim)
    got_abs, got_rot = (
        lax.all_to_all(q_abs, "head", split_axis=0, concat_axis=1, tiled=True),
        lax.all_to_all(q_rot, "head", split_axis=0, concat_axis=1, tiled=True),
    )
    got_abs = got_abs.reshape(own_rows, all_heads, latent_dim)
    got_rot = got_rot.reshape(own_rows, all_heads, rope_dim)
    own_lengths = lax.dynamic_slice_in_dim(lengths, lax.axis_index("head") * own_rows, own_rows)
    block = BLOCK_PAGES
    keys = block * page_size
    blocks = page_slots // block

    def fetch(index):
        chosen = lax.dynamic_slice_in_dim(page_table, index * block, block, 1)
        latent_block = cache_latent[chosen].reshape(own_rows, keys, latent_dim)
        rope_block = cache_rope[chosen]
        return (latent_block, rope_block)

    def score_block(index, scores):
        latent_block, rope_block = fetch(index)
        part_latent = jnp.einsum(
            "rhl,rkl->rhk", got_abs, latent_block, preferred_element_type=jnp.float32
        )
        part_rope = jnp.einsum(
            "rhe,rbek->rhbk", got_rot, rope_block, preferred_element_type=jnp.float32
        )
        block_scores = (part_latent + part_rope.reshape(own_rows, all_heads, keys)) * scale
        position = index * keys + jnp.arange(keys)
        block_scores = jnp.where(
            position[None, None, :] < own_lengths[:, None, None], block_scores, -jnp.inf
        )
        return lax.dynamic_update_slice_in_dim(scores, block_scores, index * keys, 2)

    scores = jnp.full((own_rows, all_heads, page_slots * page_size), -jnp.inf, jnp.float32)
    scores = lax.fori_loop(0, blocks, score_block, scores)
    score_new = (
        jnp.einsum("rhl,rl->rh", got_abs, new_latent, preferred_element_type=jnp.float32)
        + jnp.einsum("rhe,re->rh", got_rot, new_rope, preferred_element_type=jnp.float32)
    ) * scale
    top = jnp.maximum(jnp.max(scores, axis=2), score_new)
    weights = jnp.exp(scores - top[:, :, None])
    weight_new = jnp.exp(score_new - top)
    total = jnp.sum(weights, axis=2) + weight_new
    probs = (weights / total[:, :, None]).astype(jnp.bfloat16)
    prob_new = (weight_new / total).astype(jnp.bfloat16)

    def value_block(index, summed):
        latent_block, rope_block = fetch(index)
        block_probs = lax.dynamic_slice_in_dim(probs, index * keys, keys, 2)
        return summed + jnp.einsum(
            "rhk,rkl->rhl", block_probs, latent_block, preferred_element_type=jnp.float32
        )

    summed = jnp.einsum("rh,rl->rhl", prob_new, new_latent, preferred_element_type=jnp.float32)
    summed = lax.fori_loop(0, blocks, value_block, summed)
    attn = summed.astype(jnp.bfloat16).reshape(own_rows, all_heads * latent_dim)
    back = lax.all_to_all(attn, "head", split_axis=1, concat_axis=0, tiled=True)
    values = jnp.einsum(
        "rhl,hlv->rhv",
        back.reshape(rows_group, head_local, latent_dim),
        w_uv,
        preferred_element_type=jnp.float32,
    ).astype(jnp.bfloat16)
    dp_count = lax.axis_size("dp")
    width_part = w_out.shape[2] // head_count
    spread = lax.all_to_all(values, "dp", split_axis=2, concat_axis=0, tiled=True)
    spread = spread.reshape(dp_count, rows_group, head_local, spread.shape[2])
    panel = w_out.reshape(head_local, w_out.shape[1], head_count, width_part)
    term = jnp.einsum("ashv,hvcw->acsw", spread, panel, preferred_element_type=jnp.float32)
    term = term.reshape(dp_count * head_count * rows_group, width_part)
    mixed = lax.psum_scatter(term, ("dp", "head"), scatter_dimension=0, tiled=True)
    return mixed.astype(jnp.bfloat16)


def solution(mesh):
    in_specs = (
        P("dp", None),
        P("dp", "head"),
        P("dp", "head"),
        P("head", None, None),
        P("head", None, None),
        P("head", "dp", None),
        P(("dp", "head"), None, None),
        P(("dp", "head"), None, None),
        P(("dp", "head"), None),
        P(("dp", "head"), None),
        P("dp"),
        P(("dp", "head"), None),
    )
    out_specs = P("dp", "head")
    return jax.shard_map(body, mesh=mesh, in_specs=in_specs, out_specs=out_specs, check_vma=False)
```

profile of v0, /device:TPU:8, one launch (start us, length us, event | category | flops | bytes accessed | tf_op | source)
XLA Modules:
  0.0 1505.7 jit_solution(1781424772751977843)
XLA Ops:
  7.9 13.9 all_gather.7
  24.4 11.7 all-to-all-start.1
  36.1 3.0 all-gather.2.cloned.1.call-done
  42.3 2.5 all-to-all-done.1
  44.8 7.5 all-to-all-start
  52.8 11.1 all-to-all-done
  66.4 60.7 %while.26 = (s32[]{:T(128)}, f32[2,128,4096]{1,2,0:T(8,128)}, s32[2]{0:T(128)S(1)}, s32[2,32]{1,0:T(2,128)S(1)}, bf16[64,128,512]{2,1,0:T(8,128)(2,1)}, /*index=...) while((s32[]{:T(128)}, f32[2,128,4096]{1,2,0:T(8,128)}, ...), condition=%wide.region_1.2_spmd, body=%wide.region_0.1_spmd.sunk | while | flops 151390752 | bytes 5417437 | solution.py:99
  68.7 4.0 gather_fusion.1
  76.3 4.0 gather_fusion.1
  83.9 4.0 gather_fusion.1
  91.5 4.0 gather_fusion.1
  99.0 4.0 gather_fusion.1
  106.6 4.0 gather_fusion.1
  114.2 4.0 gather_fusion.1
  121.8 4.0 gather_fusion.1
  127.0 2.7 reduce_max.9
  129.8 5.7 copy.42
  135.6 3.1 fusion.8
  141.2 43.9 %while.27 = (s32[]{:T(128)}, f32[2,128,512]{2,1,0:T(8,128)S(1)}, bf16[2,128,4096]{2,1,0:T(8,128)(2,1)}, s32[2,32]{1,0:T(2,128)S(1)}, bf16[64,128,512]{2,1,0:T(8,...) while((s32[]{:T(128)}, f32[2,128,512]{2,1,0:T(8,128)S(1)}, ...), condition=%wide.region_5.6_spmd, body=%wide.region_4.5_spmd.sunk | while | flops 134349856 | bytes 4460953 | solution.py:119
  141.4 4.0 gather_fusion.2
  146.9 4.0 gather_fusion.2
  152.4 4.0 gather_fusion.2
  157.8 4.0 gather_fusion.2
  163.3 4.0 gather_fusion.2
  168.8 4.0 gather_fusion.2
  174.3 4.0 gather_fusion.2
  179.8 4.0 gather_fusion.2
  185.6 16.4 %all_to_all.60 = bf16[2,32,2048]{2,0,1:T(2,128)(2,1)S(1)} all-to-all(bf16[2,32,2048]{2,0,1:T(2,128)(2,1)S(1)} %copy.43), channel_id=1, replica_groups=mesh['dp'=8,'head'=32] {'head'}, dimensions={1} | all-to-all | bytes 524288 | tf_op jit(solution)/shard_map/all_to_all | solution.py:121
  203.3 3.3 all-to-all-start.3
  208.4 3.8 all-to-all-done.3
  212.4 8.1 fusion.12
  220.5 1276.9 %reduce-scatter.2.cloned.1.call-done = f32[64,224]{1,0:T(8,128)} async-done(((f32[16384,224]{1,0:T(8,128)}), f32[64,224]{1,0:T(8,128)}) %reduce-scatter.2.cloned.1.call-update) | async-done | bytes 57360 | tf_op jit(solution)/shard_map/reduce_scatter | solution.py:135
  (152 shorter events, 57.7 us)
Async XLA Ops:
  6.5 34.5 %copy-start = (bf16[4,128,512]{2,1,0:T(8,128)(2,1)S(1)}, bf16[4,128,512]{2,1,0:T(8,128)(2,1)}, u32[]{:S(2)}) copy-start(bf16[4,128,512]{2,1,0:T(8,128)(2,1)} %param.19) | copy-start | bytes 1572868
  6.5 45.8 %copy-start.7 = (s32[64]{0:T(128)S(1)}, s32[64]{0:T(128)}, u32[]{:S(2)}) copy-start(s32[64]{0:T(128)} %param.26) | copy-start | bytes 772
  6.5 45.9 %copy-start.5 = (bf16[2,512]{1,0:T(2,128)(2,1)S(1)}, bf16[2,512]{1,0:T(2,128)(2,1)}, u32[]{:S(2)}) copy-start(bf16[2,512]{1,0:T(2,128)(2,1)} %param.24) | copy-start | bytes 6148
  6.5 46.1 %copy-start.6 = (bf16[2,64]{1,0:T(2,128)(2,1)S(1)}, bf16[2,64]{1,0:T(2,128)(2,1)}, u32[]{:S(2)}) copy-start(bf16[2,64]{1,0:T(2,128)(2,1)} %param.25) | copy-start | bytes 772
  6.5 32.6 %all-gather.2.cloned.1.call-start = ((), (), s32[]{:S(2)}) async-start(), calls=%async_computation.5 | async-start | bytes 1769472 | tf_op jit(solution)/shard_map/all_gather | solution.py:51
  24.4 20.4 %all-to-all-start.1 = ((bf16[32,2,256]{2,1,0:T(2,128)(2,1)}), bf16[32,2,256]{2,1,0:T(2,128)(2,1)S(1)}, u32[]{:S(2)}, u32[]{:S(2)}) async-start(bf16[32,2,256]{2,1,0:T(2,128)(2,1)} %convert_element_type.40), calls=%async_computation.1 | async-start | bytes 65536 | tf_op jit(solution)/shard_map/all_to_all | solution.py:68
  41.1 25.3 %copy-start.4 = (s32[2,32]{1,0:T(2,128)S(1)}, s32[2,32]{1,0:T(2,128)}, u32[]{:S(2)}) copy-start(s32[2,32]{1,0:T(2,128)} %param.27) | copy-start | bytes 772
  44.8 19.1 %all-to-all-start = ((bf16[32,2,2048]{2,1,0:T(2,128)(2,1)}), bf16[32,2,2048]{2,1,0:T(2,128)(2,1)S(1)}, u32[]{:S(2)}, u32[]{:S(2)}) async-start(bf16[32,2,2048]{2,1,0:T(2,128)(2,1)} %all_to_all.45), calls=%async_computation | async-start | bytes 524288 | tf_op jit(solution)/shard_map/all_to_all | solution.py:67
  135.4 3.4 copy-start.1
  141.2 60.9 %copy-start.3 = (bf16[4,512,128]{2,1,0:T(8,128)(2,1)S(1)}, bf16[4,512,128]{2,1,0:T(8,128)(2,1)}, u32[]{:S(2)}) copy-start(bf16[4,512,128]{2,1,0:T(8,128)(2,1)} %param.20) | copy-start | bytes 1572868
  185.1 21.8 %copy-start.2 = (bf16[4,16,7168]{2,1,0:T(8,128)(2,1)S(1)}, bf16[4,16,7168]{2,1,0:T(8,128)(2,1)}, u32[]{:S(2)}) copy-start(bf16[4,16,7168]{2,1,0:T(8,128)(2,1)} %param.21) | copy-start | bytes 2752516
  203.3 8.9 all-to-all-start.3
  206.7 1290.7 %reduce-scatter.2.cloned.1.call-start = ((), (), s32[]{:S(2)}) async-start(), calls=%async_computation.6 | async-start | bytes 16842752 | tf_op jit(solution)/shard_map/reduce_scatter | solution.py:135
Sparse Core Ops, SparseCore 0:
  9.2 29.8 all-gather.1
  220.6 1276.7 reduce-scatter.1
where the time goes:
time: 1520 us; the launch traced here: 1510 us
  waiting for transfers between devices  1300 us (86%)
  local copies, waits for them, and re-layouts  93.2 us (6%)
  matrix products  34.3 us (2%)
  blocking collectives  30.3 us (2%)
  starting transfers between devices  22.8 us (2%)
    reduce_scatter x1, waiting for transfers between devices, body(): lax.psum_scatter(term, ('dp', 'head'), scatter_dimension=0, tiled=True)  1280 us
    gather x16, local copies, waits for them, and re-layouts, fetch(): latent_block = cache_latent[chosen].reshape(own_rows, keys, latent_dim)  63.9 us
  transfers between devices with their start and end apart: 5, of which 5 were waited for; matrix products, arithmetic and copies ran while one was open for 0% of the time, Pallas kernels for 0%

commit v1 on v0

v1 whole, which is shorter than its diff:
```python
import math

import jax
import jax.numpy as jnp
from jax import lax
from jax.experimental import pallas as pl
from jax.experimental.pallas import tpu as pltpu
from jax.sharding import PartitionSpec as P

BLOCK_PAGES = 8
Y = 4
Z = 8
Z_GROUPS = [[y * Z + z for z in range(Z)] for y in range(Y)]
Y_GROUPS = [[y * Z + z for y in range(Y)] for z in range(Z)]
F32 = jnp.float32
BF16 = jnp.bfloat16
WHOLE = pl.BlockSpec(memory_space=pltpu.VMEM)
SCALARS = pl.BlockSpec(memory_space=pltpu.SMEM)
IN_PLACE = pl.BlockSpec(memory_space=pl.ANY)


def dot(a, b):
    return jnp.dot(a, b, preferred_element_type=F32)


def params():
    return pltpu.CompilerParams(vmem_limit_bytes=40 * 1024 * 1024)


def project_kernel(pieces, latent_ref, *refs):
    piece_refs = refs[:pieces]
    uk_ref, cos_ref, sin_ref, out_ref = refs[pieces:]
    heads, nope_dim, width = uk_ref.shape
    both = None
    for i in range(pieces):
        term = dot(latent_ref[i], piece_refs[i][...])
        both = term if both is None else both + term
    query = both[:, : heads * nope_dim].astype(BF16)
    for j in range(heads):
        part = dot(query[:, j * nope_dim : (j + 1) * nope_dim], uk_ref[j])
        out_ref[:, j * width : (j + 1) * width] = part.astype(BF16)
    turned = both[:, heads * nope_dim :]
    lanes = turned.shape[1]
    rope_dim = lanes // heads
    lane = lax.broadcasted_iota(jnp.int32, turned.shape, 1)
    half = rope_dim // 2
    swapped = jnp.where(
        lane % rope_dim < half,
        pltpu.roll(turned, lanes - half, 1),
        pltpu.roll(turned, half, 1),
    )
    rotated = turned * cos_ref[...] + swapped * sin_ref[...]
    out_ref[:, heads * width :] = rotated.astype(BF16)


def project(latent, pieces, w_uk, cos, sin):
    heads, _, width = w_uk.shape
    rows = latent.shape[1]

    def kernel(*refs):
        project_kernel(len(pieces), *refs)

    return pl.pallas_call(
        kernel,
        out_shape=jax.ShapeDtypeStruct((rows, heads * width + cos.shape[1]), BF16),
        in_specs=[WHOLE] * (4 + len(pieces)),
        out_specs=WHOLE,
        compiler_params=params(),
        name="project",
    )(latent, *pieces, w_uk, cos, sin)


def sorter(rows, own, transposed):
    a = lax.broadcasted_iota(jnp.int32, (rows, rows), 0)
    b = lax.broadcasted_iota(jnp.int32, (rows, rows), 1)
    if transposed:
        a, b = b, a
    sources = rows // own
    return ((a % sources) * own + a // sources == b).astype(F32).astype(BF16)


def attend_kernel(
    length_ref, table_ref, query_ref, new_ref, new_rope_ref, latent_hbm, rope_hbm, out_ref,
    latents, ropes, latent_sem, rope_sem,
):
    own, blocks, keys, width = latents.shape
    rope_dim = ropes.shape[2]
    page = latent_hbm.shape[1]
    pages = keys // page
    rows = query_ref.shape[0]
    sources = rows // own
    heads = (query_ref.shape[1]) // (width + rope_dim)
    nope_rope = 128 + rope_dim
    factor = math.log2(math.e) / nope_rope**0.5
    for b in range(blocks):
        for r in range(own):
            for p in range(pages):
                index = table_ref[r, b * pages + p]
                span = pl.ds(p * page, page)
                pltpu.make_async_copy(
                    latent_hbm.at[index], latents.at[r, b, span], latent_sem.at[r, b]
                ).start()
                pltpu.make_async_copy(
                    rope_hbm.at[index], ropes.at[r, b, :, span], rope_sem.at[r, b]
                ).start()
    ordered = dot(sorter(rows, own, False), query_ref[...]).astype(BF16)
    absorbed, rotary, top, total, summed = [], [], [], [], []
    for r in range(own):
        part = ordered[r * sources : (r + 1) * sources]
        q_abs = jnp.concatenate(
            [part[:, j * width : (j + 1) * width] for j in range(heads)], axis=0
        )
        start = heads * width
        q_rot = jnp.concatenate(
            [part[:, start + j * rope_dim : start + (j + 1) * rope_dim] for j in range(heads)],
            axis=0,
        )
        new = new_ref[r : r + 1, :].astype(F32)
        new_rope = new_rope_ref[r : r + 1, :].astype(F32)
        score = jnp.sum(q_abs.astype(F32) * new, axis=1, keepdims=True)
        score += jnp.sum(q_rot.astype(F32) * new_rope, axis=1, keepdims=True)
        absorbed.append(q_abs)
        rotary.append(q_rot)
        top.append(score * factor)
        total.append(jnp.ones_like(score))
        summed.append(jnp.broadcast_to(new, q_abs.shape))
    for b in range(blocks):
        for r in range(own):
            pltpu.make_async_copy(latents.at[r, b], latents.at[r, b], latent_sem.at[r, b]).wait()
            pltpu.make_async_copy(ropes.at[r, b], ropes.at[r, b], rope_sem.at[r, b]).wait()
        for r in range(own):
            block = latents[r, b]
            scores = lax.dot_general(
                absorbed[r], block, (((1,), (1,)), ((), ())), preferred_element_type=F32
            )
            scores = (scores + dot(rotary[r], ropes[r, b])) * factor
            position = b * keys + lax.broadcasted_iota(jnp.int32, scores.shape, 1)
            scores = jnp.where(position < length_ref[r], scores, -jnp.inf)
            highest = jnp.maximum(top[r], jnp.max(scores, axis=1, keepdims=True))
            fade = jnp.exp2(top[r] - highest)
            weights = jnp.exp2(scores - highest)
            total[r] = total[r] * fade + jnp.sum(weights, axis=1, keepdims=True)
            summed[r] = summed[r] * fade + dot(weights.astype(BF16), block)
            top[r] = highest
    done = [(summed[r] / total[r]).astype(BF16) for r in range(own)]
    back = sorter(rows, own, True)
    for j in range(heads):
        piece = jnp.concatenate([d[j * sources : (j + 1) * sources] for d in done], axis=0)
        out_ref[:, j * width : (j + 1) * width] = dot(back, piece).astype(BF16)


def attend(lengths, table, query, new_latent, new_rope, cache_latent, cache_rope):
    own, slots = table.shape
    _, page, width = cache_latent.shape
    rope_dim = cache_rope.shape[1]
    blocks = slots // BLOCK_PAGES
    keys = BLOCK_PAGES * page
    heads = query.shape[1] // (width + rope_dim)
    return pl.pallas_call(
        attend_kernel,
        out_shape=jax.ShapeDtypeStruct((query.shape[0], heads * width), BF16),
        in_specs=[SCALARS, SCALARS, WHOLE, WHOLE, WHOLE, IN_PLACE, IN_PLACE],
        out_specs=WHOLE,
        scratch_shapes=[
            pltpu.VMEM((own, blocks, keys, width), BF16),
            pltpu.VMEM((own, blocks, rope_dim, keys), BF16),
            pltpu.SemaphoreType.DMA((own, blocks)),
            pltpu.SemaphoreType.DMA((own, blocks)),
        ],
        compiler_params=params(),
        name="attend",
    )(lengths, table, query, new_latent, new_rope, cache_latent, cache_rope)


def values_kernel(parts, attn_ref, uv_ref, out_ref):
    heads, width, value_dim = uv_ref.shape
    per = value_dim // parts
    columns = heads * value_dim
    source = lax.broadcasted_iota(jnp.int32, (value_dim, columns), 0)
    column = lax.broadcasted_iota(jnp.int32, (value_dim, columns), 1)
    total = None
    for j in range(heads):
        value = dot(attn_ref[:, j * width : (j + 1) * width], uv_ref[j]).astype(BF16)
        place = (source // per) * (heads * per) + j * per + source % per
        spread = dot(value, (column == place).astype(F32).astype(BF16))
        total = spread if total is None else total + spread
    out_ref[...] = total.astype(BF16)


def project_values(attn, w_uv, parts):
    heads, _, value_dim = w_uv.shape

    def kernel(*refs):
        values_kernel(parts, *refs)

    return pl.pallas_call(
        kernel,
        out_shape=jax.ShapeDtypeStruct((attn.shape[0], heads * value_dim), BF16),
        in_specs=[WHOLE] * 2,
        out_specs=WHOLE,
        compiler_params=params(),
        name="values",
    )(attn, w_uv)


def mix_kernel(values_ref, weights_ref, out_ref, sorted_ref, total_ref):
    step = pl.program_id(0)
    _, sources, per, columns = weights_ref.shape

    @pl.when(step == 0)
    def _():
        for d in range(sorted_ref.shape[0]):
            for y in range(sources):
                sorted_ref[d, :, y * per : (y + 1) * per] = values_ref[
                    y, :, d * per : (d + 1) * per
                ]
        total_ref[...] = jnp.zeros_like(total_ref)

    total_ref[...] += dot(sorted_ref[step], weights_ref[0].reshape(sources * per, columns))

    @pl.when(step == pl.num_programs(0) - 1)
    def _():
        parts, _, width = out_ref.shape
        for z in range(parts):
            out_ref[z] = total_ref[:, z * width : (z + 1) * width].astype(BF16)


def mix(values, weights, parts):
    sources, rows, _ = values.shape
    steps, _, per, columns = weights.shape
    return pl.pallas_call(
        mix_kernel,
        grid=(steps,),
        out_shape=jax.ShapeDtypeStruct((parts, rows, columns // parts), BF16),
        in_specs=[
            pl.BlockSpec(values.shape, lambda d: (0, 0, 0)),
            pl.BlockSpec((1, sources, per, columns), lambda d: (d, 0, 0, 0)),
        ],
        out_specs=pl.BlockSpec((parts, rows, columns // parts), lambda d: (0, 0, 0)),
        scratch_shapes=[
            pltpu.VMEM((steps, rows, sources * per), BF16),
            pltpu.VMEM((rows, columns), F32),
        ],
        compiler_params=params(),
        name="mix",
    )(values, weights)


def shift_dp(x, along, across):
    count = lax.axis_size("dp")
    chips = count // 2
    pairs = [
        (p * 2 + c, ((p + along) % chips) * 2 + (c ^ across)) for p in range(chips) for c in range(2)
    ]
    return lax.ppermute(x, "dp", pairs)


def gather_pieces(x):
    half = x.shape[0] // 2
    after, before, other = shift_dp(x, 1, 0), shift_dp(x, 3, 0), shift_dp(x, 0, 1)
    far_top, far_low = shift_dp(after[:half], 1, 0), shift_dp(before[half:], 3, 0)
    far = jnp.concatenate([far_top, far_low], axis=0)
    pieces = [x, other, after, shift_dp(after, 0, 1), before, shift_dp(before, 0, 1)]
    pieces += [far, shift_dp(far, 0, 1)]
    return pieces, [(0, 0), (0, 1), (1, 0), (1, 1), (3, 0), (3, 1), (2, 0), (2, 1)]


def angles(lengths, rope_dim, heads):
    half = rope_dim // 2
    freq = 10000.0 ** (-2.0 * jnp.arange(half, dtype=F32) / (2 * half))
    angle = lengths.astype(F32)[:, None] * freq
    cos, sin = jnp.cos(angle), jnp.sin(angle)
    cos = jnp.tile(cos, (1, 2 * heads))
    sin = jnp.tile(jnp.concatenate([-sin, sin], axis=1), (1, heads))
    return cos, sin


def body(
    q_latent,
    w_qnope,
    w_qrope,
    w_uk,
    w_uv,
    w_out,
    cache_latent,
    cache_rope,
    new_latent,
    new_rope,
    lengths,
    page_table,
):
    rows = q_latent.shape[0]
    heads, value_dim = w_uk.shape[0], w_uv.shape[2]
    own = page_table.shape[0]
    width_all = w_out.shape[2]
    dp_count = lax.axis_size("dp")
    sources = lax.axis_size("head")
    depth = w_out.shape[0] * w_out.shape[1]

    panel = w_out.reshape(depth, Y, width_all // Y).transpose(1, 0, 2)
    panel = lax.all_to_all(panel, "head", 0, 0, tiled=True, axis_index_groups=Y_GROUPS)
    panel = lax.all_gather(panel, "dp", axis=0)

    pieces, origins = gather_pieces(jnp.concatenate([w_qnope, w_qrope], axis=1))
    me = lax.axis_index("dp")
    chips = dp_count // 2
    order = jnp.stack(
        [((me // 2 - along) % chips) * 2 + (me % 2 + across) % 2 for along, across in origins]
    )
    latent = q_latent.reshape(rows, dp_count, -1).transpose(1, 0, 2)[order]
    cos, sin = angles(lengths, cache_rope.shape[1], heads)
    query = project(latent, pieces, w_uk, cos, sin)

    query = query.reshape(sources, own, query.shape[1])
    query = lax.all_to_all(query, "head", 0, 0, tiled=True).reshape(rows, -1)
    own_lengths = lax.dynamic_slice_in_dim(lengths, lax.axis_index("head") * own, own)
    attn = attend(own_lengths, page_table, query, new_latent, new_rope, cache_latent, cache_rope)
    attn = attn.reshape(sources, own, attn.shape[1])
    attn = lax.all_to_all(attn, "head", 0, 0, tiled=True).reshape(rows, -1)
    values = project_values(attn, w_uv, dp_count)
    values = jnp.broadcast_to(values[None], (Y, rows, heads * value_dim))
    values = lax.all_to_all(values, "head", 0, 0, tiled=True, axis_index_groups=Y_GROUPS)
    term = mix(values, panel, Z)
    term = lax.all_to_all(term, "head", 0, 0, tiled=True, axis_index_groups=Z_GROUPS)
    return jnp.sum(term.astype(F32), axis=0).astype(BF16)


def solution(mesh):
    in_specs = (
        P("dp", None),
        P("dp", "head"),
        P("dp", "head"),
        P("head", None, None),
        P("head", None, None),
        P("head", "dp", None),
        P(("dp", "head"), None, None),
        P(("dp", "head"), None, None),
        P(("dp", "head"), None),
        P(("dp", "head"), None),
        P("dp"),
        P(("dp", "head"), None),
    )
    out_specs = P("dp", "head")
    return jax.shard_map(body, mesh=mesh, in_specs=in_specs, out_specs=out_specs, check_vma=False)
```

time: 1520 us -> 159 us (0.10)
  waiting for transfers between devices: 1300 us -> 20.4 us
  local copies, waits for them, and re-layouts: 93.2 us -> 21.8 us
  matrix products: 34.3 us -> 0 us
  blocking collectives: 30.3 us -> 56.8 us
  Pallas kernels: 0 us -> 24.4 us
    reduce_scatter x1 -> x0, waiting for transfers between devices: 1280 us -> none  [body(): lax.psum_scatter(term, ('dp', 'head'), scatter_dimension=0, tiled=True)]
    gather x24 -> x1, local copies, waits for them, and re-layouts: 78.3 us -> 1.52 us  [body(): latent = q_latent.reshape(rows, dp_count, -1).transpose(1, 0, 2)[order]]
    all_to_all x1 -> x4, blocking collectives: 16.4 us -> 56.8 us  [the longest x1 17.1 us: body(): attn = lax.all_to_all(attn, 'head', 0, 0, tiled=True).reshape(rows, -1)]
    dot_general x31 -> x0, matrix products: 34.3 us -> none  [the longest x8 10.2 us: value_block(): jnp.einsum('rhk,rkl->rhl', block_probs, latent_block, preferred_element_t...]
    pallas_call x0 -> x4, Pallas kernels: none -> 24.4 us  [the longest x1 19.1 us: attend(): pl.pallas_call(attend_kernel, out_shape=jax.ShapeDtypeStruct((query.shape...]
  transfers between devices with their start and end apart: 5 -> 10, of which waited for: 5 -> 4; matrix products, arithmetic and copies ran while one was open for 0% -> 6% of each run, Pallas kernels for 0% -> 14%
where the time goes in v1:
time: 159 us; the launch traced here: 157 us
  blocking collectives  56.8 us (36%)
  Pallas kernels  24.4 us (15%)
  local copies, waits for them, and re-layouts  21.8 us (14%)
  waiting for transfers between devices  20.4 us (13%)
  starting transfers between devices  18.1 us (11%)
  between operations  13.7 us (9%)
    pallas_call x1, Pallas kernels, attend(): pl.pallas_call(attend_kernel, out_shape=jax.ShapeDtypeStruct((query.shape...  19.1 us
    all_to_all x1, blocking collectives, body(): attn = lax.all_to_all(attn, 'head', 0, 0, tiled=True).reshape(rows, -1)  17.1 us
    all_to_all x1, blocking collectives, body(): lax.all_to_all(panel, 'head', 0, 0, tiled=True, axis_index_groups=Y_GROUPS)  17 us
    all_to_all x1, blocking collectives, body(): lax.all_to_all(term, 'head', 0, 0, tiled=True, axis_index_groups=Z_GROUPS)  13.4 us
    all_to_all x1, waiting for transfers between devices, body(): query = lax.all_to_all(query, 'head', 0, 0, tiled=True).reshape(rows, -1)  11.8 us
    all_to_all x1, starting transfers between devices, body(): query = lax.all_to_all(query, 'head', 0, 0, tiled=True).reshape(rows, -1)  11 us
    unnamed x26, local copies, waits for them, and re-layouts  10.1 us
    all_to_all x1, blocking collectives, body(): lax.all_to_all(values, 'head', 0, 0, tiled=True, axis_index_groups=Y_GROUPS)  9.22 us
  transfers between devices with their start and end apart: 10, of which 4 were waited for; matrix products, arithmetic and copies ran while one was open for 6% of the time, Pallas kernels for 14%

profile of v1, /device:TPU:8, one launch (start us, length us, event | category | flops | bytes accessed | tf_op | source)
XLA Modules:
  0.0 156.7 jit_solution(11537631598030849757)
XLA Ops:
  6.6 3.0 %reshape.376 = bf16[64,4,1792]{2,1,0:T(4,128)(2,1)} reshape(bf16[4,16,7168]{2,1,0:T(8,128)(2,1)} %param.17) | data formatting | bytes 1835008 | tf_op jit(solution)/shard_map/reshape | solution.py:300
  9.6 1.3 copy.31
  10.9 17.0 %all_to_all.25 = bf16[4,64,1792]{2,1,0:T(8,128)(2,1)} all-to-all(bf16[4,64,1792]{2,1,0:T(8,128)(2,1)S(1)} %copy.31), channel_id=1, replica_groups={{0,8,16,24},{1,9,17,25},{2,10,18,26},{3,11,19,27},{4,12,20,28},{5,13,21..., dimensions={0} | all-to-all | bytes 1835008 | tf_op jit(solution)/shard_map/all_to_all | solution.py:301
  28.0 0.9 constant_dynamic-update-slice_fusion.1
  28.9 0.9 constant_dynamic-update-slice_fusion.refs_1_
  29.8 1.5 collective-permute-start.1
  31.3 1.7 %collective-permute-start.3 = (bf16[192,768]{1,0:T(8,128)(2,1)S(1)}, bf16[192,768]{1,0:T(8,128)(2,1)S(1)}, u32[]{:S(2)}, u32[]{:S(2)}) collective-permute-start(bf16[192,768]{1,0:T(8,128)(2,1)S(1)} %constant_dynamic-update-slice_fusion.refs_1_), channel_id=1, source_target_pairs={{0,192},{32,224},{64,0},{96,32},{128,64},{160,96},{192,128},{224,1... | collective-permute-start | bytes 884744 | tf_op jit(solution)/shard_map/ppermute | solution.py:255
  33.1 0.7 convert_element_type.2
  33.7 4.7 %collective-permute-done.1.refs_3_ = bf16[192,768]{1,0:T(8,128)(2,1)S(1)} collective-permute-done((bf16[192,768]{1,0:T(8,128)(2,1)S(1)}, bf16[192,768]{1,0:T(8,128)(2,1)S(1)}, u32[]{:S(2)}, u32[]{:S(2)}) %collective-permute-start.1) | collective-permute-done | bytes 294944 | tf_op jit(solution)/shard_map/ppermute | solution.py:255
  38.4 0.7 slice.10
  39.7 0.7 slice.11
  40.4 2.8 %collective-permute-start.6 = (bf16[96,768]{1,0:T(8,128)(2,1)}, bf16[96,768]{1,0:T(8,128)(2,1)}, u32[]{:S(2)}, u32[]{:S(2)}) collective-permute-start(bf16[96,768]{1,0:T(8,128)(2,1)} %slice.11), channel_id=1, source_target_pairs={{0,192},{32,224},{64,0},{96,32},{128,64},{160,96},{192,128},{224,1... | collective-permute-start | bytes 442376 | tf_op jit(solution)/shard_map/ppermute | solution.py:255
  43.7 0.7 copy.33
  45.7 3.3 %collective-permute-done.6 = bf16[96,768]{1,0:T(8,128)(2,1)} collective-permute-done((bf16[96,768]{1,0:T(8,128)(2,1)}, bf16[96,768]{1,0:T(8,128)(2,1)}, u32[]{:S(2)}, u32[]{:S(2)}) %collective-permute-start.6) | collective-permute-done | bytes 147488 | tf_op jit(solution)/shard_map/ppermute | solution.py:255
  49.0 0.9 constant_dynamic-update-slice_fusion.2.refs_7_
  50.1 1.5 gather_fusion
  51.6 0.7 copy-done.5
  52.3 1.0 copy-done.6
  53.3 1.9 %project.1 = bf16[64,2304]{1,0:T(8,128)(2,1)S(1)} custom-call(bf16[8,64,192]{2,1,0:T(8,128)(2,1)S(1)} %gather_fusion, bf16[192,768]{1,0:T(8,128)(2,1)S(1)} %constant_dynamic-update-slice_fusion.refs_1_, bf16[192,768]{1,0:T(8,128)(2,1)S(1)} %copy-done.6, bf16[192,768]{1,0:T(8,128)(2,1)S(1)} %collective-permute-done.1.refs_3_, ...), custom_call_target="tpu_custom_call" | custom-call | tf_op jit(solution)/shard_map/project/pallas_call | solution.py:63
  55.2 0.8 reshape.372
  56.1 11.0 %all-to-all-start = ((bf16[32,2,2304]{2,1,0:T(2,128)(2,1)}), bf16[32,2,2304]{2,1,0:T(2,128)(2,1)S(1)}, u32[]{:S(2)}, u32[]{:S(2)}) async-start(bf16[32,2,2304]{2,1,0:T(2,128)(2,1)} %reshape.372), calls=%async_computation | async-start | bytes 589824 | tf_op jit(solution)/shard_map/all_to_all | solution.py:315
  67.2 11.8 %all-to-all-done = bf16[32,2,2304]{2,1,0:T(2,128)(2,1)S(1)} async-done(((bf16[32,2,2304]{2,1,0:T(2,128)(2,1)}), bf16[32,2,2304]{2,1,0:T(2,128)(2,1)S(1)}, u32[]{:S(2)}, u32[]{:S(2)}) %all-to-all-start) | async-done | bytes 294944 | tf_op jit(solution)/shard_map/all_to_all | solution.py:315
  79.2 3.4 %copy-done = bf16[64,128,512]{2,1,0:T(8,128)(2,1)S(1)} copy-done((bf16[64,128,512]{2,1,0:T(8,128)(2,1)S(1)}, bf16[64,128,512]{2,1,0:T(8,128)(2,1)}, u32[]{:S(2)}) %copy-start) | copy-done | bytes 8388632
  82.5 19.1 %attend.1 = bf16[64,2048]{1,0:T(8,128)(2,1)S(1)} custom-call(s32[2]{0:T(128)S(1)} %dynamic_slice.3.length_ref, s32[2,32]{1,0:T(2,128)S(1)} %copy-done.8, bf16[64,2304]{1,0:T(8,128)(2,1)S(1)} %reshape.373.query_ref, bf16[2,512]{1,0:T(2,128)(2,1)S(1)} %copy-done.7, bf16[2,64]{1,0:T(2,128)(2,1)S(1)} %copy-done.9, bf16[64,128,512]{2,1,0:T(8,128)(2,1)S(1)} %copy-done, ...), custom_call_target="tpu_custom_call" | custom-call | tf_op jit(solution)/shard_map/attend/pallas_call | solution.py:159
  101.9 17.1 %all_to_all.26 = bf16[32,2,2048]{2,1,0:T(2,128)(2,1)S(1)} all-to-all(bf16[32,2,2048]{2,1,0:T(2,128)(2,1)S(1)} %reshape.374), channel_id=1, replica_groups=mesh['dp'=8,'head'=32] {'head'}, dimensions={0} | all-to-all | bytes 524288 | tf_op jit(solution)/shard_map/all_to_all | solution.py:319
  119.1 1.0 copy-done.4
  120.1 0.6 values.1
  120.8 9.2 %all_to_all.27.values_ref = bf16[4,64,512]{2,1,0:T(8,128)(2,1)S(1)} all-to-all(bf16[4,64,512]{2,1,0:T(8,128)(2,1)S(1)} %broadcast_in_dim.2), channel_id=1, replica_groups={{0,8,16,24},{1,9,17,25},{2,10,18,26},{3,11,19,27},{4,12,20,28},{5,13,21..., dimensions={0} | all-to-all | bytes 524288 | tf_op jit(solution)/shard_map/all_to_all | solution.py:322
  130.0 3.1 %copy-done.1 = bf16[32,64,1792]{2,1,0:T(8,128)(2,1)S(1)} copy-done((bf16[32,64,1792]{2,1,0:T(8,128)(2,1)S(1)}, bf16[32,64,1792]{2,1,0:T(8,128)(2,1)}, u32[]{:S(2)}) %copy-start.1) | copy-done | bytes 7340056
  133.1 2.7 %mix.1 = bf16[8,64,224]{2,1,0:T(8,128)(2,1)S(1)} custom-call(bf16[4,64,512]{2,1,0:T(8,128)(2,1)S(1)} %all_to_all.27.values_ref, bf16[8,4,64,1792]{3,2,1,0:T(8,128)(2,1)S(1)} %bitcast.16), custom_call_target="tpu_custom_call" | custom-call | tf_op jit(solution)/shard_map/mix/pallas_call | solution.py:231
  135.8 13.4 %all_to_all.28 = bf16[8,64,224]{2,1,0:T(8,128)(2,1)S(1)} all-to-all(bf16[8,64,224]{2,1,0:T(8,128)(2,1)S(1)} %mix.1), channel_id=1, replica_groups={{0,1,2,3,4,5,6,7},{8,9,10,11,12,13,14,15},{16,17,18,19,20,21,22,23},{24..., dimensions={0} | all-to-all | bytes 458752 | tf_op jit(solution)/shard_map/all_to_all | solution.py:324
  149.2 0.7 reduce_sum.12
  (51 shorter events, 3.1 us)
Async XLA Ops:
  6.5 60.5 %copy-start.11 = (s32[64]{0:T(128)S(1)}, s32[64]{0:T(128)}, u32[]{:S(2)}) copy-start(s32[64]{0:T(128)} %param.22) | copy-start | bytes 772
  6.5 37.0 %copy-start.10 = (bf16[64,1536]{1,0:T(8,128)(2,1)S(1)}, bf16[64,1536]{1,0:T(8,128)(2,1)}, u32[]{:S(2)}) copy-start(bf16[64,1536]{1,0:T(8,128)(2,1)} %param.12) | copy-start | bytes 589828
  6.5 45.8 %copy-start.3 = (bf16[4,128,512]{2,1,0:T(8,128)(2,1)S(1)}, bf16[4,128,512]{2,1,0:T(8,128)(2,1)}, u32[]{:S(2)}) copy-start(bf16[4,128,512]{2,1,0:T(8,128)(2,1)} %refs_9_.1) | copy-start | bytes 1572868
  6.5 72.6 %copy-start.8 = (s32[2,32]{1,0:T(2,128)S(1)}, s32[2,32]{1,0:T(2,128)}, u32[]{:S(2)}) copy-start(s32[2,32]{1,0:T(2,128)} %table_ref.1) | copy-start | bytes 772
  6.5 72.6 %copy-start.9 = (bf16[2,64]{1,0:T(2,128)(2,1)S(1)}, bf16[2,64]{1,0:T(2,128)(2,1)}, u32[]{:S(2)}) copy-start(bf16[2,64]{1,0:T(2,128)(2,1)} %new_rope_ref.1) | copy-start | bytes 772
  6.5 72.6 %copy-start.7 = (bf16[2,512]{1,0:T(2,128)(2,1)S(1)}, bf16[2,512]{1,0:T(2,128)(2,1)}, u32[]{:S(2)}) copy-start(bf16[2,512]{1,0:T(2,128)(2,1)} %new_ref.1) | copy-start | bytes 6148
  6.6 72.6 %copy-start.2 = (bf16[64,64,128]{2,1,0:T(8,128)(2,1)S(1)}, bf16[64,64,128]{2,1,0:T(8,128)(2,1)}, u32[]{:S(2)}) copy-start(bf16[64,64,128]{2,1,0:T(8,128)(2,1)} %rope_hbm.1) | copy-start | bytes 3145732
  6.6 123.4 %all-gather.3.cloned.1.call-start = ((), (), s32[]{:S(2)}) async-start(), calls=%async_computation.5 | async-start | bytes 8257536 | tf_op jit(solution)/shard_map/all_gather | solution.py:302
  29.8 8.6 %collective-permute-start.1 = (bf16[192,768]{1,0:T(8,128)(2,1)S(1)}, bf16[192,768]{1,0:T(8,128)(2,1)S(1)}, u32[]{:S(2)}, u32[]{:S(2)}) collective-permute-start(bf16[192,768]{1,0:T(8,128)(2,1)S(1)} %constant_dynamic-update-slice_fusion.refs_1_), channel_id=1, source_target_pairs={{0,64},{32,96},{64,128},{96,160},{128,192},{160,224},{192,0},{224,... | collective-permute-start | bytes 884744 | tf_op jit(solution)/shard_map/ppermute | solution.py:255
  31.3 8.4 %collective-permute-start.3 = (bf16[192,768]{1,0:T(8,128)(2,1)S(1)}, bf16[192,768]{1,0:T(8,128)(2,1)S(1)}, u32[]{:S(2)}, u32[]{:S(2)}) collective-permute-start(bf16[192,768]{1,0:T(8,128)(2,1)S(1)} %constant_dynamic-update-slice_fusion.refs_1_), channel_id=1, source_target_pairs={{0,192},{32,224},{64,0},{96,32},{128,64},{160,96},{192,128},{224,1... | collective-permute-start | bytes 884744 | tf_op jit(solution)/shard_map/ppermute | solution.py:255
  33.1 18.5 %collective-permute-start = (bf16[192,768]{1,0:T(8,128)(2,1)S(1)}, bf16[192,768]{1,0:T(8,128)(2,1)S(1)}, u32[]{:S(2)}, u32[]{:S(2)}) collective-permute-start(bf16[192,768]{1,0:T(8,128)(2,1)S(1)} %constant_dynamic-update-slice_fusion.refs_1_), channel_id=1, source_target_pairs={{0,32},{32,0},{64,96},{96,64},{128,160},{160,128},{192,224},{224,1... | collective-permute-start | bytes 884744 | tf_op jit(solution)/shard_map/ppermute | solution.py:255
  39.1 6.6 %collective-permute-start.5 = (bf16[96,768]{1,0:T(8,128)(2,1)}, bf16[96,768]{1,0:T(8,128)(2,1)S(1)}, u32[]{:S(2)}, u32[]{:S(2)}) collective-permute-start(bf16[96,768]{1,0:T(8,128)(2,1)} %slice.10), channel_id=1, source_target_pairs={{0,64},{32,96},{64,128},{96,160},{128,192},{160,224},{192,0},{224,... | collective-permute-start | bytes 442376 | tf_op jit(solution)/shard_map/ppermute | solution.py:255
  40.4 8.6 %collective-permute-start.6 = (bf16[96,768]{1,0:T(8,128)(2,1)}, bf16[96,768]{1,0:T(8,128)(2,1)}, u32[]{:S(2)}, u32[]{:S(2)}) collective-permute-start(bf16[96,768]{1,0:T(8,128)(2,1)} %slice.11), channel_id=1, source_target_pairs={{0,192},{32,224},{64,0},{96,32},{128,64},{160,96},{192,128},{224,1... | collective-permute-start | bytes 442376 | tf_op jit(solution)/shard_map/ppermute | solution.py:255
  44.6 7.7 %collective-permute-start.4 = (bf16[192,768]{1,0:T(8,128)(2,1)S(1)}, bf16[192,768]{1,0:T(8,128)(2,1)}, u32[]{:S(2)}, u32[]{:S(2)}) collective-permute-start(bf16[192,768]{1,0:T(8,128)(2,1)S(1)} %collective-permute-done.3.refs_5_), channel_id=1, source_target_pairs={{0,32},{32,0},{64,96},{96,64},{128,160},{160,128},{192,224},{224,1... | collective-permute-start | bytes 884744 | tf_op jit(solution)/shard_map/ppermute | solution.py:255
  44.6 7.7 %collective-permute-start.2 = (bf16[192,768]{1,0:T(8,128)(2,1)S(1)}, bf16[192,768]{1,0:T(8,128)(2,1)}, u32[]{:S(2)}, u32[]{:S(2)}) collective-permute-start(bf16[192,768]{1,0:T(8,128)(2,1)S(1)} %collective-permute-done.1.refs_3_), channel_id=1, source_target_pairs={{0,32},{32,0},{64,96},{96,64},{128,160},{160,128},{192,224},{224,1... | collective-permute-start | bytes 884744 | tf_op jit(solution)/shard_map/ppermute | solution.py:255
  49.9 2.4 %collective-permute-start.7 = (bf16[192,768]{1,0:T(8,128)(2,1)S(1)}, bf16[192,768]{1,0:T(8,128)(2,1)}, u32[]{:S(2)}, u32[]{:S(2)}) collective-permute-start(bf16[192,768]{1,0:T(8,128)(2,1)S(1)} %constant_dynamic-update-slice_fusion.2.refs_7_), channel_id=1, source_target_pairs={{0,32},{32,0},{64,96},{96,64},{128,160},{160,128},{192,224},{224,1... | collective-permute-start | bytes 884744 | tf_op jit(solution)/shard_map/ppermute | solution.py:255
  51.6 0.7 copy-start.5
  52.3 1.0 copy-start.6
  56.1 22.9 %all-to-all-start = ((bf16[32,2,2304]{2,1,0:T(2,128)(2,1)}), bf16[32,2,2304]{2,1,0:T(2,128)(2,1)S(1)}, u32[]{:S(2)}, u32[]{:S(2)}) async-start(bf16[32,2,2304]{2,1,0:T(2,128)(2,1)} %reshape.372), calls=%async_computation | async-start | bytes 589824 | tf_op jit(solution)/shard_map/all_to_all | solution.py:315
  79.2 3.4 %copy-start = (bf16[64,128,512]{2,1,0:T(8,128)(2,1)S(1)}, bf16[64,128,512]{2,1,0:T(8,128)(2,1)}, u32[]{:S(2)}) copy-start(bf16[64,128,512]{2,1,0:T(8,128)(2,1)} %latent_hbm.1) | copy-start | bytes 25165828
  119.1 1.0 copy-start.4
  130.0 3.1 %copy-start.1 = (bf16[32,64,1792]{2,1,0:T(8,128)(2,1)S(1)}, bf16[32,64,1792]{2,1,0:T(8,128)(2,1)}, u32[]{:S(2)}) copy-start(bf16[32,64,1792]{2,1,0:T(8,128)(2,1)} %all-gather.3.cloned.1.call-done) | copy-start | bytes 22020100
Sparse Core Ops, SparseCore 0:
  28.1 49.6 all-gather.2

commit v2 on v0

v2 whole, which is shorter than its diff:
```python
import math

import jax
import jax.numpy as jnp
from jax import lax
from jax.experimental import pallas as pl
from jax.experimental.pallas import tpu as pltpu
from jax.sharding import PartitionSpec as P

GROUP = 4
CHUNKS = 8
NOPE = 128
Y = 4
Z = 8
Z_GROUPS = [[y * Z + z for z in range(Z)] for y in range(Y)]
Y_GROUPS = [[y * Z + z for y in range(Y)] for z in range(Z)]
F32 = jnp.float32
BF16 = jnp.bfloat16
WHOLE = pl.BlockSpec(memory_space=pltpu.VMEM)
SCALARS = pl.BlockSpec(memory_space=pltpu.SMEM)
IN_HBM = pl.BlockSpec(memory_space=pltpu.HBM)


def dot(a, b):
    return jnp.dot(a, b, preferred_element_type=F32)


def in_hbm(x):
    return pltpu.with_memory_space_constraint(x, pltpu.HBM)


def params(mib):
    return pltpu.CompilerParams(vmem_limit_bytes=mib * 1024 * 1024)


def prepare_kernel(nope_hbm, rope_hbm, weights_hbm, both_ref, cut_ref, sem):
    width = nope_hbm.shape[1]
    columns = cut_ref.shape[2]
    copies = [
        pltpu.make_async_copy(nope_hbm, both_ref.at[:, :width], sem.at[0]),
        pltpu.make_async_copy(rope_hbm, both_ref.at[:, width:], sem.at[1]),
    ]
    for y in range(Y):
        source = weights_hbm.at[:, pl.ds(y * columns, columns)]
        copies.append(pltpu.make_async_copy(source, cut_ref.at[y], sem.at[2 + y]))
    for copy in copies:
        copy.start()
    for copy in copies:
        copy.wait()


def prepare(w_qnope, w_qrope, weights):
    depth = w_qnope.shape[0]
    return pl.pallas_call(
        prepare_kernel,
        out_shape=(
            jax.ShapeDtypeStruct((depth, w_qnope.shape[1] + w_qrope.shape[1]), BF16),
            jax.ShapeDtypeStruct((Y, weights.shape[0], weights.shape[1] // Y), BF16),
        ),
        in_specs=[IN_HBM] * 3,
        out_specs=(WHOLE, WHOLE),
        scratch_shapes=[pltpu.SemaphoreType.DMA((2 + Y,))],
        compiler_params=params(8),
        name="prepare",
    )(*[in_hbm(a) for a in (w_qnope, w_qrope, weights)])


def one_hot(rows, columns, place, keep=None):
    a = lax.broadcasted_iota(jnp.int32, (rows, columns), 0)
    b = lax.broadcasted_iota(jnp.int32, (rows, columns), 1)
    hit = place(a) == b
    if keep is not None:
        hit = hit & keep(a)
    return hit.astype(F32).astype(BF16)


def project_kernel(
    latent_ref, weights_hbm, uk_ref, cos_ref, sin_ref, out_ref, held_ref, sem
):
    heads, nope_dim, width = uk_ref.shape
    rows = latent_ref.shape[0]
    steps, depth, _ = held_ref.shape
    copies = [
        pltpu.make_async_copy(weights_hbm.at[pl.ds(d * depth, depth)], held_ref.at[d], sem.at[d])
        for d in range(steps)
    ]
    for copy in copies:
        copy.start()
    both = None
    for d in range(steps):
        copies[d].wait()
        term = dot(latent_ref[:, d * depth : (d + 1) * depth], held_ref[d])
        both = term if both is None else both + term
    query = both[:, : heads * nope_dim].astype(BF16)
    turned = both[:, heads * nope_dim :]
    lanes = turned.shape[1]
    rope_dim = lanes // heads
    lane = lax.broadcasted_iota(jnp.int32, turned.shape, 1)
    half = rope_dim // 2
    swapped = jnp.where(
        lane % rope_dim < half,
        pltpu.roll(turned, lanes - half, 1),
        pltpu.roll(turned, half, 1),
    )
    rotated = (turned * cos_ref[...] + swapped * sin_ref[...]).astype(BF16)
    blank = jnp.zeros((rows, out_ref.shape[1] - width - rope_dim), BF16)
    total = None
    for j in range(heads):
        part = dot(query[:, j * nope_dim : (j + 1) * nope_dim], uk_ref[j]).astype(BF16)
        part = jnp.concatenate([part, rotated[:, j * rope_dim : (j + 1) * rope_dim], blank], axis=1)
        place = one_hot(
            rows * heads, rows, lambda i: i // heads, lambda i, j=j: i % heads == j
        )
        term = dot(place, part)
        total = term if total is None else total + term
    out_ref[...] = total.astype(BF16)


def project(latent, weights, w_uk, cos, sin, parts):
    heads, _, width = w_uk.shape
    rows = latent.shape[0]
    full = width + 128 * pl.cdiv(cos.shape[1] // heads, 128)
    return pl.pallas_call(
        project_kernel,
        out_shape=jax.ShapeDtypeStruct((rows * heads, full), BF16),
        in_specs=[WHOLE, IN_HBM] + [WHOLE] * 3,
        out_specs=WHOLE,
        scratch_shapes=[
            pltpu.VMEM((parts, weights.shape[0] // parts, weights.shape[1]), BF16),
            pltpu.SemaphoreType.DMA((parts,)),
        ],
        compiler_params=params(16),
        name="project",
    )(latent, in_hbm(weights), w_uk, cos, sin)


def attend_kernel(
    length_ref, table_ref, query_ref, new_ref, new_rope_ref, latent_hbm, rope_ref, out_ref,
    scores_ref, held_ref, high_ref, absorbed_ref, rotary_ref, row_ref, slot_ref, sem,
):
    own, slots = table_ref.shape
    pool, page, width = held_ref.shape
    rope_dim = rope_ref.shape[1]
    rows = query_ref.shape[0]
    all_heads = rows // own
    heads = out_ref.shape[1] // width
    sources = all_heads // heads
    factor = math.log2(math.e) / (NOPE + rope_dim) ** 0.5
    share = pool // CHUNKS
    copies = []
    for c in range(CHUNKS):
        span = pl.ds(c * share, share)
        copies.append(pltpu.make_async_copy(latent_hbm.at[span], held_ref.at[span], sem.at[c]))
    for copy in copies:
        copy.start()
    for r in range(own):
        for i in range(slots):
            index = table_ref[r, i]
            row_ref[index] = r
            slot_ref[index] = i
    def sorted_place(i):
        return (i % all_heads) // heads * (own * heads) + i // all_heads * heads + i % heads

    ordered = dot(one_hot(rows, rows, sorted_place), query_ref[...]).astype(BF16)
    new_scores = []
    for r in range(own):
        q_abs = ordered[r * all_heads : (r + 1) * all_heads, :width]
        q_rot = ordered[r * all_heads : (r + 1) * all_heads, width : width + rope_dim]
        absorbed_ref[r] = q_abs
        rotary_ref[r] = q_rot
        new_rope = new_rope_ref[r : r + 1, :].astype(F32)
        score_new = jnp.sum(
            q_abs.astype(F32) * new_ref[r : r + 1, :].astype(F32), axis=1, keepdims=True
        )
        score_new += jnp.sum(q_rot.astype(F32) * new_rope, axis=1, keepdims=True)
        new_scores.append(score_new * factor)
    high_ref[...] = jnp.full(high_ref.shape, -jnp.inf, F32)
    for c in range(CHUNKS):
        copies[c].wait()
        for g in range(c * share, (c + 1) * share):
            r, i = row_ref[g], slot_ref[g]
            scores = lax.dot_general(
                absorbed_ref[r], held_ref[g], (((1,), (1,)), ((), ())), preferred_element_type=F32
            )
            scores = (scores + dot(rotary_ref[r], rope_ref[g])) * factor
            position = i * page + lax.broadcasted_iota(jnp.int32, scores.shape, 1)
            scores = jnp.where(position < length_ref[r], scores, -jnp.inf)
            scores_ref[r, i] = scores
            high_ref[r] = jnp.maximum(high_ref[r], scores)
    done = []
    for r in range(own):
        score_new = new_scores[r]
        top = jnp.maximum(score_new, jnp.max(high_ref[r], axis=1, keepdims=True))
        weight_new = jnp.exp2(score_new - top)
        total = None
        for i in range(slots):
            weights = jnp.exp2(scores_ref[r, i] - top)
            scores_ref[r, i] = weights
            total = weights if total is None else total + weights
        inverse = 1.0 / (jnp.sum(total, axis=1, keepdims=True) + weight_new)
        new = new_ref[r : r + 1, :].astype(F32)
        summed = (weight_new * inverse).astype(BF16).astype(F32) * new
        for i in range(0, slots, GROUP):
            group = range(i, i + GROUP)
            probs = jnp.concatenate(
                [(scores_ref[r, k] * inverse).astype(BF16) for k in group], axis=1
            )
            latents = jnp.concatenate([held_ref[table_ref[r, k]] for k in group], axis=0)
            summed += dot(probs, latents)
        done.append(summed.astype(BF16))
    count = sources // Y
    together = jnp.concatenate(done, axis=0)
    for j in range(heads):

        def place(i, j=j):
            source = (i // own) % Y * count + i // (own * Y)
            return i % own * all_heads + source * heads + j

        piece = dot(one_hot(sources * own, rows, place), together)
        out_ref[:, j * width : (j + 1) * width] = piece.astype(BF16)


def attend(lengths, table, query, heads, new_latent, new_rope, cache_latent, cache_rope):
    own, slots = table.shape
    pool, page, width = cache_latent.shape
    rope_dim = cache_rope.shape[1]
    rows = query.shape[0]
    all_heads = rows // own
    return pl.pallas_call(
        attend_kernel,
        out_shape=jax.ShapeDtypeStruct((rows // heads, heads * width), BF16),
        in_specs=[SCALARS, SCALARS] + [WHOLE] * 3 + [IN_HBM, WHOLE],
        out_specs=WHOLE,
        scratch_shapes=[
            pltpu.VMEM((own, slots, all_heads, page), F32),
            pltpu.VMEM(cache_latent.shape, BF16),
            pltpu.VMEM((own, all_heads, page), F32),
            pltpu.VMEM((own, all_heads, width), BF16),
            pltpu.VMEM((own, all_heads, rope_dim), BF16),
            pltpu.SMEM((pool,), jnp.int32),
            pltpu.SMEM((pool,), jnp.int32),
            pltpu.SemaphoreType.DMA((CHUNKS,)),
        ],
        compiler_params=params(24),
        name="attend",
    )(lengths, table, query, new_latent, new_rope, in_hbm(cache_latent), cache_rope)


def values_kernel(parts, me_ref, attn_ref, *refs):
    uv_refs, (out_ref, sorted_ref, spread_ref) = refs[:Y], refs[Y:]
    heads, width, value_dim = uv_refs[0].shape
    per = value_dim // parts
    rows = attn_ref.shape[0]
    group = rows // Y
    own = group // Z

    def place(i):
        return (i % group) // own * (Y * own) + (i // group) * own + i % own

    ordered = dot(one_hot(rows, rows, place), attn_ref[...]).astype(BF16)
    for y in range(Y):
        sorted_ref[y] = ordered[y * group : (y + 1) * group]
    columns = heads * value_dim
    source = lax.broadcasted_iota(jnp.int32, (columns, columns), 0)
    column = lax.broadcasted_iota(jnp.int32, (columns, columns), 1)
    inner = source % value_dim
    target = (inner // per) * (heads * per) + (source // value_dim) * per + inner % per
    move = (column == target).astype(F32).astype(BF16)
    for k in range(Y):
        y = lax.rem(me_ref[0] + (Y - k), Y)
        rows_y = sorted_ref[y]
        value = jnp.concatenate(
            [
                dot(rows_y[:, j * width : (j + 1) * width], uv_refs[k][j]).astype(BF16)
                for j in range(heads)
            ],
            axis=1,
        )
        spread_ref[y] = dot(value, move).astype(BF16)
    share = heads * per
    for y in range(Y):
        for d in range(parts):
            start = (d * Y + y) * share
            out_ref[:, start : start + share] = spread_ref[y, :, d * share : (d + 1) * share]


def project_values(me, attn, pieces, parts):
    heads, _, value_dim = pieces[0].shape
    rows = attn.shape[0]
    group = rows // Y

    def kernel(*refs):
        values_kernel(parts, *refs)

    return pl.pallas_call(
        kernel,
        out_shape=jax.ShapeDtypeStruct((group, Y * heads * value_dim), BF16),
        in_specs=[SCALARS] + [WHOLE] * (1 + Y),
        out_specs=WHOLE,
        scratch_shapes=[
            pltpu.VMEM((Y, group, attn.shape[1]), BF16),
            pltpu.VMEM((Y, group, heads * value_dim), BF16),
        ],
        compiler_params=params(16),
        name="values",
    )(me, attn, *pieces)


def mix_kernel(values_ref, weights_ref, out_ref, held_ref, sem):
    steps, sources, per, columns = weights_ref.shape
    depth = sources * per
    copies = [
        pltpu.make_async_copy(weights_ref.at[d], held_ref.at[d], sem.at[d]) for d in range(steps)
    ]
    for copy in copies:
        copy.start()
    total = None
    for d in range(steps):
        copies[d].wait()
        block = held_ref[d].reshape(depth, columns)
        term = dot(values_ref[:, d * depth : (d + 1) * depth], block)
        total = term if total is None else total + term
    parts, _, width = out_ref.shape
    for z in range(parts):
        out_ref[z] = total[:, z * width : (z + 1) * width].astype(BF16)


def mix(values, weights, parts):
    rows = values.shape[0]
    steps, _, _, columns = weights.shape
    return pl.pallas_call(
        mix_kernel,
        out_shape=jax.ShapeDtypeStruct((parts, rows, columns // parts), BF16),
        in_specs=[WHOLE, IN_HBM],
        out_specs=WHOLE,
        scratch_shapes=[
            pltpu.VMEM(weights.shape, BF16),
            pltpu.SemaphoreType.DMA((steps,)),
        ],
        compiler_params=params(20),
        name="mix",
    )(values, in_hbm(weights))


def finish_kernel(terms_ref, out_ref):
    total = terms_ref[0].astype(F32)
    for z in range(1, terms_ref.shape[0]):
        total += terms_ref[z].astype(F32)
    out_ref[...] = total.astype(BF16)


def finish(terms):
    return pl.pallas_call(
        finish_kernel,
        out_shape=jax.ShapeDtypeStruct(terms.shape[1:], BF16),
        in_specs=[WHOLE],
        out_specs=WHOLE,
        compiler_params=params(8),
        name="finish",
    )(terms)


def shift_y(x, along):
    pairs = [(y * Z + z, (y + along) % Y * Z + z) for y in range(Y) for z in range(Z)]
    return lax.ppermute(x, "head", pairs)


def angles(lengths, rope_dim, heads):
    half = rope_dim // 2
    freq = 10000.0 ** (-2.0 * jnp.arange(half, dtype=F32) / (2 * half))
    angle = lengths.astype(F32)[:, None] * freq
    cos, sin = jnp.cos(angle), jnp.sin(angle)
    cos = jnp.tile(cos, (1, 2 * heads))
    sin = jnp.tile(jnp.concatenate([-sin, sin], axis=1), (1, heads))
    return cos, sin


def body(
    q_latent,
    w_qnope,
    w_qrope,
    w_uk,
    w_uv,
    w_out,
    cache_latent,
    cache_rope,
    new_latent,
    new_rope,
    lengths,
    page_table,
):
    rows = q_latent.shape[0]
    heads = w_uk.shape[0]
    own = page_table.shape[0]
    width_all = w_out.shape[2]
    dp_count = lax.axis_size("dp")
    sources = lax.axis_size("head")
    depth = w_out.shape[0] * w_out.shape[1]

    head = lax.axis_index("head")
    y = head // Z
    both, cuts = prepare(w_qnope, w_qrope, w_out.reshape(depth, width_all))
    weights = lax.all_gather(both, "dp", axis=0, tiled=True)
    panel = lax.all_to_all(cuts, "head", 0, 0, tiled=True, axis_index_groups=Y_GROUPS)
    panel = lax.all_gather(panel, "dp", axis=0)
    uv = [w_uv] + [shift_y(w_uv, k) for k in range(1, Y)]

    cos, sin = angles(lengths, cache_rope.shape[1], heads)
    query = project(q_latent, weights, w_uk, cos, sin, dp_count)
    query = query.reshape(sources, own * heads, query.shape[1])
    query = lax.all_to_all(query, "head", 0, 0, tiled=True).reshape(rows * heads, -1)
    own_lengths = lax.dynamic_slice_in_dim(lengths, head * own, own)
    attn = attend(
        own_lengths, page_table, query, heads, new_latent, new_rope, cache_latent, cache_rope
    )
    attn = attn.reshape(Z, Y * own, attn.shape[1])
    attn = lax.all_to_all(attn, "head", 0, 0, tiled=True, axis_index_groups=Z_GROUPS)
    values = project_values(y.reshape(1), attn.reshape(rows, -1), uv, dp_count)
    values = jnp.broadcast_to(values[None], (Y,) + values.shape)
    values = lax.all_to_all(values, "head", 0, 0, tiled=True, axis_index_groups=Y_GROUPS)
    term = mix(values.reshape(rows, -1), panel, Z)
    term = lax.all_to_all(term, "head", 0, 0, tiled=True, axis_index_groups=Z_GROUPS)
    return finish(term)


def solution(mesh):
    in_specs = (
        P("dp", None),
        P("dp", "head"),
        P("dp", "head"),
        P("head", None, None),
        P("head", None, None),
        P("head", "dp", None),
        P(("dp", "head"), None, None),
        P(("dp", "head"), None, None),
        P(("dp", "head"), None),
        P(("dp", "head"), None),
        P("dp"),
        P(("dp", "head"), None),
    )
    out_specs = P("dp", "head")
    return jax.shard_map(body, mesh=mesh, in_specs=in_specs, out_specs=out_specs, check_vma=False)
```

time: 1520 us -> 130 us (0.09)
  waiting for transfers between devices: 1300 us -> 32.5 us
  local copies, waits for them, and re-layouts: 93.2 us -> 2.41 us
  matrix products: 34.3 us -> 0 us
  Pallas kernels: 0 us -> 21.9 us
    reduce_scatter x1 -> x0, waiting for transfers between devices: 1280 us -> none  [body(): lax.psum_scatter(term, ('dp', 'head'), scatter_dimension=0, tiled=True)]
    gather x24 -> x0, local copies, waits for them, and re-layouts: 78.3 us -> none  [the longest x16 63.9 us: fetch(): latent_block = cache_latent[chosen].reshape(own_rows, keys, latent_dim)]
    dot_general x31 -> x0, matrix products: 34.3 us -> none  [the longest x8 10.2 us: value_block(): jnp.einsum('rhk,rkl->rhl', block_probs, latent_block, preferred_element_t...]
    all_to_all x1 -> x3, blocking collectives: 16.4 us -> 39.3 us  [the longest x1 17 us: body(): lax.all_to_all(cuts, 'head', 0, 0, tiled=True, axis_index_groups=Y_GROUPS)]
    pallas_call x0 -> x6, Pallas kernels: none -> 21.9 us  [the longest x1 9.72 us: attend(): pl.pallas_call(attend_kernel, out_shape=jax.ShapeDtypeStruct((rows // hea...]
  transfers between devices with their start and end apart: 5 -> 7, of which waited for: 5 -> 5; matrix products, arithmetic and copies ran while one was open for 0% -> 1% of each run, Pallas kernels for 0% -> 12%
where the time goes in v2:
time: 130 us; the launch traced here: 129 us
  blocking collectives  39.3 us (30%)
  waiting for transfers between devices  32.5 us (25%)
  Pallas kernels  21.9 us (17%)
  starting transfers between devices  18.4 us (14%)
  between operations  13.5 us (10%)
  local copies, waits for them, and re-layouts  2.41 us (2%)
    all_to_all x1, blocking collectives, body(): lax.all_to_all(cuts, 'head', 0, 0, tiled=True, axis_index_groups=Y_GROUPS)  17 us
    all_gather x1, waiting for transfers between devices, body(): weights = lax.all_gather(both, 'dp', axis=0, tiled=True)  13.1 us
    all_to_all x1, blocking collectives, body(): lax.all_to_all(term, 'head', 0, 0, tiled=True, axis_index_groups=Z_GROUPS)  12.9 us
    all_to_all x1, starting transfers between devices, body(): lax.all_to_all(query, 'head', 0, 0, tiled=True).reshape(rows * heads, -1)  10.2 us
    pallas_call x1, Pallas kernels, attend(): pl.pallas_call(attend_kernel, out_shape=jax.ShapeDtypeStruct((rows // hea...  9.72 us
    all_to_all x1, blocking collectives, body(): lax.all_to_all(values, 'head', 0, 0, tiled=True, axis_index_groups=Y_GROUPS)  9.4 us
    all_to_all x1, waiting for transfers between devices, body(): lax.all_to_all(query, 'head', 0, 0, tiled=True).reshape(rows * heads, -1)  8.3 us
    all_to_all x1, waiting for transfers between devices, body(): lax.all_to_all(attn, 'head', 0, 0, tiled=True, axis_index_groups=Z_GROUPS)  7.77 us
  transfers between devices with their start and end apart: 7, of which 5 were waited for; matrix products, arithmetic and copies ran while one was open for 1% of the time, Pallas kernels for 12%

profile of v2, /device:TPU:8, one launch (start us, length us, event | category | flops | bytes accessed | tf_op | source)
XLA Modules:
  0.0 129.0 jit_solution(8722707380897816597)
XLA Ops:
  6.6 0.0 all-gather.4.cloned.1.call-start
  6.6 2.2 %prepare.1 = (bf16[192,768]{1,0:T(8,128)(2,1)}, bf16[4,64,1792]{2,1,0:T(8,128)(2,1)S(1)}) custom-call(bf16[192,512]{1,0:T(8,128)(2,1)} %nope_hbm.1, bf16[192,256]{1,0:T(8,128)(2,1)} %rope_hbm.1, bf16[64,7168]{1,0:T(8,128)(2,1)} %bitcast.13), custom_call_target="tpu_custom_call" | custom-call | tf_op jit(solution)/shard_map/prepare/pallas_call | solution.py:54
  8.8 0.0 all-gather.4.cloned.1.call-update
  8.9 0.0 all-gather.6.cloned.1.call-start
  8.9 17.0 %all_to_all.25 = bf16[4,64,1792]{2,1,0:T(8,128)(2,1)} all-to-all(bf16[4,64,1792]{2,1,0:T(8,128)(2,1)S(1)} %get-tuple-element.8), channel_id=1, replica_groups={{0,8,16,24},{1,9,17,25},{2,10,18,26},{3,11,19,27},{4,12,20,28},{5,13,21..., dimensions={0} | all-to-all | bytes 1835008 | tf_op jit(solution)/shard_map/all_to_all | solution.py:404
  26.0 0.0 all-gather.6.cloned.1.call-update
  26.0 0.7 convert_element_type.3
  26.6 0.1 fusion
  26.8 0.1 copy.15
  26.9 0.1 tile.21.sin_ref
  27.1 0.1 copy.16.cos_ref
  27.2 13.1 %all-gather.4.cloned.1.call-done.weights_hbm = bf16[1536,768]{1,0:T(8,128)(2,1)} async-done(((bf16[192,768]{1,0:T(8,128)(2,1)}), bf16[1536,768]{1,0:T(8,128)(2,1)}) %all-gather.4.cloned.1.call-update) | async-done | bytes 2359312 | tf_op jit(solution)/shard_map/all_gather | solution.py:403
  40.3 1.0 copy-done.1
  41.3 0.9 copy-done.3
  42.2 3.6 %project.1 = bf16[256,640]{1,0:T(8,128)(2,1)} custom-call(bf16[64,1536]{1,0:T(8,128)(2,1)S(1)} %copy-done.3, bf16[1536,768]{1,0:T(8,128)(2,1)} %all-gather.4.cloned.1.call-done.weights_hbm, bf16[4,128,512]{2,1,0:T(8,128)(2,1)S(1)} %copy-done.1, f32[64,256]{1,0:T(8,128)S(1)} %copy.16.cos_ref, f32[64,256]{1,0:T(8,128)S(1)} %tile.21.sin_ref), custom_call_target="tpu_custom_call" | custom-call | tf_op jit(solution)/shard_map/project/pallas_call | solution.py:123
  45.8 10.2 %all-to-all-start = ((bf16[32,8,640]{2,1,0:T(8,128)(2,1)}), bf16[32,8,640]{2,1,0:T(8,128)(2,1)S(1)}, u32[]{:S(2)}, u32[]{:S(2)}) async-start(bf16[32,8,640]{2,1,0:T(8,128)(2,1)} %bitcast.3), calls=%async_computation | async-start | bytes 655360 | tf_op jit(solution)/shard_map/all_to_all | solution.py:411
  56.0 2.2 %collective-permute-start.1 = (bf16[4,512,128]{2,1,0:T(8,128)(2,1)S(1)}, bf16[4,512,128]{2,1,0:T(8,128)(2,1)S(1)}, u32[]{:S(2)}, u32[]{:S(2)}) collective-permute-start(bf16[4,512,128]{2,1,0:T(8,128)(2,1)S(1)} %copy-done.2), channel_id=1, source_target_pairs={{0,16},{1,17},{2,18},{3,19},{4,20},{5,21},{6,22},{7,23},{8,24},{9,... | collective-permute-start | bytes 1572872 | tf_op jit(solution)/shard_map/ppermute | solution.py:365
  58.2 0.0 collective-permute-start
  58.2 2.0 %collective-permute-start.2 = (bf16[4,512,128]{2,1,0:T(8,128)(2,1)S(1)}, bf16[4,512,128]{2,1,0:T(8,128)(2,1)}, u32[]{:S(2)}, u32[]{:S(2)}) collective-permute-start(bf16[4,512,128]{2,1,0:T(8,128)(2,1)S(1)} %copy-done.2), channel_id=1, source_target_pairs={{0,24},{1,25},{2,26},{3,27},{4,28},{5,29},{6,30},{7,31},{8,0},{9,1... | collective-permute-start | bytes 1572872 | tf_op jit(solution)/shard_map/ppermute | solution.py:365
  60.2 0.1 dynamic_slice.3.length_ref
  60.3 8.3 %all-to-all-done = bf16[32,8,640]{2,1,0:T(8,128)(2,1)S(1)} async-done(((bf16[32,8,640]{2,1,0:T(8,128)(2,1)}), bf16[32,8,640]{2,1,0:T(8,128)(2,1)S(1)}, u32[]{:S(2)}, u32[]{:S(2)}) %all-to-all-start) | async-done | bytes 327712 | tf_op jit(solution)/shard_map/all_to_all | solution.py:411
  68.6 9.7 %attend.1 = bf16[64,2048]{1,0:T(8,128)(2,1)} custom-call(s32[2]{0:T(128)S(1)} %dynamic_slice.3.length_ref, s32[2,32]{1,0:T(2,128)S(1)} %copy-done.5, bf16[256,640]{1,0:T(8,128)(2,1)S(1)} %bitcast.9, bf16[2,512]{1,0:T(2,128)(2,1)S(1)} %copy-done.4, bf16[2,64]{1,0:T(2,128)(2,1)S(1)} %copy-done.6, bf16[64,128,512]{2,1,0:T(8,128)(2,1)} %latent_hbm.1, ...), custom_call_target="tpu_custom_call" | custom-call | tf_op jit(solution)/shard_map/attend/pallas_call | solution.py:229
  78.4 4.0 %all-to-all-start.1 = ((bf16[8,8,2048]{2,1,0:T(8,128)(2,1)}), bf16[8,8,2048]{2,1,0:T(8,128)(2,1)S(1)}, u32[]{:S(2)}, u32[]{:S(2)}) async-start(bf16[8,8,2048]{2,1,0:T(8,128)(2,1)} %bitcast.5), calls=%async_computation.1 | async-start | bytes 524288 | tf_op jit(solution)/shard_map/all_to_all | solution.py:417
  82.3 0.0 collective-permute-done.1.refs_4_
  82.3 2.5 %collective-permute-done.refs_3_ = bf16[4,512,128]{2,1,0:T(8,128)(2,1)S(1)} collective-permute-done((bf16[4,512,128]{2,1,0:T(8,128)(2,1)S(1)}, bf16[4,512,128]{2,1,0:T(8,128)(2,1)S(1)}, u32[]{:S(2)}, u32[]{:S(2)}) %collective-permute-start) | collective-permute-done | bytes 524320 | tf_op jit(solution)/shard_map/ppermute | solution.py:365
  84.8 0.8 collective-permute-done.2.refs_5_
  85.6 7.8 %all-to-all-done.1 = bf16[8,8,2048]{2,1,0:T(8,128)(2,1)S(1)} async-done(((bf16[8,8,2048]{2,1,0:T(8,128)(2,1)}), bf16[8,8,2048]{2,1,0:T(8,128)(2,1)S(1)}, u32[]{:S(2)}, u32[]{:S(2)}) %all-to-all-start.1) | async-done | bytes 262176 | tf_op jit(solution)/shard_map/all_to_all | solution.py:417
  93.4 2.2 %values.1 = bf16[16,2048]{1,0:T(8,128)(2,1)S(1)} custom-call(s32[1]{0:T(128)} %bitcast.refs_0_, bf16[64,2048]{1,0:T(8,128)(2,1)S(1)} %bitcast.11, bf16[4,512,128]{2,1,0:T(8,128)(2,1)S(1)} %copy-done.2, bf16[4,512,128]{2,1,0:T(8,128)(2,1)S(1)} %collective-permute-done.refs_3_, bf16[4,512,128]{2,1,0:T(8,128)(2,1)S(1)} %collective-permute-done.1.refs_4_, ...), custom_call_target="tpu_custom_call" | custom-call | tf_op jit(solution)/shard_map/values/pallas_call | solution.py:295
  95.6 9.4 %all_to_all.26 = bf16[4,16,2048]{2,1,0:T(8,128)(2,1)S(1)} all-to-all(bf16[4,16,2048]{2,1,0:T(8,128)(2,1)S(1)} %broadcast_in_dim.2), channel_id=1, replica_groups={{0,8,16,24},{1,9,17,25},{2,10,18,26},{3,11,19,27},{4,12,20,28},{5,13,21..., dimensions={0} | all-to-all | bytes 524288 | tf_op jit(solution)/shard_map/all_to_all | solution.py:420
  105.0 3.5 %mix.1 = bf16[8,64,224]{2,1,0:T(8,128)(2,1)S(1)} custom-call(bf16[64,2048]{1,0:T(8,128)(2,1)S(1)} %bitcast.10, bf16[8,4,64,1792]{3,2,1,0:T(8,128)(2,1)} %bitcast.12), custom_call_target="tpu_custom_call" | custom-call | tf_op jit(solution)/shard_map/mix/pallas_call | solution.py:331
  108.6 12.9 %all_to_all.27.terms_ref = bf16[8,64,224]{2,1,0:T(8,128)(2,1)S(1)} all-to-all(bf16[8,64,224]{2,1,0:T(8,128)(2,1)S(1)} %mix.1), channel_id=1, replica_groups={{0,1,2,3,4,5,6,7},{8,9,10,11,12,13,14,15},{16,17,18,19,20,21,22,23},{24..., dimensions={0} | all-to-all | bytes 458752 | tf_op jit(solution)/shard_map/all_to_all | solution.py:422
  121.5 0.7 finish.1
  (20 shorter events, 0.1 us)
Async XLA Ops:
  6.5 53.7 %copy-start.7 = (s32[64]{0:T(128)S(1)}, s32[64]{0:T(128)}, u32[]{:S(2)}) copy-start(s32[64]{0:T(128)} %param.22) | copy-start | bytes 772
  6.5 49.5 %copy-start.2 = (bf16[4,512,128]{2,1,0:T(8,128)(2,1)S(1)}, bf16[4,512,128]{2,1,0:T(8,128)(2,1)}, u32[]{:S(2)}) copy-start(bf16[4,512,128]{2,1,0:T(8,128)(2,1)} %refs_2_.1) | copy-start | bytes 1572868
  6.5 62.1 %copy-start.5 = (s32[2,32]{1,0:T(2,128)S(1)}, s32[2,32]{1,0:T(2,128)}, u32[]{:S(2)}) copy-start(s32[2,32]{1,0:T(2,128)} %table_ref.1) | copy-start | bytes 772
  6.5 62.1 %copy-start.6 = (bf16[2,64]{1,0:T(2,128)(2,1)S(1)}, bf16[2,64]{1,0:T(2,128)(2,1)}, u32[]{:S(2)}) copy-start(bf16[2,64]{1,0:T(2,128)(2,1)} %new_rope_ref.1) | copy-start | bytes 772
  6.5 62.1 %copy-start.4 = (bf16[2,512]{1,0:T(2,128)(2,1)S(1)}, bf16[2,512]{1,0:T(2,128)(2,1)}, u32[]{:S(2)}) copy-start(bf16[2,512]{1,0:T(2,128)(2,1)} %new_ref.1) | copy-start | bytes 6148
  6.5 62.1 %copy-start = (bf16[64,64,128]{2,1,0:T(8,128)(2,1)S(1)}, bf16[64,64,128]{2,1,0:T(8,128)(2,1)}, u32[]{:S(2)}) copy-start(bf16[64,64,128]{2,1,0:T(8,128)(2,1)} %rope_ref.1) | copy-start | bytes 3145732
  6.6 33.7 %all-gather.4.cloned.1.call-start = ((), (), s32[]{:S(2)}) async-start(), calls=%async_computation.5 | async-start | bytes 2654208 | tf_op jit(solution)/shard_map/all_gather | solution.py:403
  8.9 96.2 %all-gather.6.cloned.1.call-start = ((), (), s32[]{:S(2)}) async-start(), calls=%async_computation.6 | async-start | bytes 8257536 | tf_op jit(solution)/shard_map/all_gather | solution.py:405
  40.3 1.0 copy-start.1
  41.3 0.9 copy-start.3
  45.8 22.8 %all-to-all-start = ((bf16[32,8,640]{2,1,0:T(8,128)(2,1)}), bf16[32,8,640]{2,1,0:T(8,128)(2,1)S(1)}, u32[]{:S(2)}, u32[]{:S(2)}) async-start(bf16[32,8,640]{2,1,0:T(8,128)(2,1)} %bitcast.3), calls=%async_computation | async-start | bytes 655360 | tf_op jit(solution)/shard_map/all_to_all | solution.py:411
  56.0 26.3 %collective-permute-start.1 = (bf16[4,512,128]{2,1,0:T(8,128)(2,1)S(1)}, bf16[4,512,128]{2,1,0:T(8,128)(2,1)S(1)}, u32[]{:S(2)}, u32[]{:S(2)}) collective-permute-start(bf16[4,512,128]{2,1,0:T(8,128)(2,1)S(1)} %copy-done.2), channel_id=1, source_target_pairs={{0,16},{1,17},{2,18},{3,19},{4,20},{5,21},{6,22},{7,23},{8,24},{9,... | collective-permute-start | bytes 1572872 | tf_op jit(solution)/shard_map/ppermute | solution.py:365
  58.2 26.6 %collective-permute-start = (bf16[4,512,128]{2,1,0:T(8,128)(2,1)S(1)}, bf16[4,512,128]{2,1,0:T(8,128)(2,1)S(1)}, u32[]{:S(2)}, u32[]{:S(2)}) collective-permute-start(bf16[4,512,128]{2,1,0:T(8,128)(2,1)S(1)} %copy-done.2), channel_id=1, source_target_pairs={{0,8},{1,9},{2,10},{3,11},{4,12},{5,13},{6,14},{7,15},{8,16},{9,17... | collective-permute-start | bytes 1572872 | tf_op jit(solution)/shard_map/ppermute | solution.py:365
  58.2 27.4 %collective-permute-start.2 = (bf16[4,512,128]{2,1,0:T(8,128)(2,1)S(1)}, bf16[4,512,128]{2,1,0:T(8,128)(2,1)}, u32[]{:S(2)}, u32[]{:S(2)}) collective-permute-start(bf16[4,512,128]{2,1,0:T(8,128)(2,1)S(1)} %copy-done.2), channel_id=1, source_target_pairs={{0,24},{1,25},{2,26},{3,27},{4,28},{5,29},{6,30},{7,31},{8,0},{9,1... | collective-permute-start | bytes 1572872 | tf_op jit(solution)/shard_map/ppermute | solution.py:365
  78.4 15.0 %all-to-all-start.1 = ((bf16[8,8,2048]{2,1,0:T(8,128)(2,1)}), bf16[8,8,2048]{2,1,0:T(8,128)(2,1)S(1)}, u32[]{:S(2)}, u32[]{:S(2)}) async-start(bf16[8,8,2048]{2,1,0:T(8,128)(2,1)} %bitcast.5), calls=%async_computation.1 | async-start | bytes 524288 | tf_op jit(solution)/shard_map/all_to_all | solution.py:417
Sparse Core Ops, SparseCore 0:
  9.2 31.0 all-gather.3
  42.1 48.4 all-gather.5

commit v3 on v2

--- a/solution.py
+++ b/solution.py
@@ -33,36 +33,73 @@
     return pltpu.CompilerParams(vmem_limit_bytes=mib * 1024 * 1024)
 
 
-def prepare_kernel(nope_hbm, rope_hbm, weights_hbm, both_ref, cut_ref, sem):
+def prepare_kernel(
+    place_ref, y_ref, latent_hbm, nope_hbm, rope_hbm, weights_hbm, both_ref, out_ref, *refs
+):
+    cut_refs, (held_ref, sem) = refs[:Y], refs[Y:]
     width = nope_hbm.shape[1]
-    columns = cut_ref.shape[2]
+    columns = cut_refs[0].shape[1]
     copies = [
         pltpu.make_async_copy(nope_hbm, both_ref.at[:, :width], sem.at[0]),
         pltpu.make_async_copy(rope_hbm, both_ref.at[:, width:], sem.at[1]),
+        pltpu.make_async_copy(latent_hbm, held_ref, sem.at[2]),
     ]
-    for y in range(Y):
-        source = weights_hbm.at[:, pl.ds(y * columns, columns)]
-        copies.append(pltpu.make_async_copy(source, cut_ref.at[y], sem.at[2 + y]))
+    for k in range(Y):
+        start = pl.multiple_of(lax.rem(y_ref[0] + k, Y) * columns, 128)
+        source = weights_hbm.at[:, pl.ds(start, columns)]
+        copies.append(pltpu.make_async_copy(source, cut_refs[k], sem.at[3 + k]))
+    for copy in copies:
+        copy.start()
+    copies[2].wait()
+    parts, _, depth = out_ref.shape
+    for d in range(parts):
+        out_ref[place_ref[d]] = held_ref[:, d * depth : (d + 1) * depth]
+    for copy in copies[:2] + copies[3:]:
+        copy.wait()
+
+
+def prepare(place, y, q_latent, w_qnope, w_qrope, weights):
+    rows, width = q_latent.shape
+    parts = place.shape[0]
+    cut = jax.ShapeDtypeStruct((weights.shape[0], weights.shape[1] // Y), BF16)
+    arrays = [in_hbm(a) for a in (q_latent, w_qnope, w_qrope, weights)]
+    return pl.pallas_call(
+        prepare_kernel,
+        out_shape=(
+            jax.ShapeDtypeStruct((w_qnope.shape[0], w_qnope.shape[1] + w_qrope.shape[1]), BF16),
+            jax.ShapeDtypeStruct((parts, rows, width // parts), BF16),
+        )
+        + (cut,) * Y,
+        in_specs=[SCALARS] * 2 + [IN_HBM] * 4,
+        out_specs=(WHOLE,) * (2 + Y),
+        scratch_shapes=[pltpu.VMEM(q_latent.shape, BF16), pltpu.SemaphoreType.DMA((3 + Y,))],
+        compiler_params=params(8),
+        name="prepare",
+    )(place, y, *arrays)
+
+
+def stack_kernel(y_ref, *refs):
+    pieces, (out_ref, sem) = refs[:Y], refs[Y:]
+    copies = []
+    for k in range(Y):
+        target = out_ref.at[lax.rem(y_ref[0] + (Y - k), Y)]
+        copies.append(pltpu.make_async_copy(pieces[k], target, sem.at[k]))
     for copy in copies:
         copy.start()
     for copy in copies:
         copy.wait()
 
 
-def prepare(w_qnope, w_qrope, weights):
-    depth = w_qnope.shape[0]
-    return pl.pallas_call(
-        prepare_kernel,
-        out_shape=(
-            jax.ShapeDtypeStruct((depth, w_qnope.shape[1] + w_qrope.shape[1]), BF16),
-            jax.ShapeDtypeStruct((Y, weights.shape[0], weights.shape[1] // Y), BF16),
-        ),
-        in_specs=[IN_HBM] * 3,
-        out_specs=(WHOLE, WHOLE),
-        scratch_shapes=[pltpu.SemaphoreType.DMA((2 + Y,))],
+def stack(y, pieces):
+    return pl.pallas_call(
+        stack_kernel,
+        out_shape=jax.ShapeDtypeStruct((Y,) + pieces[0].shape, BF16),
+        in_specs=[SCALARS] + [pl.BlockSpec(memory_space=pl.ANY)] * Y,
+        out_specs=IN_HBM,
+        scratch_shapes=[pltpu.SemaphoreType.DMA((Y,))],
         compiler_params=params(8),
-        name="prepare",
-    )(*[in_hbm(a) for a in (w_qnope, w_qrope, weights)])
+        name="stack",
+    )(y, *pieces)
 
 
 def one_hot(rows, columns, place, keep=None):
@@ -74,22 +111,16 @@
     return hit.astype(F32).astype(BF16)
 
 
-def project_kernel(
-    latent_ref, weights_hbm, uk_ref, cos_ref, sin_ref, out_ref, held_ref, sem
-):
+def project_kernel(pieces, latent_ref, *refs):
+    piece_refs = refs[:pieces]
+    uk_hbm, cos_ref, sin_ref, out_ref, uk_ref, sem = refs[pieces:]
     heads, nope_dim, width = uk_ref.shape
-    rows = latent_ref.shape[0]
-    steps, depth, _ = held_ref.shape
-    copies = [
-        pltpu.make_async_copy(weights_hbm.at[pl.ds(d * depth, depth)], held_ref.at[d], sem.at[d])
-        for d in range(steps)
-    ]
-    for copy in copies:
-        copy.start()
+    rows = latent_ref.shape[1]
+    copy = pltpu.make_async_copy(uk_hbm, uk_ref, sem)
+    copy.start()
     both = None
-    for d in range(steps):
-        copies[d].wait()
-        term = dot(latent_ref[:, d * depth : (d + 1) * depth], held_ref[d])
+    for i in range(pieces):
+        term = dot(latent_ref[i], piece_refs[i][...])
         both = term if both is None else both + term
     query = both[:, : heads * nope_dim].astype(BF16)
     turned = both[:, heads * nope_dim :]
@@ -104,6 +135,7 @@
     )
     rotated = (turned * cos_ref[...] + swapped * sin_ref[...]).astype(BF16)
     blank = jnp.zeros((rows, out_ref.shape[1] - width - rope_dim), BF16)
+    copy.wait()
     total = None
     for j in range(heads):
         part = dot(query[:, j * nope_dim : (j + 1) * nope_dim], uk_ref[j]).astype(BF16)
@@ -116,22 +148,23 @@
     out_ref[...] = total.astype(BF16)
 
 
-def project(latent, weights, w_uk, cos, sin, parts):
+def project(latent, pieces, w_uk, cos, sin):
     heads, _, width = w_uk.shape
-    rows = latent.shape[0]
+    rows = latent.shape[1]
     full = width + 128 * pl.cdiv(cos.shape[1] // heads, 128)
-    return pl.pallas_call(
-        project_kernel,
+
+    def kernel(*refs):
+        project_kernel(len(pieces), *refs)
+
+    return pl.pallas_call(
+        kernel,
         out_shape=jax.ShapeDtypeStruct((rows * heads, full), BF16),
-        in_specs=[WHOLE, IN_HBM] + [WHOLE] * 3,
+        in_specs=[WHOLE] * (1 + len(pieces)) + [IN_HBM] + [WHOLE] * 2,
         out_specs=WHOLE,
-        scratch_shapes=[
-            pltpu.VMEM((parts, weights.shape[0] // parts, weights.shape[1]), BF16),
-            pltpu.SemaphoreType.DMA((parts,)),
-        ],
+        scratch_shapes=[pltpu.VMEM(w_uk.shape, BF16), pltpu.SemaphoreType.DMA(())],
         compiler_params=params(16),
         name="project",
-    )(latent, in_hbm(weights), w_uk, cos, sin)
+    )(latent, *pieces, in_hbm(w_uk), cos, sin)
 
 
 def attend_kernel(
@@ -247,8 +280,11 @@
 
 
 def values_kernel(parts, me_ref, attn_ref, *refs):
-    uv_refs, (out_ref, sorted_ref, spread_ref) = refs[:Y], refs[Y:]
-    heads, width, value_dim = uv_refs[0].shape
+    uv_hbms, (out_ref, sorted_ref, spread_ref, uv_refs, sem) = refs[:Y], refs[Y:]
+    copies = [pltpu.make_async_copy(uv_hbms[k], uv_refs.at[k], sem.at[k]) for k in range(Y)]
+    for copy in copies:
+        copy.start()
+    heads, width, value_dim = uv_hbms[0].shape
     per = value_dim // parts
     rows = attn_ref.shape[0]
     group = rows // Y
@@ -269,9 +305,10 @@
     for k in range(Y):
         y = lax.rem(me_ref[0] + (Y - k), Y)
         rows_y = sorted_ref[y]
+        copies[k].wait()
         value = jnp.concatenate(
             [
-                dot(rows_y[:, j * width : (j + 1) * width], uv_refs[k][j]).astype(BF16)
+                dot(rows_y[:, j * width : (j + 1) * width], uv_refs[k, j]).astype(BF16)
                 for j in range(heads)
             ],
             axis=1,
@@ -295,15 +332,17 @@
     return pl.pallas_call(
         kernel,
         out_shape=jax.ShapeDtypeStruct((group, Y * heads * value_dim), BF16),
-        in_specs=[SCALARS] + [WHOLE] * (1 + Y),
+        in_specs=[SCALARS, WHOLE] + [IN_HBM] * Y,
         out_specs=WHOLE,
         scratch_shapes=[
             pltpu.VMEM((Y, group, attn.shape[1]), BF16),
             pltpu.VMEM((Y, group, heads * value_dim), BF16),
+            pltpu.VMEM((Y,) + pieces[0].shape, BF16),
+            pltpu.SemaphoreType.DMA((Y,)),
         ],
         compiler_params=params(16),
         name="values",
-    )(me, attn, *pieces)
+    )(me, attn, *[in_hbm(piece) for piece in pieces])
 
 
 def mix_kernel(values_ref, weights_ref, out_ref, held_ref, sem):
@@ -360,9 +399,35 @@
     )(terms)
 
 
+def shift_dp(x, along, across):
+    chips = lax.axis_size("dp") // 2
+    pairs = [
+        (p * 2 + c, (p + along * (1 - 2 * c)) % chips * 2 + (c ^ across))
+        for p in range(chips)
+        for c in range(2)
+    ]
+    return lax.ppermute(x, "dp", pairs)
+
+
 def shift_y(x, along):
     pairs = [(y * Z + z, (y + along) % Y * Z + z) for y in range(Y) for z in range(Z)]
     return lax.ppermute(x, "head", pairs)
+
+
+def piece_places():
+    me = lax.axis_index("dp")
+    chips = lax.axis_size("dp") // 2
+    chip, core = me // 2, me % 2
+    sign = 1 - 2 * core
+    other = lax.rem(core + 1, 2)
+    steps = [0, -1, 1, 2]
+    origins = [lax.rem(chip + sign * step + chips, chips) * 2 + core for step in steps]
+    origins += [lax.rem(chip - sign * step + 2 * chips, chips) * 2 + other for step in steps]
+    origins = jnp.stack(origins)
+    parts = jnp.arange(2 * chips)
+    return jnp.sum(
+        jnp.where(origins[None, :] == parts[:, None], parts[None, :], 0), axis=1
+    ).astype(jnp.int32)
 
 
 def angles(lengths, rope_dim, heads):
@@ -399,14 +464,19 @@
 
     head = lax.axis_index("head")
     y = head // Z
-    both, cuts = prepare(w_qnope, w_qrope, w_out.reshape(depth, width_all))
-    weights = lax.all_gather(both, "dp", axis=0, tiled=True)
-    panel = lax.all_to_all(cuts, "head", 0, 0, tiled=True, axis_index_groups=Y_GROUPS)
-    panel = lax.all_gather(panel, "dp", axis=0)
+    cos, sin = angles(lengths, cache_rope.shape[1], heads)
+    y_scalar = y.reshape(1)
+    flat = w_out.reshape(depth, width_all)
+    both, latent, *cuts = prepare(piece_places(), y_scalar, q_latent, w_qnope, w_qrope, flat)
+    ahead, behind = shift_dp(both, 1, 0), shift_dp(both, -1, 0)
+    cuts = [cuts[0]] + [shift_y(cuts[k], k) for k in range(1, Y)]
+    ahead, behind, cuts, cos, sin = lax.optimization_barrier((ahead, behind, cuts, cos, sin))
+    same = [both, ahead, behind, shift_dp(ahead, 1, 0)]
+    other = [shift_dp(piece, 0, 1) for piece in same[:3]] + [shift_dp(ahead, 1, 1)]
+    panel = lax.all_gather(stack(y_scalar, cuts), "dp", axis=0)
     uv = [w_uv] + [shift_y(w_uv, k) for k in range(1, Y)]
 
-    cos, sin = angles(lengths, cache_rope.shape[1], heads)
-    query = project(q_latent, weights, w_uk, cos, sin, dp_count)
+    query = project(latent, same + other, w_uk, cos, sin)
     query = query.reshape(sources, own * heads, query.shape[1])
     query = lax.all_to_all(query, "head", 0, 0, tiled=True).reshape(rows * heads, -1)
     own_lengths = lax.dynamic_slice_in_dim(lengths, head * own, own)
@@ -415,7 +485,7 @@
     )
     attn = attn.reshape(Z, Y * own, attn.shape[1])
     attn = lax.all_to_all(attn, "head", 0, 0, tiled=True, axis_index_groups=Z_GROUPS)
-    values = project_values(y.reshape(1), attn.reshape(rows, -1), uv, dp_count)
+    values = project_values(y_scalar, attn.reshape(rows, -1), uv, dp_count)
     values = jnp.broadcast_to(values[None], (Y,) + values.shape)
     values = lax.all_to_all(values, "head", 0, 0, tiled=True, axis_index_groups=Y_GROUPS)
     term = mix(values.reshape(rows, -1), panel, Z)

time: 130 us -> 135 us (1.038)
  blocking collectives: 39.3 us -> 21.8 us
  starting transfers between devices: 18.4 us -> 32.2 us
  waiting for transfers between devices: 32.5 us -> 36.7 us
  local copies, waits for them, and re-layouts: 2.41 us -> 5.27 us
  Pallas kernels: 21.9 us -> 23.6 us
    all_to_all x1 -> x0, blocking collectives: 17 us -> none  [body(): lax.all_to_all(cuts, 'head', 0, 0, tiled=True, axis_index_groups=Y_GROUPS)]
    all_gather x2 -> x1, waiting for transfers between devices: 13.1 us -> 0.01 us  [body(): panel = lax.all_gather(stack(y_scalar, cuts), 'dp', axis=0)]
    ppermute x0 -> x7, waiting for transfers between devices: none -> 7.03 us  [shift_dp(): return lax.ppermute(x, 'dp', pairs)]
    ppermute x0 -> x7, starting transfers between devices: none -> 5.49 us  [shift_dp(): return lax.ppermute(x, 'dp', pairs)]
    ppermute x3 -> x6, starting transfers between devices: 4.22 us -> 9.15 us  [shift_y(): return lax.ppermute(x, 'head', pairs)]
    ppermute x3 -> x6, waiting for transfers between devices: 3.28 us -> 8.19 us  [shift_y(): return lax.ppermute(x, 'head', pairs)]
    all_to_all x1, waiting for transfers between devices: 8.3 us -> 11.1 us  [body(): lax.all_to_all(query, 'head', 0, 0, tiled=True).reshape(rows * heads, -1)]
    all_to_all x1, waiting for transfers between devices: 7.77 us -> 10.4 us  [body(): lax.all_to_all(attn, 'head', 0, 0, tiled=True, axis_index_groups=Z_GROUPS)]
  transfers between devices with their start and end apart: 7 -> 16, of which waited for: 5 -> 7; matrix products, arithmetic and copies ran while one was open for 1% -> 2% of each run, Pallas kernels for 12% -> 12%
where the time goes in v3:
time: 135 us; the launch traced here: 134 us
  waiting for transfers between devices  36.7 us (27%)
  starting transfers between devices  32.2 us (24%)
  Pallas kernels  23.6 us (17%)
  blocking collectives  21.8 us (16%)
  between operations  13.7 us (10%)
  local copies, waits for them, and re-layouts  5.27 us (4%)
    all_to_all x1, blocking collectives, body(): lax.all_to_all(term, 'head', 0, 0, tiled=True, axis_index_groups=Z_GROUPS)  12.9 us
    all_to_all x1, starting transfers between devices, body(): lax.all_to_all(query, 'head', 0, 0, tiled=True).reshape(rows * heads, -1)  11.5 us
    all_to_all x1, waiting for transfers between devices, body(): lax.all_to_all(query, 'head', 0, 0, tiled=True).reshape(rows * heads, -1)  11.1 us
    all_to_all x1, waiting for transfers between devices, body(): lax.all_to_all(attn, 'head', 0, 0, tiled=True, axis_index_groups=Z_GROUPS)  10.4 us
    pallas_call x1, Pallas kernels, attend(): pl.pallas_call(attend_kernel, out_shape=jax.ShapeDtypeStruct((rows // hea...  10.1 us
    ppermute x6, starting transfers between devices, shift_y(): return lax.ppermute(x, 'head', pairs)  9.15 us
    all_to_all x1, blocking collectives, body(): lax.all_to_all(values, 'head', 0, 0, tiled=True, axis_index_groups=Y_GROUPS)  8.88 us
    ppermute x6, waiting for transfers between devices, shift_y(): return lax.ppermute(x, 'head', pairs)  8.19 us
  transfers between devices with their start and end apart: 16, of which 7 were waited for; matrix products, arithmetic and copies ran while one was open for 2% of the time, Pallas kernels for 12%

profile of v3, /device:TPU:8, one launch (start us, length us, event | category | flops | bytes accessed | tf_op | source)
XLA Modules:
  0.0 134.2 jit_solution(13957802357043125396)
XLA Ops:
  6.9 2.7 %prepare.1 = (bf16[192,768]{1,0:T(8,128)(2,1)S(1)}, bf16[8,64,192]{2,1,0:T(8,128)(2,1)S(1)}, bf16[64,1792]{1,0:T(8,128)(2,1)S(1)}, bf16[64,1792]{1,0:T(8,128)(2,...) custom-call(s32[8]{0:T(128)S(1)} %select_reduce_fusion.place_ref, s32[1]{0:T(128)} %bitcast.y_ref.refs_0_, ...), custom_call_target="tpu_custom_call" | custom-call | tf_op jit(solution)/shard_map/prepare/pallas_call | solution.py:66
  9.7 0.7 copy-done.2
  10.4 2.8 %collective-permute-start.1 = (bf16[192,768]{1,0:T(8,128)(2,1)S(1)}, bf16[192,768]{1,0:T(8,128)(2,1)S(1)}, u32[]{:S(2)}, u32[]{:S(2)}) collective-permute-start(bf16[192,768]{1,0:T(8,128)(2,1)S(1)} %get-tuple-element.20.refs_1_), channel_id=1, source_target_pairs={{0,192},{32,96},{64,0},{96,160},{128,64},{160,224},{192,128},{224,... | collective-permute-start | bytes 884744 | tf_op jit(solution)/shard_map/ppermute | solution.py:409
  13.1 1.6 %collective-permute-start.2 = (bf16[64,1792]{1,0:T(8,128)(2,1)}, bf16[64,1792]{1,0:T(8,128)(2,1)S(1)}, u32[]{:S(2)}, u32[]{:S(2)}) collective-permute-start(bf16[64,1792]{1,0:T(8,128)(2,1)} %get-tuple-element.22), channel_id=1, source_target_pairs={{0,8},{1,9},{2,10},{3,11},{4,12},{5,13},{6,14},{7,15},{8,16},{9,17... | collective-permute-start | bytes 688136 | tf_op jit(solution)/shard_map/ppermute | solution.py:414
  14.7 1.9 %collective-permute-start.3 = (bf16[64,1792]{1,0:T(8,128)(2,1)S(1)}, bf16[64,1792]{1,0:T(8,128)(2,1)S(1)}, u32[]{:S(2)}, u32[]{:S(2)}) collective-permute-start(bf16[64,1792]{1,0:T(8,128)(2,1)S(1)} %get-tuple-element.23), channel_id=1, source_target_pairs={{0,16},{1,17},{2,18},{3,19},{4,20},{5,21},{6,22},{7,23},{8,24},{9,... | collective-permute-start | bytes 688136 | tf_op jit(solution)/shard_map/ppermute | solution.py:414
  16.6 1.4 %collective-permute-start.4 = (bf16[64,1792]{1,0:T(8,128)(2,1)S(1)}, bf16[64,1792]{1,0:T(8,128)(2,1)S(1)}, u32[]{:S(2)}, u32[]{:S(2)}) collective-permute-start(bf16[64,1792]{1,0:T(8,128)(2,1)S(1)} %get-tuple-element.24), channel_id=1, source_target_pairs={{0,24},{1,25},{2,26},{3,27},{4,28},{5,29},{6,30},{7,31},{8,0},{9,1... | collective-permute-start | bytes 688136 | tf_op jit(solution)/shard_map/ppermute | solution.py:414
  18.1 0.7 convert_element_type.3
  19.1 2.7 %collective-permute-done.2.refs_1_ = bf16[64,1792]{1,0:T(8,128)(2,1)S(1)} collective-permute-done((bf16[64,1792]{1,0:T(8,128)(2,1)}, bf16[64,1792]{1,0:T(8,128)(2,1)S(1)}, u32[]{:S(2)}, u32[]{:S(2)}) %collective-permute-start.2) | collective-permute-done | bytes 229408 | tf_op jit(solution)/shard_map/ppermute | solution.py:414
  21.8 2.9 %collective-permute-done.3.refs_2_ = bf16[64,1792]{1,0:T(8,128)(2,1)S(1)} collective-permute-done((bf16[64,1792]{1,0:T(8,128)(2,1)S(1)}, bf16[64,1792]{1,0:T(8,128)(2,1)S(1)}, u32[]{:S(2)}, u32[]{:S(2)}) %collective-permute-start.3) | collective-permute-done | bytes 229408 | tf_op jit(solution)/shard_map/ppermute | solution.py:414
  24.8 2.6 %collective-permute-done.4.refs_3_ = bf16[64,1792]{1,0:T(8,128)(2,1)S(1)} collective-permute-done((bf16[64,1792]{1,0:T(8,128)(2,1)S(1)}, bf16[64,1792]{1,0:T(8,128)(2,1)S(1)}, u32[]{:S(2)}, u32[]{:S(2)}) %collective-permute-start.4) | collective-permute-done | bytes 229408 | tf_op jit(solution)/shard_map/ppermute | solution.py:414
  27.3 0.7 tile.8
  28.0 1.0 stack.37
  29.2 0.5 collective-permute-start.8
  29.7 1.7 %collective-permute-start.7 = (bf16[192,768]{1,0:T(8,128)(2,1)S(1)}, bf16[192,768]{1,0:T(8,128)(2,1)S(1)}, u32[]{:S(2)}, u32[]{:S(2)}) collective-permute-start(bf16[192,768]{1,0:T(8,128)(2,1)S(1)} %collective-permute-done.refs_2_), channel_id=1, source_target_pairs={{0,32},{32,0},{64,96},{96,64},{128,160},{160,128},{192,224},{224,1... | collective-permute-start | bytes 884744 | tf_op jit(solution)/shard_map/ppermute | solution.py:409
  31.8 1.6 %copy.18.refs_10_ = f32[64,256]{1,0:T(8,128)} copy(f32[64,256]{0,1:T(8,128)} %bitcast.22) | data formatting | bytes 131072 | tf_op jit(solution)/shard_map/optimization_barrier | solution.py:473
  33.4 2.4 %collective-permute-done.9.refs_8_ = bf16[192,768]{1,0:T(8,128)(2,1)S(1)} collective-permute-done((bf16[192,768]{1,0:T(8,128)(2,1)S(1)}, bf16[192,768]{1,0:T(8,128)(2,1)S(1)}, u32[]{:S(2)}, u32[]{:S(2)}) %collective-permute-start.9) | collective-permute-done | bytes 294944 | tf_op jit(solution)/shard_map/ppermute | solution.py:409
  35.8 4.6 %collective-permute-done.5.refs_4_ = bf16[192,768]{1,0:T(8,128)(2,1)S(1)} collective-permute-done((bf16[192,768]{1,0:T(8,128)(2,1)S(1)}, bf16[192,768]{1,0:T(8,128)(2,1)S(1)}, u32[]{:S(2)}, u32[]{:S(2)}) %collective-permute-start.5) | collective-permute-done | bytes 294944 | tf_op jit(solution)/shard_map/ppermute | solution.py:409
  40.5 0.8 copy-done.1
  41.3 1.0 copy-done.3
  42.3 2.9 %project.1 = bf16[256,640]{1,0:T(8,128)(2,1)} custom-call(bf16[8,64,192]{2,1,0:T(8,128)(2,1)S(1)} %copy-done.3, bf16[192,768]{1,0:T(8,128)(2,1)S(1)} %get-tuple-element.20.refs_1_, bf16[192,768]{1,0:T(8,128)(2,1)S(1)} %collective-permute-done.refs_2_, bf16[192,768]{1,0:T(8,128)(2,1)S(1)} %collective-permute-done.1.refs_3_, ...), custom_call_target="tpu_custom_call" | custom-call | tf_op jit(solution)/shard_map/project/pallas_call | solution.py:159
  45.2 11.5 %all-to-all-start = ((bf16[32,8,640]{2,1,0:T(8,128)(2,1)}), bf16[32,8,640]{2,1,0:T(8,128)(2,1)S(1)}, u32[]{:S(2)}, u32[]{:S(2)}) async-start(bf16[32,8,640]{2,1,0:T(8,128)(2,1)} %bitcast.11), calls=%async_computation | async-start | bytes 655360 | tf_op jit(solution)/shard_map/all_to_all | solution.py:481
  56.7 2.2 %collective-permute-start.11 = (bf16[4,512,128]{2,1,0:T(8,128)(2,1)}, bf16[4,512,128]{2,1,0:T(8,128)(2,1)S(1)}, u32[]{:S(2)}, u32[]{:S(2)}) collective-permute-start(bf16[4,512,128]{2,1,0:T(8,128)(2,1)} %refs_2_.1), channel_id=1, source_target_pairs={{0,16},{1,17},{2,18},{3,19},{4,20},{5,21},{6,22},{7,23},{8,24},{9,... | collective-permute-start | bytes 1572872 | tf_op jit(solution)/shard_map/ppermute | solution.py:414
  58.9 2.0 %collective-permute-start.12 = (bf16[4,512,128]{2,1,0:T(8,128)(2,1)}, bf16[4,512,128]{2,1,0:T(8,128)(2,1)S(1)}, u32[]{:S(2)}, u32[]{:S(2)}) collective-permute-start(bf16[4,512,128]{2,1,0:T(8,128)(2,1)} %refs_2_.1), channel_id=1, source_target_pairs={{0,24},{1,25},{2,26},{3,27},{4,28},{5,29},{6,30},{7,31},{8,0},{9,1... | collective-permute-start | bytes 1572872 | tf_op jit(solution)/shard_map/ppermute | solution.py:414
  61.0 11.1 %all-to-all-done = bf16[32,8,640]{2,1,0:T(8,128)(2,1)S(1)} async-done(((bf16[32,8,640]{2,1,0:T(8,128)(2,1)}), bf16[32,8,640]{2,1,0:T(8,128)(2,1)S(1)}, u32[]{:S(2)}, u32[]{:S(2)}) %all-to-all-start) | async-done | bytes 327712 | tf_op jit(solution)/shard_map/all_to_all | solution.py:481
  72.1 10.1 %attend.1 = bf16[64,2048]{1,0:T(8,128)(2,1)} custom-call(s32[2]{0:T(128)S(1)} %dynamic_slice.3.length_ref, s32[2,32]{1,0:T(2,128)S(1)} %copy-done.5, bf16[256,640]{1,0:T(8,128)(2,1)S(1)} %bitcast.17, bf16[2,512]{1,0:T(2,128)(2,1)S(1)} %copy-done.4, bf16[2,64]{1,0:T(2,128)(2,1)S(1)} %copy-done.6, bf16[64,128,512]{2,1,0:T(8,128)(2,1)} %latent_hbm.3, ...), custom_call_target="tpu_custom_call" | custom-call | tf_op jit(solution)/shard_map/attend/pallas_call | solution.py:262
  82.2 6.1 %all-to-all-start.1 = ((bf16[8,8,2048]{2,1,0:T(8,128)(2,1)}), bf16[8,8,2048]{2,1,0:T(8,128)(2,1)S(1)}, u32[]{:S(2)}, u32[]{:S(2)}) async-start(bf16[8,8,2048]{2,1,0:T(8,128)(2,1)} %bitcast.13), calls=%async_computation.1 | async-start | bytes 524288 | tf_op jit(solution)/shard_map/all_to_all | solution.py:487
  88.3 10.4 %all-to-all-done.1 = bf16[8,8,2048]{2,1,0:T(8,128)(2,1)S(1)} async-done(((bf16[8,8,2048]{2,1,0:T(8,128)(2,1)}), bf16[8,8,2048]{2,1,0:T(8,128)(2,1)S(1)}, u32[]{:S(2)}, u32[]{:S(2)}) %all-to-all-start.1) | async-done | bytes 262176 | tf_op jit(solution)/shard_map/all_to_all | solution.py:487
  98.7 2.6 %values.1 = bf16[16,2048]{1,0:T(8,128)(2,1)S(1)} custom-call(s32[1]{0:T(128)} %bitcast.y_ref.refs_0_, bf16[64,2048]{1,0:T(8,128)(2,1)S(1)} %bitcast.19, bf16[4,512,128]{2,1,0:T(8,128)(2,1)} %refs_2_.1, bf16[4,512,128]{2,1,0:T(8,128)(2,1)} %copy-done.8, bf16[4,512,128]{2,1,0:T(8,128)(2,1)} %copy-done.7, bf16[4,512,128]{2,1,0:T(8,128)(2,1)} %copy-done.9), custom_call_target="tpu_custom_call" | custom-call | tf_op jit(solution)/shard_map/values/pallas_call | solution.py:332
  101.4 8.9 %all_to_all.20 = bf16[4,16,2048]{2,1,0:T(8,128)(2,1)S(1)} all-to-all(bf16[4,16,2048]{2,1,0:T(8,128)(2,1)S(1)} %broadcast_in_dim.16), channel_id=1, replica_groups={{0,8,16,24},{1,9,17,25},{2,10,18,26},{3,11,19,27},{4,12,20,28},{5,13,21..., dimensions={0} | all-to-all | bytes 524288 | tf_op jit(solution)/shard_map/all_to_all | solution.py:490
  110.3 3.5 %mix.1 = bf16[8,64,224]{2,1,0:T(8,128)(2,1)S(1)} custom-call(bf16[64,2048]{1,0:T(8,128)(2,1)S(1)} %bitcast.18, bf16[8,4,64,1792]{3,2,1,0:T(8,128)(2,1)} %bitcast.20), custom_call_target="tpu_custom_call" | custom-call | tf_op jit(solution)/shard_map/mix/pallas_call | solution.py:370
  113.9 12.9 %all_to_all.21.terms_ref = bf16[8,64,224]{2,1,0:T(8,128)(2,1)S(1)} all-to-all(bf16[8,64,224]{2,1,0:T(8,128)(2,1)S(1)} %mix.1), channel_id=1, replica_groups={{0,1,2,3,4,5,6,7},{8,9,10,11,12,13,14,15},{16,17,18,19,20,21,22,23},{24..., dimensions={0} | all-to-all | bytes 458752 | tf_op jit(solution)/shard_map/all_to_all | solution.py:492
  126.7 0.7 finish.1
  (45 shorter events, 1.4 us)
Async XLA Ops:
  6.5 54.4 %copy-start.10 = (s32[64]{0:T(128)S(1)}, s32[64]{0:T(128)}, u32[]{:S(2)}) copy-start(s32[64]{0:T(128)} %param.22) | copy-start | bytes 772
  6.5 65.6 %copy-start.5 = (s32[2,32]{1,0:T(2,128)S(1)}, s32[2,32]{1,0:T(2,128)}, u32[]{:S(2)}) copy-start(s32[2,32]{1,0:T(2,128)} %table_ref.1) | copy-start | bytes 772
  6.5 65.6 %copy-start.6 = (bf16[2,64]{1,0:T(2,128)(2,1)S(1)}, bf16[2,64]{1,0:T(2,128)(2,1)}, u32[]{:S(2)}) copy-start(bf16[2,64]{1,0:T(2,128)(2,1)} %new_rope_ref.1) | copy-start | bytes 772
  6.5 65.6 %copy-start.4 = (bf16[2,512]{1,0:T(2,128)(2,1)S(1)}, bf16[2,512]{1,0:T(2,128)(2,1)}, u32[]{:S(2)}) copy-start(bf16[2,512]{1,0:T(2,128)(2,1)} %new_ref.1) | copy-start | bytes 6148
  6.5 65.6 %copy-start = (bf16[64,64,128]{2,1,0:T(8,128)(2,1)S(1)}, bf16[64,64,128]{2,1,0:T(8,128)(2,1)}, u32[]{:S(2)}) copy-start(bf16[64,64,128]{2,1,0:T(8,128)(2,1)} %rope_ref.1) | copy-start | bytes 3145732
  6.5 103.8 %all-gather.3.cloned.1.call-start = ((), (), s32[]{:S(2)}) async-start(), calls=%async_computation.4 | async-start | bytes 8257536 | tf_op jit(solution)/shard_map/all_gather | solution.py:476
  9.7 0.7 copy-start.2
  10.4 17.0 %collective-permute-start.1 = (bf16[192,768]{1,0:T(8,128)(2,1)S(1)}, bf16[192,768]{1,0:T(8,128)(2,1)S(1)}, u32[]{:S(2)}, u32[]{:S(2)}) collective-permute-start(bf16[192,768]{1,0:T(8,128)(2,1)S(1)} %get-tuple-element.20.refs_1_), channel_id=1, source_target_pairs={{0,192},{32,96},{64,0},{96,160},{128,64},{160,224},{192,128},{224,... | collective-permute-start | bytes 884744 | tf_op jit(solution)/shard_map/ppermute | solution.py:409
  13.1 14.2 %collective-permute-start = (bf16[192,768]{1,0:T(8,128)(2,1)S(1)}, bf16[192,768]{1,0:T(8,128)(2,1)S(1)}, u32[]{:S(2)}, u32[]{:S(2)}) collective-permute-start(bf16[192,768]{1,0:T(8,128)(2,1)S(1)} %get-tuple-element.20.refs_1_), channel_id=1, source_target_pairs={{0,64},{32,224},{64,128},{96,32},{128,192},{160,96},{192,0},{224,1... | collective-permute-start | bytes 884744 | tf_op jit(solution)/shard_map/ppermute | solution.py:409
  13.1 8.7 %collective-permute-start.2 = (bf16[64,1792]{1,0:T(8,128)(2,1)}, bf16[64,1792]{1,0:T(8,128)(2,1)S(1)}, u32[]{:S(2)}, u32[]{:S(2)}) collective-permute-start(bf16[64,1792]{1,0:T(8,128)(2,1)} %get-tuple-element.22), channel_id=1, source_target_pairs={{0,8},{1,9},{2,10},{3,11},{4,12},{5,13},{6,14},{7,15},{8,16},{9,17... | collective-permute-start | bytes 688136 | tf_op jit(solution)/shard_map/ppermute | solution.py:414
  14.7 10.0 %collective-permute-start.3 = (bf16[64,1792]{1,0:T(8,128)(2,1)S(1)}, bf16[64,1792]{1,0:T(8,128)(2,1)S(1)}, u32[]{:S(2)}, u32[]{:S(2)}) collective-permute-start(bf16[64,1792]{1,0:T(8,128)(2,1)S(1)} %get-tuple-element.23), channel_id=1, source_target_pairs={{0,16},{1,17},{2,18},{3,19},{4,20},{5,21},{6,22},{7,23},{8,24},{9,... | collective-permute-start | bytes 688136 | tf_op jit(solution)/shard_map/ppermute | solution.py:414
  16.6 10.7 %collective-permute-start.4 = (bf16[64,1792]{1,0:T(8,128)(2,1)S(1)}, bf16[64,1792]{1,0:T(8,128)(2,1)S(1)}, u32[]{:S(2)}, u32[]{:S(2)}) collective-permute-start(bf16[64,1792]{1,0:T(8,128)(2,1)S(1)} %get-tuple-element.24), channel_id=1, source_target_pairs={{0,24},{1,25},{2,26},{3,27},{4,28},{5,29},{6,30},{7,31},{8,0},{9,1... | collective-permute-start | bytes 688136 | tf_op jit(solution)/shard_map/ppermute | solution.py:414
  29.1 4.4 %collective-permute-start.6 = (bf16[192,768]{1,0:T(8,128)(2,1)S(1)}, bf16[192,768]{1,0:T(8,128)(2,1)S(1)}, u32[]{:S(2)}, u32[]{:S(2)}) collective-permute-start(bf16[192,768]{1,0:T(8,128)(2,1)S(1)} %get-tuple-element.20.refs_1_), channel_id=1, source_target_pairs={{0,32},{32,0},{64,96},{96,64},{128,160},{160,128},{192,224},{224,1... | collective-permute-start | bytes 884744 | tf_op jit(solution)/shard_map/ppermute | solution.py:409
  29.2 4.3 %collective-permute-start.8 = (bf16[192,768]{1,0:T(8,128)(2,1)S(1)}, bf16[192,768]{1,0:T(8,128)(2,1)S(1)}, u32[]{:S(2)}, u32[]{:S(2)}) collective-permute-start(bf16[192,768]{1,0:T(8,128)(2,1)S(1)} %collective-permute-done.1.refs_3_), channel_id=1, source_target_pairs={{0,32},{32,0},{64,96},{96,64},{128,160},{160,128},{192,224},{224,1... | collective-permute-start | bytes 884744 | tf_op jit(solution)/shard_map/ppermute | solution.py:409
  29.7 6.1 %collective-permute-start.9 = (bf16[192,768]{1,0:T(8,128)(2,1)S(1)}, bf16[192,768]{1,0:T(8,128)(2,1)S(1)}, u32[]{:S(2)}, u32[]{:S(2)}) collective-permute-start(bf16[192,768]{1,0:T(8,128)(2,1)S(1)} %collective-permute-done.refs_2_), channel_id=1, source_target_pairs={{0,96},{32,192},{64,160},{96,0},{128,224},{160,64},{192,32},{224,1... | collective-permute-start | bytes 884744 | tf_op jit(solution)/shard_map/ppermute | solution.py:409
  29.7 6.1 %collective-permute-start.7 = (bf16[192,768]{1,0:T(8,128)(2,1)S(1)}, bf16[192,768]{1,0:T(8,128)(2,1)S(1)}, u32[]{:S(2)}, u32[]{:S(2)}) collective-permute-start(bf16[192,768]{1,0:T(8,128)(2,1)S(1)} %collective-permute-done.refs_2_), channel_id=1, source_target_pairs={{0,32},{32,0},{64,96},{96,64},{128,160},{160,128},{192,224},{224,1... | collective-permute-start | bytes 884744 | tf_op jit(solution)/shard_map/ppermute | solution.py:409
  31.3 9.1 %collective-permute-start.5 = (bf16[192,768]{1,0:T(8,128)(2,1)S(1)}, bf16[192,768]{1,0:T(8,128)(2,1)S(1)}, u32[]{:S(2)}, u32[]{:S(2)}) collective-permute-start(bf16[192,768]{1,0:T(8,128)(2,1)S(1)} %collective-permute-done.refs_2_), channel_id=1, source_target_pairs={{0,64},{32,224},{64,128},{96,32},{128,192},{160,96},{192,0},{224,1... | collective-permute-start | bytes 884744 | tf_op jit(solution)/shard_map/ppermute | solution.py:409
  40.5 0.8 copy-start.1
  41.3 1.0 copy-start.3
  45.2 26.9 %all-to-all-start = ((bf16[32,8,640]{2,1,0:T(8,128)(2,1)}), bf16[32,8,640]{2,1,0:T(8,128)(2,1)S(1)}, u32[]{:S(2)}, u32[]{:S(2)}) async-start(bf16[32,8,640]{2,1,0:T(8,128)(2,1)} %bitcast.11), calls=%async_computation | async-start | bytes 655360 | tf_op jit(solution)/shard_map/all_to_all | solution.py:481
  56.7 31.5 %collective-permute-start.11 = (bf16[4,512,128]{2,1,0:T(8,128)(2,1)}, bf16[4,512,128]{2,1,0:T(8,128)(2,1)S(1)}, u32[]{:S(2)}, u32[]{:S(2)}) collective-permute-start(bf16[4,512,128]{2,1,0:T(8,128)(2,1)} %refs_2_.1), channel_id=1, source_target_pairs={{0,16},{1,17},{2,18},{3,19},{4,20},{5,21},{6,22},{7,23},{8,24},{9,... | collective-permute-start | bytes 1572872 | tf_op jit(solution)/shard_map/ppermute | solution.py:414
  58.9 29.3 %collective-permute-start.10 = (bf16[4,512,128]{2,1,0:T(8,128)(2,1)}, bf16[4,512,128]{2,1,0:T(8,128)(2,1)S(1)}, u32[]{:S(2)}, u32[]{:S(2)}) collective-permute-start(bf16[4,512,128]{2,1,0:T(8,128)(2,1)} %refs_2_.1), channel_id=1, source_target_pairs={{0,8},{1,9},{2,10},{3,11},{4,12},{5,13},{6,14},{7,15},{8,16},{9,17... | collective-permute-start | bytes 1572872 | tf_op jit(solution)/shard_map/ppermute | solution.py:414
  58.9 29.4 %collective-permute-start.12 = (bf16[4,512,128]{2,1,0:T(8,128)(2,1)}, bf16[4,512,128]{2,1,0:T(8,128)(2,1)S(1)}, u32[]{:S(2)}, u32[]{:S(2)}) collective-permute-start(bf16[4,512,128]{2,1,0:T(8,128)(2,1)} %refs_2_.1), channel_id=1, source_target_pairs={{0,24},{1,25},{2,26},{3,27},{4,28},{5,29},{6,30},{7,31},{8,0},{9,1... | collective-permute-start | bytes 1572872 | tf_op jit(solution)/shard_map/ppermute | solution.py:414
  82.2 16.5 %all-to-all-start.1 = ((bf16[8,8,2048]{2,1,0:T(8,128)(2,1)}), bf16[8,8,2048]{2,1,0:T(8,128)(2,1)S(1)}, u32[]{:S(2)}, u32[]{:S(2)}) async-start(bf16[8,8,2048]{2,1,0:T(8,128)(2,1)} %bitcast.13), calls=%async_computation.1 | async-start | bytes 524288 | tf_op jit(solution)/shard_map/all_to_all | solution.py:487
  88.3 10.5 %copy-start.7 = (bf16[4,512,128]{2,1,0:T(8,128)(2,1)}, bf16[4,512,128]{2,1,0:T(8,128)(2,1)S(1)}, u32[]{:S(2)}) copy-start(bf16[4,512,128]{2,1,0:T(8,128)(2,1)S(1)} %collective-permute-done.11.refs_4_) | copy-start | bytes 1572868
  88.3 10.5 %copy-start.8 = (bf16[4,512,128]{2,1,0:T(8,128)(2,1)}, bf16[4,512,128]{2,1,0:T(8,128)(2,1)S(1)}, u32[]{:S(2)}) copy-start(bf16[4,512,128]{2,1,0:T(8,128)(2,1)S(1)} %collective-permute-done.10.refs_3_) | copy-start | bytes 1572868
  88.3 10.4 %copy-start.9 = (bf16[4,512,128]{2,1,0:T(8,128)(2,1)}, bf16[4,512,128]{2,1,0:T(8,128)(2,1)S(1)}, u32[]{:S(2)}) copy-start(bf16[4,512,128]{2,1,0:T(8,128)(2,1)S(1)} %collective-permute-done.12.refs_5_) | copy-start | bytes 1572868
Sparse Core Ops, SparseCore 0:
  29.2 49.2 all-gather.2

commit v4 on v3

--- a/solution.py
+++ b/solution.py
@@ -33,49 +33,37 @@
     return pltpu.CompilerParams(vmem_limit_bytes=mib * 1024 * 1024)
 
 
-def prepare_kernel(
-    place_ref, y_ref, latent_hbm, nope_hbm, rope_hbm, weights_hbm, both_ref, out_ref, *refs
-):
-    cut_refs, (held_ref, sem) = refs[:Y], refs[Y:]
+def prepare_kernel(y_ref, nope_hbm, rope_hbm, weights_hbm, both_ref, *refs):
+    cut_refs, sem = refs[:Y], refs[Y]
     width = nope_hbm.shape[1]
     columns = cut_refs[0].shape[1]
     copies = [
         pltpu.make_async_copy(nope_hbm, both_ref.at[:, :width], sem.at[0]),
         pltpu.make_async_copy(rope_hbm, both_ref.at[:, width:], sem.at[1]),
-        pltpu.make_async_copy(latent_hbm, held_ref, sem.at[2]),
     ]
     for k in range(Y):
         start = pl.multiple_of(lax.rem(y_ref[0] + k, Y) * columns, 128)
         source = weights_hbm.at[:, pl.ds(start, columns)]
-        copies.append(pltpu.make_async_copy(source, cut_refs[k], sem.at[3 + k]))
+        copies.append(pltpu.make_async_copy(source, cut_refs[k], sem.at[2 + k]))
     for copy in copies:
         copy.start()
-    copies[2].wait()
-    parts, _, depth = out_ref.shape
-    for d in range(parts):
-        out_ref[place_ref[d]] = held_ref[:, d * depth : (d + 1) * depth]
-    for copy in copies[:2] + copies[3:]:
+    for copy in copies:
         copy.wait()
 
 
-def prepare(place, y, q_latent, w_qnope, w_qrope, weights):
-    rows, width = q_latent.shape
-    parts = place.shape[0]
+def prepare(y, w_qnope, w_qrope, weights):
+    depth = w_qnope.shape[0]
     cut = jax.ShapeDtypeStruct((weights.shape[0], weights.shape[1] // Y), BF16)
-    arrays = [in_hbm(a) for a in (q_latent, w_qnope, w_qrope, weights)]
     return pl.pallas_call(
         prepare_kernel,
-        out_shape=(
-            jax.ShapeDtypeStruct((w_qnope.shape[0], w_qnope.shape[1] + w_qrope.shape[1]), BF16),
-            jax.ShapeDtypeStruct((parts, rows, width // parts), BF16),
-        )
+        out_shape=(jax.ShapeDtypeStruct((depth, w_qnope.shape[1] + w_qrope.shape[1]), BF16),)
         + (cut,) * Y,
-        in_specs=[SCALARS] * 2 + [IN_HBM] * 4,
-        out_specs=(WHOLE,) * (2 + Y),
-        scratch_shapes=[pltpu.VMEM(q_latent.shape, BF16), pltpu.SemaphoreType.DMA((3 + Y,))],
+        in_specs=[SCALARS] + [IN_HBM] * 3,
+        out_specs=(WHOLE,) * (1 + Y),
+        scratch_shapes=[pltpu.SemaphoreType.DMA((2 + Y,))],
         compiler_params=params(8),
         name="prepare",
-    )(place, y, *arrays)
+    )(y, *[in_hbm(a) for a in (w_qnope, w_qrope, weights)])
 
 
 def stack_kernel(y_ref, *refs):
@@ -111,16 +99,24 @@
     return hit.astype(F32).astype(BF16)
 
 
-def project_kernel(pieces, latent_ref, *refs):
+def project_kernel(pieces, place_ref, latent_hbm, *refs):
     piece_refs = refs[:pieces]
-    uk_hbm, cos_ref, sin_ref, out_ref, uk_ref, sem = refs[pieces:]
+    uk_hbm, cos_ref, sin_ref, out_ref, held_ref, sorted_ref, uk_ref, sem = refs[pieces:]
     heads, nope_dim, width = uk_ref.shape
-    rows = latent_ref.shape[1]
-    copy = pltpu.make_async_copy(uk_hbm, uk_ref, sem)
-    copy.start()
+    rows = latent_hbm.shape[0]
+    copies = [
+        pltpu.make_async_copy(latent_hbm, held_ref, sem.at[0]),
+        pltpu.make_async_copy(uk_hbm, uk_ref, sem.at[1]),
+    ]
+    for copy in copies:
+        copy.start()
+    copies[0].wait()
+    depth = sorted_ref.shape[2]
+    for d in range(pieces):
+        sorted_ref[place_ref[d]] = held_ref[:, d * depth : (d + 1) * depth]
     both = None
     for i in range(pieces):
-        term = dot(latent_ref[i], piece_refs[i][...])
+        term = dot(sorted_ref[i], piece_refs[i][...])
         both = term if both is None else both + term
     query = both[:, : heads * nope_dim].astype(BF16)
     turned = both[:, heads * nope_dim :]
@@ -133,9 +129,11 @@
         pltpu.roll(turned, lanes - half, 1),
         pltpu.roll(turned, half, 1),
     )
-    rotated = (turned * cos_ref[...] + swapped * sin_ref[...]).astype(BF16)
+    cos = jnp.concatenate([cos_ref[...]] * (2 * heads), axis=1)
+    sin = jnp.concatenate([-sin_ref[...], sin_ref[...]] * heads, axis=1)
+    rotated = (turned * cos + swapped * sin).astype(BF16)
     blank = jnp.zeros((rows, out_ref.shape[1] - width - rope_dim), BF16)
-    copy.wait()
+    copies[1].wait()
     total = None
     for j in range(heads):
         part = dot(query[:, j * nope_dim : (j + 1) * nope_dim], uk_ref[j]).astype(BF16)
@@ -148,27 +146,33 @@
     out_ref[...] = total.astype(BF16)
 
 
-def project(latent, pieces, w_uk, cos, sin):
+def project(place, latent, pieces, w_uk, cos, sin):
     heads, _, width = w_uk.shape
-    rows = latent.shape[1]
-    full = width + 128 * pl.cdiv(cos.shape[1] // heads, 128)
+    rows = latent.shape[0]
+    count = len(pieces)
+    full = width + 128 * pl.cdiv(2 * cos.shape[1], 128)
 
     def kernel(*refs):
-        project_kernel(len(pieces), *refs)
+        project_kernel(count, *refs)
 
     return pl.pallas_call(
         kernel,
         out_shape=jax.ShapeDtypeStruct((rows * heads, full), BF16),
-        in_specs=[WHOLE] * (1 + len(pieces)) + [IN_HBM] + [WHOLE] * 2,
+        in_specs=[SCALARS, IN_HBM] + [WHOLE] * count + [IN_HBM] + [WHOLE] * 2,
         out_specs=WHOLE,
-        scratch_shapes=[pltpu.VMEM(w_uk.shape, BF16), pltpu.SemaphoreType.DMA(())],
+        scratch_shapes=[
+            pltpu.VMEM(latent.shape, BF16),
+            pltpu.VMEM((count, rows, latent.shape[1] // count), BF16),
+            pltpu.VMEM(w_uk.shape, BF16),
+            pltpu.SemaphoreType.DMA((2,)),
+        ],
         compiler_params=params(16),
         name="project",
-    )(latent, *pieces, in_hbm(w_uk), cos, sin)
+    )(place, in_hbm(latent), *pieces, in_hbm(w_uk), cos, sin)
 
 
 def attend_kernel(
-    length_ref, table_ref, query_ref, new_ref, new_rope_ref, latent_hbm, rope_ref, out_ref,
+    heads,     length_ref, table_ref, query_ref, new_ref, new_rope_ref, latent_hbm, rope_ref, out_ref,
     scores_ref, held_ref, high_ref, absorbed_ref, rotary_ref, row_ref, slot_ref, sem,
 ):
     own, slots = table_ref.shape
@@ -176,8 +180,6 @@
     rope_dim = rope_ref.shape[1]
     rows = query_ref.shape[0]
     all_heads = rows // own
-    heads = out_ref.shape[1] // width
-    sources = all_heads // heads
     factor = math.log2(math.e) / (NOPE + rope_dim) ** 0.5
     share = pool // CHUNKS
     copies = []
@@ -241,16 +243,11 @@
             latents = jnp.concatenate([held_ref[table_ref[r, k]] for k in group], axis=0)
             summed += dot(probs, latents)
         done.append(summed.astype(BF16))
-    count = sources // Y
-    together = jnp.concatenate(done, axis=0)
-    for j in range(heads):
-
-        def place(i, j=j):
-            source = (i // own) % Y * count + i // (own * Y)
-            return i % own * all_heads + source * heads + j
-
-        piece = dot(one_hot(sources * own, rows, place), together)
-        out_ref[:, j * width : (j + 1) * width] = piece.astype(BF16)
+    def place(i):
+        row = i % (own * heads) // heads
+        return row * all_heads + i // (own * heads) * heads + i % heads
+
+    out_ref[...] = dot(one_hot(rows, rows, place), jnp.concatenate(done, axis=0)).astype(BF16)
 
 
 def attend(lengths, table, query, heads, new_latent, new_rope, cache_latent, cache_rope):
@@ -259,9 +256,13 @@
     rope_dim = cache_rope.shape[1]
     rows = query.shape[0]
     all_heads = rows // own
-    return pl.pallas_call(
-        attend_kernel,
-        out_shape=jax.ShapeDtypeStruct((rows // heads, heads * width), BF16),
+
+    def kernel(*refs):
+        attend_kernel(heads, *refs)
+
+    return pl.pallas_call(
+        kernel,
+        out_shape=jax.ShapeDtypeStruct((rows, width), BF16),
         in_specs=[SCALARS, SCALARS] + [WHOLE] * 3 + [IN_HBM, WHOLE],
         out_specs=WHOLE,
         scratch_shapes=[
@@ -279,70 +280,44 @@
     )(lengths, table, query, new_latent, new_rope, in_hbm(cache_latent), cache_rope)
 
 
-def values_kernel(parts, me_ref, attn_ref, *refs):
-    uv_hbms, (out_ref, sorted_ref, spread_ref, uv_refs, sem) = refs[:Y], refs[Y:]
-    copies = [pltpu.make_async_copy(uv_hbms[k], uv_refs.at[k], sem.at[k]) for k in range(Y)]
-    for copy in copies:
-        copy.start()
-    heads, width, value_dim = uv_hbms[0].shape
+def values_kernel(parts, attn_ref, uv_hbm, out_ref, uv_ref, sem):
+    copy = pltpu.make_async_copy(uv_hbm, uv_ref, sem)
+    copy.start()
+    heads, width, value_dim = uv_ref.shape
     per = value_dim // parts
-    rows = attn_ref.shape[0]
-    group = rows // Y
-    own = group // Z
-
-    def place(i):
-        return (i % group) // own * (Y * own) + (i // group) * own + i % own
-
-    ordered = dot(one_hot(rows, rows, place), attn_ref[...]).astype(BF16)
-    for y in range(Y):
-        sorted_ref[y] = ordered[y * group : (y + 1) * group]
+    count = attn_ref.shape[0]
+    rows = count // heads
+    place = one_hot(count, count, lambda i: i % rows * heads + i // rows)
+    ordered = dot(place, attn_ref[...]).astype(BF16)
     columns = heads * value_dim
     source = lax.broadcasted_iota(jnp.int32, (columns, columns), 0)
     column = lax.broadcasted_iota(jnp.int32, (columns, columns), 1)
     inner = source % value_dim
     target = (inner // per) * (heads * per) + (source // value_dim) * per + inner % per
     move = (column == target).astype(F32).astype(BF16)
-    for k in range(Y):
-        y = lax.rem(me_ref[0] + (Y - k), Y)
-        rows_y = sorted_ref[y]
-        copies[k].wait()
-        value = jnp.concatenate(
-            [
-                dot(rows_y[:, j * width : (j + 1) * width], uv_refs[k, j]).astype(BF16)
-                for j in range(heads)
-            ],
-            axis=1,
-        )
-        spread_ref[y] = dot(value, move).astype(BF16)
-    share = heads * per
-    for y in range(Y):
-        for d in range(parts):
-            start = (d * Y + y) * share
-            out_ref[:, start : start + share] = spread_ref[y, :, d * share : (d + 1) * share]
-
-
-def project_values(me, attn, pieces, parts):
-    heads, _, value_dim = pieces[0].shape
-    rows = attn.shape[0]
-    group = rows // Y
+    copy.wait()
+    value = jnp.concatenate(
+        [dot(ordered[j * rows : (j + 1) * rows], uv_ref[j]).astype(BF16) for j in range(heads)],
+        axis=1,
+    )
+    out_ref[...] = dot(value, move).astype(BF16)
+
+
+def project_values(attn, w_uv, parts):
+    heads, _, value_dim = w_uv.shape
 
     def kernel(*refs):
         values_kernel(parts, *refs)
 
     return pl.pallas_call(
         kernel,
-        out_shape=jax.ShapeDtypeStruct((group, Y * heads * value_dim), BF16),
-        in_specs=[SCALARS, WHOLE] + [IN_HBM] * Y,
+        out_shape=jax.ShapeDtypeStruct((attn.shape[0] // heads, heads * value_dim), BF16),
+        in_specs=[WHOLE, IN_HBM],
         out_specs=WHOLE,
-        scratch_shapes=[
-            pltpu.VMEM((Y, group, attn.shape[1]), BF16),
-            pltpu.VMEM((Y, group, heads * value_dim), BF16),
-            pltpu.VMEM((Y,) + pieces[0].shape, BF16),
-            pltpu.SemaphoreType.DMA((Y,)),
-        ],
+        scratch_shapes=[pltpu.VMEM(w_uv.shape, BF16), pltpu.SemaphoreType.DMA(())],
         compiler_params=params(16),
         name="values",
-    )(me, attn, *[in_hbm(piece) for piece in pieces])
+    )(attn, in_hbm(w_uv))
 
 
 def mix_kernel(values_ref, weights_ref, out_ref, held_ref, sem):
@@ -357,7 +332,10 @@
     for d in range(steps):
         copies[d].wait()
         block = held_ref[d].reshape(depth, columns)
-        term = dot(values_ref[:, d * depth : (d + 1) * depth], block)
+        part = jnp.concatenate(
+            [values_ref[y, :, d * per : (d + 1) * per] for y in range(sources)], axis=1
+        )
+        term = dot(part, block)
         total = term if total is None else total + term
     parts, _, width = out_ref.shape
     for z in range(parts):
@@ -365,7 +343,7 @@
 
 
 def mix(values, weights, parts):
-    rows = values.shape[0]
+    rows = values.shape[1]
     steps, _, _, columns = weights.shape
     return pl.pallas_call(
         mix_kernel,
@@ -430,14 +408,11 @@
     ).astype(jnp.int32)
 
 
-def angles(lengths, rope_dim, heads):
+def angles(lengths, rope_dim):
     half = rope_dim // 2
     freq = 10000.0 ** (-2.0 * jnp.arange(half, dtype=F32) / (2 * half))
     angle = lengths.astype(F32)[:, None] * freq
-    cos, sin = jnp.cos(angle), jnp.sin(angle)
-    cos = jnp.tile(cos, (1, 2 * heads))
-    sin = jnp.tile(jnp.concatenate([-sin, sin], axis=1), (1, heads))
-    return cos, sin
+    return jnp.cos(angle), jnp.sin(angle)
 
 
 def body(
@@ -464,31 +439,37 @@
 
     head = lax.axis_index("head")
     y = head // Z
-    cos, sin = angles(lengths, cache_rope.shape[1], heads)
+    cos, sin = angles(lengths, cache_rope.shape[1])
     y_scalar = y.reshape(1)
     flat = w_out.reshape(depth, width_all)
-    both, latent, *cuts = prepare(piece_places(), y_scalar, q_latent, w_qnope, w_qrope, flat)
-    ahead, behind = shift_dp(both, 1, 0), shift_dp(both, -1, 0)
-    cuts = [cuts[0]] + [shift_y(cuts[k], k) for k in range(1, Y)]
-    ahead, behind, cuts, cos, sin = lax.optimization_barrier((ahead, behind, cuts, cos, sin))
-    same = [both, ahead, behind, shift_dp(ahead, 1, 0)]
-    other = [shift_dp(piece, 0, 1) for piece in same[:3]] + [shift_dp(ahead, 1, 1)]
+    both, *cuts = prepare(y_scalar, w_qnope, w_qrope, flat)
+    ahead, behind, beside = shift_dp(both, 1, 0), shift_dp(both, -1, 0), shift_dp(both, 0, 1)
+    cuts[1], cuts[3] = shift_y(cuts[1], 1), shift_y(cuts[3], 3)
+    ahead, behind, beside, cuts, cos, sin = lax.optimization_barrier(
+        (ahead, behind, beside, cuts, cos, sin)
+    )
+    far = shift_dp(ahead, 1, 0)
+    ahead_beside, behind_beside = shift_dp(ahead, 0, 1), shift_dp(behind, 0, 1)
+    cuts[2] = shift_y(cuts[2], 2)
+    cuts, far, ahead_beside, behind_beside = lax.optimization_barrier(
+        (cuts, far, ahead_beside, behind_beside)
+    )
     panel = lax.all_gather(stack(y_scalar, cuts), "dp", axis=0)
-    uv = [w_uv] + [shift_y(w_uv, k) for k in range(1, Y)]
-
-    query = project(latent, same + other, w_uk, cos, sin)
+    pieces = [both, ahead, behind, far]
+    pieces += [beside, ahead_beside, behind_beside, shift_dp(far, 0, 1)]
+    query = project(piece_places(), q_latent, pieces, w_uk, cos, sin)
     query = query.reshape(sources, own * heads, query.shape[1])
     query = lax.all_to_all(query, "head", 0, 0, tiled=True).reshape(rows * heads, -1)
     own_lengths = lax.dynamic_slice_in_dim(lengths, head * own, own)
     attn = attend(
         own_lengths, page_table, query, heads, new_latent, new_rope, cache_latent, cache_rope
     )
-    attn = attn.reshape(Z, Y * own, attn.shape[1])
-    attn = lax.all_to_all(attn, "head", 0, 0, tiled=True, axis_index_groups=Z_GROUPS)
-    values = project_values(y_scalar, attn.reshape(rows, -1), uv, dp_count)
+    attn = attn.reshape(sources, own * heads, attn.shape[1])
+    attn = lax.all_to_all(attn, "head", 0, 0, tiled=True).reshape(rows * heads, -1)
+    values = project_values(attn, w_uv, dp_count)
     values = jnp.broadcast_to(values[None], (Y,) + values.shape)
     values = lax.all_to_all(values, "head", 0, 0, tiled=True, axis_index_groups=Y_GROUPS)
-    term = mix(values.reshape(rows, -1), panel, Z)
+    term = mix(values, panel, Z)
     term = lax.all_to_all(term, "head", 0, 0, tiled=True, axis_index_groups=Z_GROUPS)
     return finish(term)
 

time: 135 us -> 123 us (0.911)
  blocking collectives: 21.8 us -> 39.4 us
  starting transfers between devices: 32.2 us -> 21 us
  waiting for transfers between devices: 36.7 us -> 26.2 us
  local copies, waits for them, and re-layouts: 5.27 us -> 0.2 us
  Pallas kernels: 23.6 us -> 21 us
    all_to_all x0 -> x1, blocking collectives: none -> 16.7 us  [body(): lax.all_to_all(attn, 'head', 0, 0, tiled=True).reshape(rows * heads, -1)]
    all_to_all x1 -> x0, waiting for transfers between devices: 10.4 us -> none  [body(): lax.all_to_all(attn, 'head', 0, 0, tiled=True, axis_index_groups=Z_GROUPS)]
    all_to_all x1 -> x0, starting transfers between devices: 6.05 us -> none  [body(): lax.all_to_all(attn, 'head', 0, 0, tiled=True, axis_index_groups=Z_GROUPS)]
    ppermute x7, waiting for transfers between devices: 7.03 us -> 1.28 us  [shift_dp(): return lax.ppermute(x, 'dp', pairs)]
    ppermute x6 -> x3, waiting for transfers between devices: 8.19 us -> 12.5 us  [shift_y(): return lax.ppermute(x, 'head', pairs)]
    pallas_call x3, Pallas kernels: 15.4 us -> 11.9 us  [the longest x1 8.99 us: attend(): pl.pallas_call(kernel, out_shape=jax.ShapeDtypeStruct((rows, width), BF16...]
    ppermute x6 -> x3, starting transfers between devices: 9.15 us -> 5.64 us  [shift_y(): return lax.ppermute(x, 'head', pairs)]
    unnamed x22 -> x10, local copies, waits for them, and re-layouts: 2.55 us -> 0.02 us
  transfers between devices with their start and end apart: 16 -> 12, of which waited for: 7 -> 5; matrix products, arithmetic and copies ran while one was open for 2% -> 1% of each run, Pallas kernels for 12% -> 12%
where the time goes in v4:
time: 123 us; the launch traced here: 122 us
  blocking collectives  39.4 us (32%)
  waiting for transfers between devices  26.2 us (21%)
  starting transfers between devices  21 us (17%)
  Pallas kernels  21 us (17%)
  between operations  13.5 us (11%)
    all_to_all x1, blocking collectives, body(): lax.all_to_all(attn, 'head', 0, 0, tiled=True).reshape(rows * heads, -1)  16.7 us
    all_to_all x1, blocking collectives, body(): lax.all_to_all(term, 'head', 0, 0, tiled=True, axis_index_groups=Z_GROUPS)  13.5 us
    ppermute x3, waiting for transfers between devices, shift_y(): return lax.ppermute(x, 'head', pairs)  12.5 us
    all_to_all x1, waiting for transfers between devices, body(): lax.all_to_all(query, 'head', 0, 0, tiled=True).reshape(rows * heads, -1)  12.4 us
    all_to_all x1, starting transfers between devices, body(): lax.all_to_all(query, 'head', 0, 0, tiled=True).reshape(rows * heads, -1)  11.3 us
    all_to_all x1, blocking collectives, body(): lax.all_to_all(values, 'head', 0, 0, tiled=True, axis_index_groups=Y_GROUPS)  9.19 us
    pallas_call x1, Pallas kernels, attend(): pl.pallas_call(kernel, out_shape=jax.ShapeDtypeStruct((rows, width), BF16...  8.99 us
    ppermute x3, starting transfers between devices, shift_y(): return lax.ppermute(x, 'head', pairs)  5.64 us
  transfers between devices with their start and end apart: 12, of which 5 were waited for; matrix products, arithmetic and copies ran while one was open for 1% of the time, Pallas kernels for 12%

profile of v4, /device:TPU:8, one launch (start us, length us, event | category | flops | bytes accessed | tf_op | source)
XLA Modules:
  0.0 122.3 jit_solution(3831483207462298437)
XLA Ops:
  6.5 0.0 all-gather.3.cloned.1.call-start
  6.6 1.5 %prepare.1 = (bf16[192,768]{1,0:T(8,128)(2,1)S(1)}, bf16[64,1792]{1,0:T(8,128)(2,1)S(1)}, bf16[64,1792]{1,0:T(8,128)(2,1)S(1)}, bf16[64,1792]{1,0:T(8,128)(2,1)S(1)}, bf16[64,1792]{1,0:T(8,128)(2,1)S(1)}) custom-call(s32[1]{0:T(128)} %bitcast.8.y_ref, bf16[192,512]{1,0:T(8,128)(2,1)} %nope_hbm.1, bf16[192,256]{1,0:T(8,128)(2,1)} %rope_hbm.1, ...), custom_call_target="tpu_custom_call" | custom-call | tf_op jit(solution)/shard_map/prepare/pallas_call | solution.py:57
  8.1 0.1 collective-permute-start.2
  8.2 2.8 %collective-permute-start.1 = (bf16[192,768]{1,0:T(8,128)(2,1)S(1)}, bf16[192,768]{1,0:T(8,128)(2,1)S(1)}, u32[]{:S(2)}, u32[]{:S(2)}) collective-permute-start(bf16[192,768]{1,0:T(8,128)(2,1)S(1)} %get-tuple-element.26.refs_2_), channel_id=1, source_target_pairs={{0,192},{32,96},{64,0},{96,160},{128,64},{160,224},{192,128},{224,... | collective-permute-start | bytes 884744 | tf_op jit(solution)/shard_map/ppermute | solution.py:387
  11.0 1.6 %collective-permute-start.3 = (bf16[64,1792]{1,0:T(8,128)(2,1)S(1)}, bf16[64,1792]{1,0:T(8,128)(2,1)S(1)}, u32[]{:S(2)}, u32[]{:S(2)}) collective-permute-start(bf16[64,1792]{1,0:T(8,128)(2,1)S(1)} %get-tuple-element.28), channel_id=1, source_target_pairs={{0,8},{1,9},{2,10},{3,11},{4,12},{5,13},{6,14},{7,15},{8,16},{9,17... | collective-permute-start | bytes 688136 | tf_op jit(solution)/shard_map/ppermute | solution.py:392
  12.6 0.4 collective-permute-start.4
  13.1 0.7 convert_element_type.3
  13.7 0.2 multiply_sine_fusion
  13.9 5.4 %collective-permute-done.3.refs_1_ = bf16[64,1792]{1,0:T(8,128)(2,1)S(1)} collective-permute-done((bf16[64,1792]{1,0:T(8,128)(2,1)S(1)}, bf16[64,1792]{1,0:T(8,128)(2,1)S(1)}, u32[]{:S(2)}, u32[]{:S(2)}) %collective-permute-start.3) | collective-permute-done | bytes 229408 | tf_op jit(solution)/shard_map/ppermute | solution.py:392
  19.3 0.9 collective-permute-done.4.refs_3_
  20.2 0.1 collective-permute-start.8
  20.3 0.5 collective-permute-start.7
  20.8 0.3 collective-permute-start.6
  21.1 3.6 %collective-permute-start.5 = (bf16[64,1792]{1,0:T(8,128)(2,1)S(1)}, bf16[64,1792]{1,0:T(8,128)(2,1)S(1)}, u32[]{:S(2)}, u32[]{:S(2)}) collective-permute-start(bf16[64,1792]{1,0:T(8,128)(2,1)S(1)} %get-tuple-element.35), channel_id=1, source_target_pairs={{0,16},{1,17},{2,18},{3,19},{4,20},{5,21},{6,22},{7,23},{8,24},{9,... | collective-permute-start | bytes 688136 | tf_op jit(solution)/shard_map/ppermute | solution.py:392
  24.7 6.3 %collective-permute-done.5.refs_2_ = bf16[64,1792]{1,0:T(8,128)(2,1)S(1)} collective-permute-done((bf16[64,1792]{1,0:T(8,128)(2,1)S(1)}, bf16[64,1792]{1,0:T(8,128)(2,1)S(1)}, u32[]{:S(2)}, u32[]{:S(2)}) %collective-permute-start.5) | collective-permute-done | bytes 229408 | tf_op jit(solution)/shard_map/ppermute | solution.py:392
  31.0 1.0 stack.37
  32.0 0.0 all-gather.3.cloned.1.call-update
  32.0 0.2 collective-permute-start.9
  32.2 0.1 stack.36
  32.3 0.1 select_reduce_fusion.refs_0_
  32.4 1.3 %collective-permute-done.9.refs_9_ = bf16[192,768]{1,0:T(8,128)(2,1)S(1)} collective-permute-done((bf16[192,768]{1,0:T(8,128)(2,1)S(1)}, bf16[192,768]{1,0:T(8,128)(2,1)S(1)}, u32[]{:S(2)}, u32[]{:S(2)}) %collective-permute-start.9) | collective-permute-done | bytes 294944 | tf_op jit(solution)/shard_map/ppermute | solution.py:387
  33.7 3.9 %project.1 = bf16[256,640]{1,0:T(8,128)(2,1)} custom-call(s32[8]{0:T(128)S(1)} %select_reduce_fusion.refs_0_, bf16[64,1536]{1,0:T(8,128)(2,1)} %refs_1_.3, bf16[192,768]{1,0:T(8,128)(2,1)S(1)} %get-tuple-element.26.refs_2_, bf16[192,768]{1,0:T(8,128)(2,1)S(1)} %collective-permute-done.refs_3_, bf16[192,768]{1,0:T(8,128)(2,1)S(1)} %collective-permute-done.1.refs_4_, ...), custom_call_target="tpu_custom_call" | custom-call | tf_op jit(solution)/shard_map/project/pallas_call | solution.py:158
  37.6 11.3 %all-to-all-start = ((bf16[32,8,640]{2,1,0:T(8,128)(2,1)}), bf16[32,8,640]{2,1,0:T(8,128)(2,1)S(1)}, u32[]{:S(2)}, u32[]{:S(2)}) async-start(bf16[32,8,640]{2,1,0:T(8,128)(2,1)} %bitcast.10), calls=%async_computation | async-start | bytes 655360 | tf_op jit(solution)/shard_map/all_to_all | solution.py:462
  49.0 0.1 dynamic_slice.3.refs_0_
  49.0 12.4 %all-to-all-done = bf16[32,8,640]{2,1,0:T(8,128)(2,1)S(1)} async-done(((bf16[32,8,640]{2,1,0:T(8,128)(2,1)}), bf16[32,8,640]{2,1,0:T(8,128)(2,1)S(1)}, u32[]{:S(2)}, u32[]{:S(2)}) %all-to-all-start) | async-done | bytes 327712 | tf_op jit(solution)/shard_map/all_to_all | solution.py:462
  61.4 9.0 %attend.1 = bf16[256,512]{1,0:T(8,128)(2,1)S(1)} custom-call(s32[2]{0:T(128)S(1)} %dynamic_slice.3.refs_0_, s32[2,32]{1,0:T(2,128)S(1)} %copy-done.2, bf16[256,640]{1,0:T(8,128)(2,1)S(1)} %bitcast.15, bf16[2,512]{1,0:T(2,128)(2,1)S(1)} %copy-done.1, bf16[2,64]{1,0:T(2,128)(2,1)S(1)} %copy-done.3, bf16[64,128,512]{2,1,0:T(8,128)(2,1)} %refs_5_.1, ...), custom_call_target="tpu_custom_call" | custom-call | tf_op jit(solution)/shard_map/attend/pallas_call | solution.py:263
  70.4 16.7 %all_to_all.20 = bf16[32,8,512]{2,1,0:T(8,128)(2,1)S(1)} all-to-all(bf16[32,8,512]{2,1,0:T(8,128)(2,1)S(1)} %bitcast.16), channel_id=1, replica_groups=mesh['dp'=8,'head'=32] {'head'}, dimensions={0} | all-to-all | bytes 524288 | tf_op jit(solution)/shard_map/all_to_all | solution.py:468
  87.1 1.4 %values.1 = bf16[64,512]{1,0:T(8,128)(2,1)S(1)} custom-call(bf16[256,512]{1,0:T(8,128)(2,1)S(1)} %bitcast.17, bf16[4,512,128]{2,1,0:T(8,128)(2,1)} %refs_1_.5), custom_call_target="tpu_custom_call" | custom-call | tf_op jit(solution)/shard_map/values/pallas_call | solution.py:312
  88.6 9.2 %all_to_all.21.values_ref = bf16[4,64,512]{2,1,0:T(8,128)(2,1)S(1)} all-to-all(bf16[4,64,512]{2,1,0:T(8,128)(2,1)S(1)} %broadcast_in_dim.16), channel_id=1, replica_groups={{0,8,16,24},{1,9,17,25},{2,10,18,26},{3,11,19,27},{4,12,20,28},{5,13,21..., dimensions={0} | all-to-all | bytes 524288 | tf_op jit(solution)/shard_map/all_to_all | solution.py:471
  97.8 3.6 %mix.1 = bf16[8,64,224]{2,1,0:T(8,128)(2,1)S(1)} custom-call(bf16[4,64,512]{2,1,0:T(8,128)(2,1)S(1)} %all_to_all.21.values_ref, bf16[8,4,64,1792]{3,2,1,0:T(8,128)(2,1)} %bitcast.18), custom_call_target="tpu_custom_call" | custom-call | tf_op jit(solution)/shard_map/mix/pallas_call | solution.py:348
  101.4 13.5 %all_to_all.22.terms_ref = bf16[8,64,224]{2,1,0:T(8,128)(2,1)S(1)} all-to-all(bf16[8,64,224]{2,1,0:T(8,128)(2,1)S(1)} %mix.1), channel_id=1, replica_groups={{0,1,2,3,4,5,6,7},{8,9,10,11,12,13,14,15},{16,17,18,19,20,21,22,23},{24..., dimensions={0} | all-to-all | bytes 458752 | tf_op jit(solution)/shard_map/all_to_all | solution.py:473
  114.8 0.7 finish.1
  (20 shorter events, 0.1 us)
Async XLA Ops:
  6.5 42.4 %copy-start.4 = (s32[64]{0:T(128)S(1)}, s32[64]{0:T(128)}, u32[]{:S(2)}) copy-start(s32[64]{0:T(128)} %param.22) | copy-start | bytes 772
  6.5 54.9 %copy-start.2 = (s32[2,32]{1,0:T(2,128)S(1)}, s32[2,32]{1,0:T(2,128)}, u32[]{:S(2)}) copy-start(s32[2,32]{1,0:T(2,128)} %refs_1_.4) | copy-start | bytes 772
  6.5 54.9 %copy-start.3 = (bf16[2,64]{1,0:T(2,128)(2,1)S(1)}, bf16[2,64]{1,0:T(2,128)(2,1)}, u32[]{:S(2)}) copy-start(bf16[2,64]{1,0:T(2,128)(2,1)} %refs_4_.1) | copy-start | bytes 772
  6.5 54.9 %copy-start.1 = (bf16[2,512]{1,0:T(2,128)(2,1)S(1)}, bf16[2,512]{1,0:T(2,128)(2,1)}, u32[]{:S(2)}) copy-start(bf16[2,512]{1,0:T(2,128)(2,1)} %refs_3_.1) | copy-start | bytes 6148
  6.5 54.9 %copy-start = (bf16[64,64,128]{2,1,0:T(8,128)(2,1)S(1)}, bf16[64,64,128]{2,1,0:T(8,128)(2,1)}, u32[]{:S(2)}) copy-start(bf16[64,64,128]{2,1,0:T(8,128)(2,1)} %refs_6_.1) | copy-start | bytes 3145732
  6.5 91.2 %all-gather.3.cloned.1.call-start = ((), (), s32[]{:S(2)}) async-start(), calls=%async_computation.4 | async-start | bytes 8257536 | tf_op jit(solution)/shard_map/all_gather | solution.py:457
  8.1 12.1 %collective-permute-start.2 = (bf16[192,768]{1,0:T(8,128)(2,1)S(1)}, bf16[192,768]{1,0:T(8,128)(2,1)S(1)}, u32[]{:S(2)}, u32[]{:S(2)}) collective-permute-start(bf16[192,768]{1,0:T(8,128)(2,1)S(1)} %get-tuple-element.26.refs_2_), channel_id=1, source_target_pairs={{0,32},{32,0},{64,96},{96,64},{128,160},{160,128},{192,224},{224,1... | collective-permute-start | bytes 884744 | tf_op jit(solution)/shard_map/ppermute | solution.py:387
  8.2 12.0 %collective-permute-start.1 = (bf16[192,768]{1,0:T(8,128)(2,1)S(1)}, bf16[192,768]{1,0:T(8,128)(2,1)S(1)}, u32[]{:S(2)}, u32[]{:S(2)}) collective-permute-start(bf16[192,768]{1,0:T(8,128)(2,1)S(1)} %get-tuple-element.26.refs_2_), channel_id=1, source_target_pairs={{0,192},{32,96},{64,0},{96,160},{128,64},{160,224},{192,128},{224,... | collective-permute-start | bytes 884744 | tf_op jit(solution)/shard_map/ppermute | solution.py:387
  11.0 9.2 %collective-permute-start = (bf16[192,768]{1,0:T(8,128)(2,1)S(1)}, bf16[192,768]{1,0:T(8,128)(2,1)S(1)}, u32[]{:S(2)}, u32[]{:S(2)}) collective-permute-start(bf16[192,768]{1,0:T(8,128)(2,1)S(1)} %get-tuple-element.26.refs_2_), channel_id=1, source_target_pairs={{0,64},{32,224},{64,128},{96,32},{128,192},{160,96},{192,0},{224,1... | collective-permute-start | bytes 884744 | tf_op jit(solution)/shard_map/ppermute | solution.py:387
  11.0 8.3 %collective-permute-start.3 = (bf16[64,1792]{1,0:T(8,128)(2,1)S(1)}, bf16[64,1792]{1,0:T(8,128)(2,1)S(1)}, u32[]{:S(2)}, u32[]{:S(2)}) collective-permute-start(bf16[64,1792]{1,0:T(8,128)(2,1)S(1)} %get-tuple-element.28), channel_id=1, source_target_pairs={{0,8},{1,9},{2,10},{3,11},{4,12},{5,13},{6,14},{7,15},{8,16},{9,17... | collective-permute-start | bytes 688136 | tf_op jit(solution)/shard_map/ppermute | solution.py:392
  12.6 7.6 %collective-permute-start.4 = (bf16[64,1792]{1,0:T(8,128)(2,1)S(1)}, bf16[64,1792]{1,0:T(8,128)(2,1)S(1)}, u32[]{:S(2)}, u32[]{:S(2)}) collective-permute-start(bf16[64,1792]{1,0:T(8,128)(2,1)S(1)} %get-tuple-element.30), channel_id=1, source_target_pairs={{0,24},{1,25},{2,26},{3,27},{4,28},{5,29},{6,30},{7,31},{8,0},{9,1... | collective-permute-start | bytes 688136 | tf_op jit(solution)/shard_map/ppermute | solution.py:392
  20.2 10.8 %collective-permute-start.8 = (bf16[192,768]{1,0:T(8,128)(2,1)S(1)}, bf16[192,768]{1,0:T(8,128)(2,1)S(1)}, u32[]{:S(2)}, u32[]{:S(2)}) collective-permute-start(bf16[192,768]{1,0:T(8,128)(2,1)S(1)} %collective-permute-done.1.refs_4_), channel_id=1, source_target_pairs={{0,32},{32,0},{64,96},{96,64},{128,160},{160,128},{192,224},{224,1... | collective-permute-start | bytes 884744 | tf_op jit(solution)/shard_map/ppermute | solution.py:387
  20.3 10.7 %collective-permute-start.7 = (bf16[192,768]{1,0:T(8,128)(2,1)S(1)}, bf16[192,768]{1,0:T(8,128)(2,1)S(1)}, u32[]{:S(2)}, u32[]{:S(2)}) collective-permute-start(bf16[192,768]{1,0:T(8,128)(2,1)S(1)} %collective-permute-done.refs_3_), channel_id=1, source_target_pairs={{0,32},{32,0},{64,96},{96,64},{128,160},{160,128},{192,224},{224,1... | collective-permute-start | bytes 884744 | tf_op jit(solution)/shard_map/ppermute | solution.py:387
  20.8 10.2 %collective-permute-start.6 = (bf16[192,768]{1,0:T(8,128)(2,1)S(1)}, bf16[192,768]{1,0:T(8,128)(2,1)S(1)}, u32[]{:S(2)}, u32[]{:S(2)}) collective-permute-start(bf16[192,768]{1,0:T(8,128)(2,1)S(1)} %collective-permute-done.refs_3_), channel_id=1, source_target_pairs={{0,64},{32,224},{64,128},{96,32},{128,192},{160,96},{192,0},{224,1... | collective-permute-start | bytes 884744 | tf_op jit(solution)/shard_map/ppermute | solution.py:387
  21.1 9.9 %collective-permute-start.5 = (bf16[64,1792]{1,0:T(8,128)(2,1)S(1)}, bf16[64,1792]{1,0:T(8,128)(2,1)S(1)}, u32[]{:S(2)}, u32[]{:S(2)}) collective-permute-start(bf16[64,1792]{1,0:T(8,128)(2,1)S(1)} %get-tuple-element.35), channel_id=1, source_target_pairs={{0,16},{1,17},{2,18},{3,19},{4,20},{5,21},{6,22},{7,23},{8,24},{9,... | collective-permute-start | bytes 688136 | tf_op jit(solution)/shard_map/ppermute | solution.py:392
  32.0 1.7 %collective-permute-start.9 = (bf16[192,768]{1,0:T(8,128)(2,1)S(1)}, bf16[192,768]{1,0:T(8,128)(2,1)S(1)}, u32[]{:S(2)}, u32[]{:S(2)}) collective-permute-start(bf16[192,768]{1,0:T(8,128)(2,1)S(1)} %collective-permute-done.6.refs_5_), channel_id=1, source_target_pairs={{0,32},{32,0},{64,96},{96,64},{128,160},{160,128},{192,224},{224,1... | collective-permute-start | bytes 884744 | tf_op jit(solution)/shard_map/ppermute | solution.py:387
  37.6 23.8 %all-to-all-start = ((bf16[32,8,640]{2,1,0:T(8,128)(2,1)}), bf16[32,8,640]{2,1,0:T(8,128)(2,1)S(1)}, u32[]{:S(2)}, u32[]{:S(2)}) async-start(bf16[32,8,640]{2,1,0:T(8,128)(2,1)} %bitcast.10), calls=%async_computation | async-start | bytes 655360 | tf_op jit(solution)/shard_map/all_to_all | solution.py:462
Sparse Core Ops, SparseCore 0:
  32.1 48.4 all-gather.2

commit v5 on v4

--- a/solution.py
+++ b/solution.py
@@ -8,7 +8,7 @@
 from jax.sharding import PartitionSpec as P
 
 GROUP = 4
-CHUNKS = 8
+CHUNKS = 4
 NOPE = 128
 Y = 4
 Z = 8
@@ -66,6 +66,37 @@
     )(y, *[in_hbm(a) for a in (w_qnope, w_qrope, weights)])
 
 
+def arrange_kernel(place_ref, latent_hbm, uk_hbm, out_ref, uk_ref, held_ref, sem):
+    copies = [
+        pltpu.make_async_copy(latent_hbm, held_ref, sem.at[0]),
+        pltpu.make_async_copy(uk_hbm, uk_ref, sem.at[1]),
+    ]
+    for copy in copies:
+        copy.start()
+    copies[0].wait()
+    parts, _, depth = out_ref.shape
+    for d in range(parts):
+        out_ref[place_ref[d]] = held_ref[:, d * depth : (d + 1) * depth]
+    copies[1].wait()
+
+
+def arrange(place, latent, w_uk):
+    rows, width = latent.shape
+    parts = place.shape[0]
+    return pl.pallas_call(
+        arrange_kernel,
+        out_shape=(
+            jax.ShapeDtypeStruct((parts, rows, width // parts), BF16),
+            jax.ShapeDtypeStruct(w_uk.shape, BF16),
+        ),
+        in_specs=[SCALARS] + [IN_HBM] * 2,
+        out_specs=(WHOLE, WHOLE),
+        scratch_shapes=[pltpu.VMEM(latent.shape, BF16), pltpu.SemaphoreType.DMA((2,))],
+        compiler_params=params(8),
+        name="arrange",
+    )(place, in_hbm(latent), in_hbm(w_uk))
+
+
 def stack_kernel(y_ref, *refs):
     pieces, (out_ref, sem) = refs[:Y], refs[Y:]
     copies = []
@@ -99,24 +130,14 @@
     return hit.astype(F32).astype(BF16)
 
 
-def project_kernel(pieces, place_ref, latent_hbm, *refs):
+def project_kernel(pieces, latent_ref, *refs):
     piece_refs = refs[:pieces]
-    uk_hbm, cos_ref, sin_ref, out_ref, held_ref, sorted_ref, uk_ref, sem = refs[pieces:]
+    uk_ref, cos_ref, sin_ref, out_ref = refs[pieces:]
     heads, nope_dim, width = uk_ref.shape
-    rows = latent_hbm.shape[0]
-    copies = [
-        pltpu.make_async_copy(latent_hbm, held_ref, sem.at[0]),
-        pltpu.make_async_copy(uk_hbm, uk_ref, sem.at[1]),
-    ]
-    for copy in copies:
-        copy.start()
-    copies[0].wait()
-    depth = sorted_ref.shape[2]
-    for d in range(pieces):
-        sorted_ref[place_ref[d]] = held_ref[:, d * depth : (d + 1) * depth]
+    rows = latent_ref.shape[1]
     both = None
     for i in range(pieces):
-        term = dot(sorted_ref[i], piece_refs[i][...])
+        term = dot(latent_ref[i], piece_refs[i][...])
         both = term if both is None else both + term
     query = both[:, : heads * nope_dim].astype(BF16)
     turned = both[:, heads * nope_dim :]
@@ -133,7 +154,6 @@
     sin = jnp.concatenate([-sin_ref[...], sin_ref[...]] * heads, axis=1)
     rotated = (turned * cos + swapped * sin).astype(BF16)
     blank = jnp.zeros((rows, out_ref.shape[1] - width - rope_dim), BF16)
-    copies[1].wait()
     total = None
     for j in range(heads):
         part = dot(query[:, j * nope_dim : (j + 1) * nope_dim], uk_ref[j]).astype(BF16)
@@ -146,9 +166,9 @@
     out_ref[...] = total.astype(BF16)
 
 
-def project(place, latent, pieces, w_uk, cos, sin):
+def project(latent, pieces, w_uk, cos, sin):
     heads, _, width = w_uk.shape
-    rows = latent.shape[0]
+    rows = latent.shape[1]
     count = len(pieces)
     full = width + 128 * pl.cdiv(2 * cos.shape[1], 128)
 
@@ -158,17 +178,11 @@
     return pl.pallas_call(
         kernel,
         out_shape=jax.ShapeDtypeStruct((rows * heads, full), BF16),
-        in_specs=[SCALARS, IN_HBM] + [WHOLE] * count + [IN_HBM] + [WHOLE] * 2,
+        in_specs=[WHOLE] * (4 + count),
         out_specs=WHOLE,
-        scratch_shapes=[
-            pltpu.VMEM(latent.shape, BF16),
-            pltpu.VMEM((count, rows, latent.shape[1] // count), BF16),
-            pltpu.VMEM(w_uk.shape, BF16),
-            pltpu.SemaphoreType.DMA((2,)),
-        ],
         compiler_params=params(16),
         name="project",
-    )(place, in_hbm(latent), *pieces, in_hbm(w_uk), cos, sin)
+    )(latent, *pieces, w_uk, cos, sin)
 
 
 def attend_kernel(
@@ -398,9 +412,8 @@
     chip, core = me // 2, me % 2
     sign = 1 - 2 * core
     other = lax.rem(core + 1, 2)
-    steps = [0, -1, 1, 2]
-    origins = [lax.rem(chip + sign * step + chips, chips) * 2 + core for step in steps]
-    origins += [lax.rem(chip - sign * step + 2 * chips, chips) * 2 + other for step in steps]
+    origins = [lax.rem(chip + sign * step + chips, chips) * 2 + core for step in (0, -1, 1, 2)]
+    origins += [lax.rem(chip - sign * step + 2 * chips, chips) * 2 + other for step in (0, -1, 1, 2)]
     origins = jnp.stack(origins)
     parts = jnp.arange(2 * chips)
     return jnp.sum(
@@ -444,20 +457,22 @@
     flat = w_out.reshape(depth, width_all)
     both, *cuts = prepare(y_scalar, w_qnope, w_qrope, flat)
     ahead, behind, beside = shift_dp(both, 1, 0), shift_dp(both, -1, 0), shift_dp(both, 0, 1)
-    cuts[1], cuts[3] = shift_y(cuts[1], 1), shift_y(cuts[3], 3)
-    ahead, behind, beside, cuts, cos, sin = lax.optimization_barrier(
-        (ahead, behind, beside, cuts, cos, sin)
+    cuts[2] = shift_y(cuts[2], 2)
+    latent, uk = arrange(piece_places(), q_latent, w_uk)
+    ahead, behind, beside, cuts, cos, sin, latent, uk = lax.optimization_barrier(
+        (ahead, behind, beside, cuts, cos, sin, latent, uk)
     )
     far = shift_dp(ahead, 1, 0)
     ahead_beside, behind_beside = shift_dp(ahead, 0, 1), shift_dp(behind, 0, 1)
-    cuts[2] = shift_y(cuts[2], 2)
-    cuts, far, ahead_beside, behind_beside = lax.optimization_barrier(
-        (cuts, far, ahead_beside, behind_beside)
+    cuts[1], cuts[3] = shift_y(cuts[1], 1), shift_y(cuts[3], 3)
+    far, cuts, ahead_beside, behind_beside = lax.optimization_barrier(
+        (far, cuts, ahead_beside, behind_beside)
     )
+    pieces = [both, ahead, behind, far, beside]
+    pieces += [ahead_beside, behind_beside, shift_dp(far, 0, 1)]
+    cuts, pieces = lax.optimization_barrier((cuts, pieces))
     panel = lax.all_gather(stack(y_scalar, cuts), "dp", axis=0)
-    pieces = [both, ahead, behind, far]
-    pieces += [beside, ahead_beside, behind_beside, shift_dp(far, 0, 1)]
-    query = project(piece_places(), q_latent, pieces, w_uk, cos, sin)
+    query = project(latent, pieces, uk, cos, sin)
     query = query.reshape(sources, own * heads, query.shape[1])
     query = lax.all_to_all(query, "head", 0, 0, tiled=True).reshape(rows * heads, -1)
     own_lengths = lax.dynamic_slice_in_dim(lengths, head * own, own)

time: 123 us -> 128 us (1.041)
  local copies, waits for them, and re-layouts: 0.2 us -> 8.5 us
  starting transfers between devices: 21 us -> 19.6 us
  waiting for transfers between devices: 26.2 us -> 24.9 us
    unnamed x10 -> x34, local copies, waits for them, and re-layouts: 0.02 us -> 8.32 us
    pallas_call x1, Pallas kernels: 3.91 us -> 2.15 us  [project(): pl.pallas_call(kernel, out_shape=jax.ShapeDtypeStruct((rows * heads, full...]
    pallas_call x0 -> x1, Pallas kernels: none -> 1.7 us  [arrange(): pl.pallas_call(arrange_kernel, out_shape=(jax.ShapeDtypeStruct((parts, ro...]
  transfers between devices with their start and end apart: 12 -> 12, of which waited for: 5 -> 5; matrix products, arithmetic and copies ran while one was open for 1% -> 1% of each run, Pallas kernels for 12% -> 11%
where the time goes in v5:
time: 128 us
  blocking collectives  39.4 us (31%)
  waiting for transfers between devices  24.9 us (19%)
  Pallas kernels  20.8 us (16%)
  starting transfers between devices  19.6 us (15%)
  between operations  13.6 us (11%)
  local copies, waits for them, and re-layouts  8.5 us (7%)
    all_to_all x1, blocking collectives, body(): lax.all_to_all(attn, 'head', 0, 0, tiled=True).reshape(rows * heads, -1)  16.7 us
    all_to_all x1, blocking collectives, body(): lax.all_to_all(term, 'head', 0, 0, tiled=True, axis_index_groups=Z_GROUPS)  13.5 us
    all_to_all x1, waiting for transfers between devices, body(): lax.all_to_all(query, 'head', 0, 0, tiled=True).reshape(rows * heads, -1)  12.4 us
    ppermute x3, waiting for transfers between devices, shift_y(): return lax.ppermute(x, 'head', pairs)  11.6 us
    all_to_all x1, starting transfers between devices, body(): lax.all_to_all(query, 'head', 0, 0, tiled=True).reshape(rows * heads, -1)  11.5 us
    all_to_all x1, blocking collectives, body(): lax.all_to_all(values, 'head', 0, 0, tiled=True, axis_index_groups=Y_GROUPS)  9.18 us
    pallas_call x1, Pallas kernels, attend(): pl.pallas_call(kernel, out_shape=jax.ShapeDtypeStruct((rows, width), BF16...  8.78 us
    unnamed x34, local copies, waits for them, and re-layouts  8.32 us
  transfers between devices with their start and end apart: 12, of which 5 were waited for; matrix products, arithmetic and copies ran while one was open for 1% of the time, Pallas kernels for 11%

profile of v5, /device:TPU:8, one launch (start us, length us, event | category | flops | bytes accessed | tf_op | source)
XLA Modules:
  0.0 127.8 jit_solution(12709037546968433588)
XLA Ops:
  6.6 1.5 %prepare.1 = (bf16[192,768]{1,0:T(8,128)(2,1)S(1)}, bf16[64,1792]{1,0:T(8,128)(2,1)S(1)}, bf16[64,1792]{1,0:T(8,128)(2,1)S(1)}, bf16[64,1792]{1,0:T(8,128)(2,1)S(1)}, bf16[64,1792]{1,0:T(8,128)(2,1)S(1)}) custom-call(s32[1]{0:T(128)} %bitcast.y_ref, bf16[192,512]{1,0:T(8,128)(2,1)} %nope_hbm.1, bf16[192,256]{1,0:T(8,128)(2,1)} %rope_hbm.1, ...), custom_call_target="tpu_custom_call" | custom-call | tf_op jit(solution)/shard_map/prepare/pallas_call | solution.py:57
  8.1 0.7 copy-done.7
  8.8 2.8 %collective-permute-start.1 = (bf16[192,768]{1,0:T(8,128)(2,1)S(1)}, bf16[192,768]{1,0:T(8,128)(2,1)S(1)}, u32[]{:S(2)}, u32[]{:S(2)}) collective-permute-start(bf16[192,768]{1,0:T(8,128)(2,1)S(1)} %get-tuple-element.64.refs_1_), channel_id=1, source_target_pairs={{0,192},{32,96},{64,0},{96,160},{128,64},{160,224},{192,128},{224,... | collective-permute-start | bytes 884744 | tf_op jit(solution)/shard_map/ppermute | solution.py:401
  11.6 2.4 %collective-permute-start.3 = (bf16[64,1792]{1,0:T(8,128)(2,1)S(1)}, bf16[64,1792]{1,0:T(8,128)(2,1)S(1)}, u32[]{:S(2)}, u32[]{:S(2)}) collective-permute-start(bf16[64,1792]{1,0:T(8,128)(2,1)S(1)} %get-tuple-element.45), channel_id=1, source_target_pairs={{0,16},{1,17},{2,18},{3,19},{4,20},{5,21},{6,22},{7,23},{8,24},{9,... | collective-permute-start | bytes 688136 | tf_op jit(solution)/shard_map/ppermute | solution.py:406
  14.2 0.7 convert_element_type.3
  14.8 1.7 %arrange.1 = (bf16[8,64,192]{2,1,0:T(8,128)(2,1)S(1)}, bf16[4,128,512]{2,1,0:T(8,128)(2,1)S(1)}) custom-call(s32[8]{0:T(128)S(1)} %select_reduce_fusion.place_ref, bf16[64,1536]{1,0:T(8,128)(2,1)} %latent_hbm.1, bf16[4,128,512]{2,1,0:T(8,128)(2,1)} %uk_hbm.1), custom_call_target="tpu_custom_call" | custom-call | tf_op jit(solution)/shard_map/arrange/pallas_call | solution.py:86
  16.5 0.7 copy-done.5
  17.5 3.5 %collective-permute-done.3.refs_2_ = bf16[64,1792]{1,0:T(8,128)(2,1)S(1)} collective-permute-done((bf16[64,1792]{1,0:T(8,128)(2,1)S(1)}, bf16[64,1792]{1,0:T(8,128)(2,1)S(1)}, u32[]{:S(2)}, u32[]{:S(2)}) %collective-permute-start.3) | collective-permute-done | bytes 229408 | tf_op jit(solution)/shard_map/ppermute | solution.py:406
  21.0 0.7 copy-done.9
  21.8 0.5 collective-permute-start.7
  22.6 1.6 %collective-permute-start.5 = (bf16[64,1792]{1,0:T(8,128)(2,1)}, bf16[64,1792]{1,0:T(8,128)(2,1)S(1)}, u32[]{:S(2)}, u32[]{:S(2)}) collective-permute-start(bf16[64,1792]{1,0:T(8,128)(2,1)} %copy-done.15), channel_id=1, source_target_pairs={{0,8},{1,9},{2,10},{3,11},{4,12},{5,13},{6,14},{7,15},{8,16},{9,17... | collective-permute-start | bytes 688136 | tf_op jit(solution)/shard_map/ppermute | solution.py:406
  24.6 6.5 %collective-permute-done.5.refs_1_ = bf16[64,1792]{1,0:T(8,128)(2,1)S(1)} collective-permute-done((bf16[64,1792]{1,0:T(8,128)(2,1)}, bf16[64,1792]{1,0:T(8,128)(2,1)S(1)}, u32[]{:S(2)}, u32[]{:S(2)}) %collective-permute-start.5) | collective-permute-done | bytes 229408 | tf_op jit(solution)/shard_map/ppermute | solution.py:406
  31.2 1.5 %collective-permute-done.6.refs_3_ = bf16[64,1792]{1,0:T(8,128)(2,1)S(1)} collective-permute-done((bf16[64,1792]{1,0:T(8,128)(2,1)}, bf16[64,1792]{1,0:T(8,128)(2,1)S(1)}, u32[]{:S(2)}, u32[]{:S(2)}) %collective-permute-start.6) | collective-permute-done | bytes 229408 | tf_op jit(solution)/shard_map/ppermute | solution.py:406
  32.8 0.7 copy-done.1
  33.5 0.8 collective-permute-done.9.refs_8_
  34.4 0.7 copy-done.3
  35.1 0.9 copy-done.8
  36.1 0.9 copy-done.10
  37.0 1.0 stack.37
  38.1 1.0 copy-done.2
  39.0 1.0 copy-done.4
  40.0 0.9 copy-done.6
  40.9 2.1 %project.1 = bf16[256,640]{1,0:T(8,128)(2,1)} custom-call(bf16[8,64,192]{2,1,0:T(8,128)(2,1)S(1)} %copy-done.6, bf16[192,768]{1,0:T(8,128)(2,1)S(1)} %get-tuple-element.64.refs_1_, bf16[192,768]{1,0:T(8,128)(2,1)S(1)} %collective-permute-done.refs_2_, bf16[192,768]{1,0:T(8,128)(2,1)S(1)} %collective-permute-done.1.refs_3_, bf16[192,768]{1,0:T(8,128)(2,1)S(1)} %copy-done.2, ...), custom_call_target="tpu_custom_call" | custom-call | tf_op jit(solution)/shard_map/project/pallas_call | solution.py:178
  43.1 11.5 %all-to-all-start = ((bf16[32,8,640]{2,1,0:T(8,128)(2,1)}), bf16[32,8,640]{2,1,0:T(8,128)(2,1)S(1)}, u32[]{:S(2)}, u32[]{:S(2)}) async-start(bf16[32,8,640]{2,1,0:T(8,128)(2,1)} %bitcast.10), calls=%async_computation | async-start | bytes 655360 | tf_op jit(solution)/shard_map/all_to_all | solution.py:477
  54.6 12.4 %all-to-all-done = bf16[32,8,640]{2,1,0:T(8,128)(2,1)S(1)} async-done(((bf16[32,8,640]{2,1,0:T(8,128)(2,1)}), bf16[32,8,640]{2,1,0:T(8,128)(2,1)S(1)}, u32[]{:S(2)}, u32[]{:S(2)}) %all-to-all-start) | async-done | bytes 327712 | tf_op jit(solution)/shard_map/all_to_all | solution.py:477
  67.0 8.8 %attend.1 = bf16[256,512]{1,0:T(8,128)(2,1)S(1)} custom-call(s32[2]{0:T(128)S(1)} %dynamic_slice.3.refs_0_, s32[2,32]{1,0:T(2,128)S(1)} %copy-done.12, bf16[256,640]{1,0:T(8,128)(2,1)S(1)} %bitcast.15, bf16[2,512]{1,0:T(2,128)(2,1)S(1)} %copy-done.11, bf16[2,64]{1,0:T(2,128)(2,1)S(1)} %copy-done.13, bf16[64,128,512]{2,1,0:T(8,128)(2,1)} %refs_5_.1, ...), custom_call_target="tpu_custom_call" | custom-call | tf_op jit(solution)/shard_map/attend/pallas_call | solution.py:277
  75.8 16.7 %all_to_all.20 = bf16[32,8,512]{2,1,0:T(8,128)(2,1)S(1)} all-to-all(bf16[32,8,512]{2,1,0:T(8,128)(2,1)S(1)} %bitcast.16), channel_id=1, replica_groups=mesh['dp'=8,'head'=32] {'head'}, dimensions={0} | all-to-all | bytes 524288 | tf_op jit(solution)/shard_map/all_to_all | solution.py:483
  92.5 1.4 %values.1 = bf16[64,512]{1,0:T(8,128)(2,1)S(1)} custom-call(bf16[256,512]{1,0:T(8,128)(2,1)S(1)} %bitcast.17, bf16[4,512,128]{2,1,0:T(8,128)(2,1)} %refs_1_.3), custom_call_target="tpu_custom_call" | custom-call | tf_op jit(solution)/shard_map/values/pallas_call | solution.py:326
  94.0 9.2 %all_to_all.21.values_ref = bf16[4,64,512]{2,1,0:T(8,128)(2,1)S(1)} all-to-all(bf16[4,64,512]{2,1,0:T(8,128)(2,1)S(1)} %broadcast_in_dim.16), channel_id=1, replica_groups={{0,8,16,24},{1,9,17,25},{2,10,18,26},{3,11,19,27},{4,12,20,28},{5,13,21..., dimensions={0} | all-to-all | bytes 524288 | tf_op jit(solution)/shard_map/all_to_all | solution.py:486
  103.2 3.6 %mix.1 = bf16[8,64,224]{2,1,0:T(8,128)(2,1)S(1)} custom-call(bf16[4,64,512]{2,1,0:T(8,128)(2,1)S(1)} %all_to_all.21.values_ref, bf16[8,4,64,1792]{3,2,1,0:T(8,128)(2,1)} %bitcast.18), custom_call_target="tpu_custom_call" | custom-call | tf_op jit(solution)/shard_map/mix/pallas_call | solution.py:362
  106.8 13.5 %all_to_all.22.terms_ref = bf16[8,64,224]{2,1,0:T(8,128)(2,1)S(1)} all-to-all(bf16[8,64,224]{2,1,0:T(8,128)(2,1)S(1)} %mix.1), channel_id=1, replica_groups={{0,1,2,3,4,5,6,7},{8,9,10,11,12,13,14,15},{16,17,18,19,20,21,22,23},{24..., dimensions={0} | all-to-all | bytes 458752 | tf_op jit(solution)/shard_map/all_to_all | solution.py:488
  120.3 0.7 finish.1
  (45 shorter events, 1.5 us)
Async XLA Ops:
  6.5 48.0 %copy-start.16 = (s32[64]{0:T(128)S(1)}, s32[64]{0:T(128)}, u32[]{:S(2)}) copy-start(s32[64]{0:T(128)} %param.22) | copy-start | bytes 772
  6.5 60.5 %copy-start.12 = (s32[2,32]{1,0:T(2,128)S(1)}, s32[2,32]{1,0:T(2,128)}, u32[]{:S(2)}) copy-start(s32[2,32]{1,0:T(2,128)} %refs_1_.2) | copy-start | bytes 772
  6.5 60.5 %copy-start.13 = (bf16[2,64]{1,0:T(2,128)(2,1)S(1)}, bf16[2,64]{1,0:T(2,128)(2,1)}, u32[]{:S(2)}) copy-start(bf16[2,64]{1,0:T(2,128)(2,1)} %refs_4_.1) | copy-start | bytes 772
  6.5 60.5 %copy-start.11 = (bf16[2,512]{1,0:T(2,128)(2,1)S(1)}, bf16[2,512]{1,0:T(2,128)(2,1)}, u32[]{:S(2)}) copy-start(bf16[2,512]{1,0:T(2,128)(2,1)} %refs_3_.1) | copy-start | bytes 6148
  6.5 60.5 %copy-start = (bf16[64,64,128]{2,1,0:T(8,128)(2,1)S(1)}, bf16[64,64,128]{2,1,0:T(8,128)(2,1)}, u32[]{:S(2)}) copy-start(bf16[64,64,128]{2,1,0:T(8,128)(2,1)} %refs_6_.1) | copy-start | bytes 3145732
  6.5 96.6 %all-gather.3.cloned.1.call-start = ((), (), s32[]{:S(2)}) async-start(), calls=%async_computation.4 | async-start | bytes 8257536 | tf_op jit(solution)/shard_map/all_gather | solution.py:474
  8.1 0.7 copy-start.7
  8.8 2.8 %copy-start.14 = (bf16[64,1792]{1,0:T(8,128)(2,1)}, bf16[64,1792]{1,0:T(8,128)(2,1)S(1)}, u32[]{:S(2)}) copy-start(bf16[64,1792]{1,0:T(8,128)(2,1)S(1)} %get-tuple-element.54) | copy-start | bytes 688132
  8.8 2.8 %copy-start.15 = (bf16[64,1792]{1,0:T(8,128)(2,1)}, bf16[64,1792]{1,0:T(8,128)(2,1)S(1)}, u32[]{:S(2)}) copy-start(bf16[64,1792]{1,0:T(8,128)(2,1)S(1)} %get-tuple-element.52) | copy-start | bytes 688132
  8.8 12.9 %collective-permute-start.2 = (bf16[192,768]{1,0:T(8,128)(2,1)S(1)}, bf16[192,768]{1,0:T(8,128)(2,1)S(1)}, u32[]{:S(2)}, u32[]{:S(2)}) collective-permute-start(bf16[192,768]{1,0:T(8,128)(2,1)S(1)} %get-tuple-element.64.refs_1_), channel_id=1, source_target_pairs={{0,32},{32,0},{64,96},{96,64},{128,160},{160,128},{192,224},{224,1... | collective-permute-start | bytes 884744 | tf_op jit(solution)/shard_map/ppermute | solution.py:401
  8.8 12.9 %collective-permute-start.1 = (bf16[192,768]{1,0:T(8,128)(2,1)S(1)}, bf16[192,768]{1,0:T(8,128)(2,1)S(1)}, u32[]{:S(2)}, u32[]{:S(2)}) collective-permute-start(bf16[192,768]{1,0:T(8,128)(2,1)S(1)} %get-tuple-element.64.refs_1_), channel_id=1, source_target_pairs={{0,192},{32,96},{64,0},{96,160},{128,64},{160,224},{192,128},{224,... | collective-permute-start | bytes 884744 | tf_op jit(solution)/shard_map/ppermute | solution.py:401
  11.5 10.2 %collective-permute-start = (bf16[192,768]{1,0:T(8,128)(2,1)S(1)}, bf16[192,768]{1,0:T(8,128)(2,1)S(1)}, u32[]{:S(2)}, u32[]{:S(2)}) collective-permute-start(bf16[192,768]{1,0:T(8,128)(2,1)S(1)} %get-tuple-element.64.refs_1_), channel_id=1, source_target_pairs={{0,64},{32,224},{64,128},{96,32},{128,192},{160,96},{192,0},{224,1... | collective-permute-start | bytes 884744 | tf_op jit(solution)/shard_map/ppermute | solution.py:401
  11.6 9.4 %collective-permute-start.3 = (bf16[64,1792]{1,0:T(8,128)(2,1)S(1)}, bf16[64,1792]{1,0:T(8,128)(2,1)S(1)}, u32[]{:S(2)}, u32[]{:S(2)}) collective-permute-start(bf16[64,1792]{1,0:T(8,128)(2,1)S(1)} %get-tuple-element.45), channel_id=1, source_target_pairs={{0,16},{1,17},{2,18},{3,19},{4,20},{5,21},{6,22},{7,23},{8,24},{9,... | collective-permute-start | bytes 688136 | tf_op jit(solution)/shard_map/ppermute | solution.py:406
  16.5 0.7 copy-start.5
  21.0 0.7 copy-start.9
  21.7 11.0 %collective-permute-start.8 = (bf16[192,768]{1,0:T(8,128)(2,1)S(1)}, bf16[192,768]{1,0:T(8,128)(2,1)S(1)}, u32[]{:S(2)}, u32[]{:S(2)}) collective-permute-start(bf16[192,768]{1,0:T(8,128)(2,1)S(1)} %collective-permute-done.1.refs_3_), channel_id=1, source_target_pairs={{0,32},{32,0},{64,96},{96,64},{128,160},{160,128},{192,224},{224,1... | collective-permute-start | bytes 884744 | tf_op jit(solution)/shard_map/ppermute | solution.py:401
  21.8 10.9 %collective-permute-start.7 = (bf16[192,768]{1,0:T(8,128)(2,1)S(1)}, bf16[192,768]{1,0:T(8,128)(2,1)S(1)}, u32[]{:S(2)}, u32[]{:S(2)}) collective-permute-start(bf16[192,768]{1,0:T(8,128)(2,1)S(1)} %collective-permute-done.refs_2_), channel_id=1, source_target_pairs={{0,32},{32,0},{64,96},{96,64},{128,160},{160,128},{192,224},{224,1... | collective-permute-start | bytes 884744 | tf_op jit(solution)/shard_map/ppermute | solution.py:401
  22.3 10.4 %collective-permute-start.4 = (bf16[192,768]{1,0:T(8,128)(2,1)S(1)}, bf16[192,768]{1,0:T(8,128)(2,1)S(1)}, u32[]{:S(2)}, u32[]{:S(2)}) collective-permute-start(bf16[192,768]{1,0:T(8,128)(2,1)S(1)} %collective-permute-done.refs_2_), channel_id=1, source_target_pairs={{0,64},{32,224},{64,128},{96,32},{128,192},{160,96},{192,0},{224,1... | collective-permute-start | bytes 884744 | tf_op jit(solution)/shard_map/ppermute | solution.py:401
  22.6 8.6 %collective-permute-start.5 = (bf16[64,1792]{1,0:T(8,128)(2,1)}, bf16[64,1792]{1,0:T(8,128)(2,1)S(1)}, u32[]{:S(2)}, u32[]{:S(2)}) collective-permute-start(bf16[64,1792]{1,0:T(8,128)(2,1)} %copy-done.15), channel_id=1, source_target_pairs={{0,8},{1,9},{2,10},{3,11},{4,12},{5,13},{6,14},{7,15},{8,16},{9,17... | collective-permute-start | bytes 688136 | tf_op jit(solution)/shard_map/ppermute | solution.py:406
  24.2 8.5 %collective-permute-start.6 = (bf16[64,1792]{1,0:T(8,128)(2,1)}, bf16[64,1792]{1,0:T(8,128)(2,1)S(1)}, u32[]{:S(2)}, u32[]{:S(2)}) collective-permute-start(bf16[64,1792]{1,0:T(8,128)(2,1)} %copy-done.14), channel_id=1, source_target_pairs={{0,24},{1,25},{2,26},{3,27},{4,28},{5,29},{6,30},{7,31},{8,0},{9,1... | collective-permute-start | bytes 688136 | tf_op jit(solution)/shard_map/ppermute | solution.py:406
  32.7 1.7 %collective-permute-start.9 = (bf16[192,768]{1,0:T(8,128)(2,1)S(1)}, bf16[192,768]{1,0:T(8,128)(2,1)S(1)}, u32[]{:S(2)}, u32[]{:S(2)}) collective-permute-start(bf16[192,768]{1,0:T(8,128)(2,1)S(1)} %collective-permute-done.4.refs_4_), channel_id=1, source_target_pairs={{0,32},{32,0},{64,96},{96,64},{128,160},{160,128},{192,224},{224,1... | collective-permute-start | bytes 884744 | tf_op jit(solution)/shard_map/ppermute | solution.py:401
  32.8 0.7 copy-start.1
  34.4 0.7 copy-start.3
  35.1 0.9 copy-start.8
  36.1 0.9 copy-start.10
  38.1 1.0 copy-start.2
  39.0 1.0 copy-start.4
  40.0 0.9 copy-start.6
  43.1 23.9 %all-to-all-start = ((bf16[32,8,640]{2,1,0:T(8,128)(2,1)}), bf16[32,8,640]{2,1,0:T(8,128)(2,1)S(1)}, u32[]{:S(2)}, u32[]{:S(2)}) async-start(bf16[32,8,640]{2,1,0:T(8,128)(2,1)} %bitcast.10), calls=%async_computation | async-start | bytes 655360 | tf_op jit(solution)/shard_map/all_to_all | solution.py:477
Sparse Core Ops, SparseCore 0:
  38.2 48.2 all-gather.2

commit v6 on v5

--- a/solution.py
+++ b/solution.py
@@ -53,48 +53,40 @@
 
 def prepare(y, w_qnope, w_qrope, weights):
     depth = w_qnope.shape[0]
-    cut = jax.ShapeDtypeStruct((weights.shape[0], weights.shape[1] // Y), BF16)
+    cut = pltpu.HBM((weights.shape[0], weights.shape[1] // Y), BF16)
     return pl.pallas_call(
         prepare_kernel,
         out_shape=(jax.ShapeDtypeStruct((depth, w_qnope.shape[1] + w_qrope.shape[1]), BF16),)
         + (cut,) * Y,
         in_specs=[SCALARS] + [IN_HBM] * 3,
-        out_specs=(WHOLE,) * (1 + Y),
+        out_specs=(WHOLE,) + (IN_HBM,) * Y,
         scratch_shapes=[pltpu.SemaphoreType.DMA((2 + Y,))],
         compiler_params=params(8),
         name="prepare",
     )(y, *[in_hbm(a) for a in (w_qnope, w_qrope, weights)])
 
 
-def arrange_kernel(place_ref, latent_hbm, uk_hbm, out_ref, uk_ref, held_ref, sem):
-    copies = [
-        pltpu.make_async_copy(latent_hbm, held_ref, sem.at[0]),
-        pltpu.make_async_copy(uk_hbm, uk_ref, sem.at[1]),
-    ]
-    for copy in copies:
-        copy.start()
-    copies[0].wait()
+def arrange_kernel(place_ref, latent_hbm, out_ref, held_ref, sem):
+    copy = pltpu.make_async_copy(latent_hbm, held_ref, sem)
+    copy.start()
+    copy.wait()
     parts, _, depth = out_ref.shape
     for d in range(parts):
         out_ref[place_ref[d]] = held_ref[:, d * depth : (d + 1) * depth]
-    copies[1].wait()
-
-
-def arrange(place, latent, w_uk):
+
+
+def arrange(place, latent):
     rows, width = latent.shape
     parts = place.shape[0]
     return pl.pallas_call(
         arrange_kernel,
-        out_shape=(
-            jax.ShapeDtypeStruct((parts, rows, width // parts), BF16),
-            jax.ShapeDtypeStruct(w_uk.shape, BF16),
-        ),
-        in_specs=[SCALARS] + [IN_HBM] * 2,
-        out_specs=(WHOLE, WHOLE),
-        scratch_shapes=[pltpu.VMEM(latent.shape, BF16), pltpu.SemaphoreType.DMA((2,))],
+        out_shape=jax.ShapeDtypeStruct((parts, rows, width // parts), BF16),
+        in_specs=[SCALARS, IN_HBM],
+        out_specs=WHOLE,
+        scratch_shapes=[pltpu.VMEM(latent.shape, BF16), pltpu.SemaphoreType.DMA(())],
         compiler_params=params(8),
         name="arrange",
-    )(place, in_hbm(latent), in_hbm(w_uk))
+    )(place, in_hbm(latent))
 
 
 def stack_kernel(y_ref, *refs):
@@ -113,12 +105,12 @@
     return pl.pallas_call(
         stack_kernel,
         out_shape=jax.ShapeDtypeStruct((Y,) + pieces[0].shape, BF16),
-        in_specs=[SCALARS] + [pl.BlockSpec(memory_space=pl.ANY)] * Y,
+        in_specs=[SCALARS] + [IN_HBM] * Y,
         out_specs=IN_HBM,
         scratch_shapes=[pltpu.SemaphoreType.DMA((Y,))],
         compiler_params=params(8),
         name="stack",
-    )(y, *pieces)
+    )(y, *[in_hbm(piece) for piece in pieces])
 
 
 def one_hot(rows, columns, place, keep=None):
@@ -132,9 +124,11 @@
 
 def project_kernel(pieces, latent_ref, *refs):
     piece_refs = refs[:pieces]
-    uk_ref, cos_ref, sin_ref, out_ref = refs[pieces:]
+    uk_hbm, cos_ref, sin_ref, out_ref, uk_ref, sem = refs[pieces:]
     heads, nope_dim, width = uk_ref.shape
     rows = latent_ref.shape[1]
+    copy = pltpu.make_async_copy(uk_hbm, uk_ref, sem)
+    copy.start()
     both = None
     for i in range(pieces):
         term = dot(latent_ref[i], piece_refs[i][...])
@@ -154,6 +148,7 @@
     sin = jnp.concatenate([-sin_ref[...], sin_ref[...]] * heads, axis=1)
     rotated = (turned * cos + swapped * sin).astype(BF16)
     blank = jnp.zeros((rows, out_ref.shape[1] - width - rope_dim), BF16)
+    copy.wait()
     total = None
     for j in range(heads):
         part = dot(query[:, j * nope_dim : (j + 1) * nope_dim], uk_ref[j]).astype(BF16)
@@ -178,11 +173,12 @@
     return pl.pallas_call(
         kernel,
         out_shape=jax.ShapeDtypeStruct((rows * heads, full), BF16),
-        in_specs=[WHOLE] * (4 + count),
+        in_specs=[WHOLE] * (1 + count) + [IN_HBM] + [WHOLE] * 2,
         out_specs=WHOLE,
+        scratch_shapes=[pltpu.VMEM(w_uk.shape, BF16), pltpu.SemaphoreType.DMA(())],
         compiler_params=params(16),
         name="project",
-    )(latent, *pieces, w_uk, cos, sin)
+    )(latent, *pieces, in_hbm(w_uk), cos, sin)
 
 
 def attend_kernel(
@@ -457,14 +453,14 @@
     flat = w_out.reshape(depth, width_all)
     both, *cuts = prepare(y_scalar, w_qnope, w_qrope, flat)
     ahead, behind, beside = shift_dp(both, 1, 0), shift_dp(both, -1, 0), shift_dp(both, 0, 1)
-    cuts[2] = shift_y(cuts[2], 2)
-    latent, uk = arrange(piece_places(), q_latent, w_uk)
-    ahead, behind, beside, cuts, cos, sin, latent, uk = lax.optimization_barrier(
-        (ahead, behind, beside, cuts, cos, sin, latent, uk)
+    cuts[2], cuts[1] = shift_y(cuts[2], 2), shift_y(cuts[1], 1)
+    latent = arrange(piece_places(), q_latent)
+    ahead, behind, beside, cuts, cos, sin, latent = lax.optimization_barrier(
+        (ahead, behind, beside, cuts, cos, sin, latent)
     )
     far = shift_dp(ahead, 1, 0)
     ahead_beside, behind_beside = shift_dp(ahead, 0, 1), shift_dp(behind, 0, 1)
-    cuts[1], cuts[3] = shift_y(cuts[1], 1), shift_y(cuts[3], 3)
+    cuts[3] = shift_y(cuts[3], 3)
     far, cuts, ahead_beside, behind_beside = lax.optimization_barrier(
         (far, cuts, ahead_beside, behind_beside)
     )
@@ -472,7 +468,7 @@
     pieces += [ahead_beside, behind_beside, shift_dp(far, 0, 1)]
     cuts, pieces = lax.optimization_barrier((cuts, pieces))
     panel = lax.all_gather(stack(y_scalar, cuts), "dp", axis=0)
-    query = project(latent, pieces, uk, cos, sin)
+    query = project(latent, pieces, w_uk, cos, sin)
     query = query.reshape(sources, own * heads, query.shape[1])
     query = lax.all_to_all(query, "head", 0, 0, tiled=True).reshape(rows * heads, -1)
     own_lengths = lax.dynamic_slice_in_dim(lengths, head * own, own)

time: 128 us -> 183 us (1.43)
  Pallas kernels: 20.8 us -> 77 us
  local copies, waits for them, and re-layouts: 8.5 us -> 2.54 us
  starting transfers between devices: 19.6 us -> 23.9 us
    pallas_call x1, Pallas kernels: 1.03 us -> 28.9 us  [stack(): pl.pallas_call(stack_kernel, out_shape=jax.ShapeDtypeStruct((Y,) + pieces...]
    pallas_call x1, Pallas kernels: 1.48 us -> 29 us  [prepare(): pl.pallas_call(prepare_kernel, out_shape=(jax.ShapeDtypeStruct((depth, w_...]
    unnamed x34 -> x20, local copies, waits for them, and re-layouts: 8.32 us -> 2.36 us
    ppermute x3, starting transfers between devices: 4.41 us -> 8.64 us  [shift_y(): return lax.ppermute(x, 'head', pairs)]
  transfers between devices with their start and end apart: 12 -> 12, of which waited for: 5 -> 5; matrix products, arithmetic and copies ran while one was open for 1% -> 1% of each run, Pallas kernels for 11% -> 8%
where the time goes in v6:
time: 183 us; the launch traced here: 182 us
  Pallas kernels  77 us (42%)
  blocking collectives  39.4 us (22%)
  waiting for transfers between devices  24.9 us (14%)
  starting transfers between devices  23.9 us (13%)
  between operations  13.6 us (7%)
  local copies, waits for them, and re-layouts  2.54 us (1%)
    pallas_call x1, Pallas kernels, prepare(): pl.pallas_call(prepare_kernel, out_shape=(jax.ShapeDtypeStruct((depth, w_...  29 us
    pallas_call x1, Pallas kernels, stack(): pl.pallas_call(stack_kernel, out_shape=jax.ShapeDtypeStruct((Y,) + pieces...  28.9 us
    all_to_all x1, blocking collectives, body(): lax.all_to_all(attn, 'head', 0, 0, tiled=True).reshape(rows * heads, -1)  16.8 us
    all_to_all x1, blocking collectives, body(): lax.all_to_all(term, 'head', 0, 0, tiled=True, axis_index_groups=Z_GROUPS)  13.5 us
    all_to_all x1, waiting for transfers between devices, body(): lax.all_to_all(query, 'head', 0, 0, tiled=True).reshape(rows * heads, -1)  12.4 us
    all_to_all x1, starting transfers between devices, body(): lax.all_to_all(query, 'head', 0, 0, tiled=True).reshape(rows * heads, -1)  11.4 us
    ppermute x3, waiting for transfers between devices, shift_y(): return lax.ppermute(x, 'head', pairs)  10.9 us
    all_to_all x1, blocking collectives, body(): lax.all_to_all(values, 'head', 0, 0, tiled=True, axis_index_groups=Y_GROUPS)  9.17 us
  transfers between devices with their start and end apart: 12, of which 5 were waited for; matrix products, arithmetic and copies ran while one was open for 1% of the time, Pallas kernels for 8%

profile of v6, /device:TPU:8, one launch (start us, length us, event | category | flops | bytes accessed | tf_op | source)
XLA Modules:
  0.0 182.2 jit_solution(1762359451013687460)
XLA Ops:
  6.6 29.0 %prepare.1 = (bf16[192,768]{1,0:T(8,128)(2,1)S(1)}, bf16[64,1792]{1,0:T(8,128)(2,1)}, bf16[64,1792]{1,0:T(8,128)(2,1)}, bf16[64,1792]{1,0:T(8,128)(2,1)}, bf16[64,1792]{1,0:T(8,128)(2,1)}) custom-call(s32[1]{0:T(128)} %bitcast.y_ref, bf16[192,512]{1,0:T(8,128)(2,1)} %nope_hbm.1, bf16[192,256]{1,0:T(8,128)(2,1)} %rope_hbm.1, bf16[64,7168]{1,0:T(8,128)(2,1)} %bitcast.19), custom_call_target="tpu_custom_call" | custom-call | tf_op jit(solution)/shard_map/prepare/pallas_call | solution.py:57
  35.6 0.1 collective-permute-start.2
  35.7 2.8 %collective-permute-start.1 = (bf16[192,768]{1,0:T(8,128)(2,1)S(1)}, bf16[192,768]{1,0:T(8,128)(2,1)S(1)}, u32[]{:S(2)}, u32[]{:S(2)}) collective-permute-start(bf16[192,768]{1,0:T(8,128)(2,1)S(1)} %get-tuple-element.59.refs_1_), channel_id=1, source_target_pairs={{0,192},{32,96},{64,0},{96,160},{128,64},{160,224},{192,128},{224,... | collective-permute-start | bytes 884744 | tf_op jit(solution)/shard_map/ppermute | solution.py:397
  38.5 1.6 collective-permute-start.3
  40.1 1.9 %collective-permute-start.4 = (bf16[64,1792]{1,0:T(8,128)(2,1)}, bf16[64,1792]{1,0:T(8,128)(2,1)S(1)}, u32[]{:S(2)}, u32[]{:S(2)}) collective-permute-start(bf16[64,1792]{1,0:T(8,128)(2,1)} %get-tuple-element.42), channel_id=1, source_target_pairs={{0,16},{1,17},{2,18},{3,19},{4,20},{5,21},{6,22},{7,23},{8,24},{9,... | collective-permute-start | bytes 688136 | tf_op jit(solution)/shard_map/ppermute | solution.py:402
  42.0 0.1 stack.36
  42.1 0.1 select_reduce_fusion.place_ref
  42.2 0.7 convert_element_type.3
  42.9 1.6 arrange.1.refs_0_
  44.5 0.2 multiply_sine_fusion
  44.7 2.5 %collective-permute-done.3.refs_1_ = bf16[64,1792]{1,0:T(8,128)(2,1)S(1)} collective-permute-done((bf16[64,1792]{1,0:T(8,128)(2,1)}, bf16[64,1792]{1,0:T(8,128)(2,1)S(1)}, u32[]{:S(2)}, u32[]{:S(2)}) %collective-permute-start.3) | collective-permute-done | bytes 229408 | tf_op jit(solution)/shard_map/ppermute | solution.py:402
  47.2 2.2 %collective-permute-done.4.refs_2_ = bf16[64,1792]{1,0:T(8,128)(2,1)S(1)} collective-permute-done((bf16[64,1792]{1,0:T(8,128)(2,1)}, bf16[64,1792]{1,0:T(8,128)(2,1)S(1)}, u32[]{:S(2)}, u32[]{:S(2)}) %collective-permute-start.4) | collective-permute-done | bytes 229408 | tf_op jit(solution)/shard_map/ppermute | solution.py:402
  49.4 0.7 copy-done.7
  50.1 0.5 collective-permute-start.7
  50.6 0.3 collective-permute-start.5
  50.9 5.1 %collective-permute-start.6 = (bf16[64,1792]{1,0:T(8,128)(2,1)}, bf16[64,1792]{1,0:T(8,128)(2,1)S(1)}, u32[]{:S(2)}, u32[]{:S(2)}) collective-permute-start(bf16[64,1792]{1,0:T(8,128)(2,1)} %get-tuple-element.49), channel_id=1, source_target_pairs={{0,24},{1,25},{2,26},{3,27},{4,28},{5,29},{6,30},{7,31},{8,0},{9,1... | collective-permute-start | bytes 688136 | tf_op jit(solution)/shard_map/ppermute | solution.py:402
  56.0 6.2 %collective-permute-done.6.refs_3_ = bf16[64,1792]{1,0:T(8,128)(2,1)S(1)} collective-permute-done((bf16[64,1792]{1,0:T(8,128)(2,1)}, bf16[64,1792]{1,0:T(8,128)(2,1)S(1)}, u32[]{:S(2)}, u32[]{:S(2)}) %collective-permute-start.6) | collective-permute-done | bytes 229408 | tf_op jit(solution)/shard_map/ppermute | solution.py:402
  62.2 0.1 collective-permute-start.9
  62.3 1.6 collective-permute-done.9.refs_8_
  63.9 0.7 copy-done.1
  64.6 28.9 %stack.37 = bf16[4,64,1792]{2,1,0:T(8,128)(2,1)} custom-call(s32[1]{0:T(128)} %bitcast.y_ref, bf16[64,1792]{1,0:T(8,128)(2,1)} %get-tuple-element.69.refs_0_, bf16[64,1792]{1,0:T(8,128)(2,1)} %copy-done.6, bf16[64,1792]{1,0:T(8,128)(2,1)} %copy-done.7, bf16[64,1792]{1,0:T(8,128)(2,1)} %copy-done.8), custom_call_target="tpu_custom_call" | custom-call | tf_op jit(solution)/shard_map/stack/pallas_call | solution.py:105
  93.6 1.0 copy-done.2
  94.5 3.1 %project.1 = bf16[256,640]{1,0:T(8,128)(2,1)} custom-call(bf16[8,64,192]{2,1,0:T(8,128)(2,1)S(1)} %arrange.1.refs_0_, bf16[192,768]{1,0:T(8,128)(2,1)S(1)} %get-tuple-element.59.refs_1_, bf16[192,768]{1,0:T(8,128)(2,1)S(1)} %collective-permute-done.refs_2_, bf16[192,768]{1,0:T(8,128)(2,1)S(1)} %collective-permute-done.1.refs_3_, ...), custom_call_target="tpu_custom_call" | custom-call | tf_op jit(solution)/shard_map/project/pallas_call | solution.py:173
  97.7 11.4 %all-to-all-start = ((bf16[32,8,640]{2,1,0:T(8,128)(2,1)}), bf16[32,8,640]{2,1,0:T(8,128)(2,1)S(1)}, u32[]{:S(2)}, u32[]{:S(2)}) async-start(bf16[32,8,640]{2,1,0:T(8,128)(2,1)} %bitcast.10), calls=%async_computation | async-start | bytes 655360 | tf_op jit(solution)/shard_map/all_to_all | solution.py:473
  109.1 12.4 %all-to-all-done = bf16[32,8,640]{2,1,0:T(8,128)(2,1)S(1)} async-done(((bf16[32,8,640]{2,1,0:T(8,128)(2,1)}), bf16[32,8,640]{2,1,0:T(8,128)(2,1)S(1)}, u32[]{:S(2)}, u32[]{:S(2)}) %all-to-all-start) | async-done | bytes 327712 | tf_op jit(solution)/shard_map/all_to_all | solution.py:473
  121.5 8.7 %attend.1 = bf16[256,512]{1,0:T(8,128)(2,1)S(1)} custom-call(s32[2]{0:T(128)S(1)} %dynamic_slice.3.refs_0_, s32[2,32]{1,0:T(2,128)S(1)} %copy-done.4, bf16[256,640]{1,0:T(8,128)(2,1)S(1)} %bitcast.15, bf16[2,512]{1,0:T(2,128)(2,1)S(1)} %copy-done.3, bf16[2,64]{1,0:T(2,128)(2,1)S(1)} %copy-done.5, bf16[64,128,512]{2,1,0:T(8,128)(2,1)} %refs_5_.1, ...), custom_call_target="tpu_custom_call" | custom-call | tf_op jit(solution)/shard_map/attend/pallas_call | solution.py:273
  130.2 16.8 %all_to_all.20 = bf16[32,8,512]{2,1,0:T(8,128)(2,1)S(1)} all-to-all(bf16[32,8,512]{2,1,0:T(8,128)(2,1)S(1)} %bitcast.16), channel_id=1, replica_groups=mesh['dp'=8,'head'=32] {'head'}, dimensions={0} | all-to-all | bytes 524288 | tf_op jit(solution)/shard_map/all_to_all | solution.py:479
  147.0 1.4 values.1
  148.4 9.2 %all_to_all.21.values_ref = bf16[4,64,512]{2,1,0:T(8,128)(2,1)S(1)} all-to-all(bf16[4,64,512]{2,1,0:T(8,128)(2,1)S(1)} %broadcast_in_dim.16), channel_id=1, replica_groups={{0,8,16,24},{1,9,17,25},{2,10,18,26},{3,11,19,27},{4,12,20,28},{5,13,21..., dimensions={0} | all-to-all | bytes 524288 | tf_op jit(solution)/shard_map/all_to_all | solution.py:482
  157.6 3.6 %mix.1 = bf16[8,64,224]{2,1,0:T(8,128)(2,1)S(1)} custom-call(bf16[4,64,512]{2,1,0:T(8,128)(2,1)S(1)} %all_to_all.21.values_ref, bf16[8,4,64,1792]{3,2,1,0:T(8,128)(2,1)} %bitcast.18), custom_call_target="tpu_custom_call" | custom-call | tf_op jit(solution)/shard_map/mix/pallas_call | solution.py:358
  161.2 13.5 %all_to_all.22.terms_ref = bf16[8,64,224]{2,1,0:T(8,128)(2,1)S(1)} all-to-all(bf16[8,64,224]{2,1,0:T(8,128)(2,1)S(1)} %mix.1), channel_id=1, replica_groups={{0,1,2,3,4,5,6,7},{8,9,10,11,12,13,14,15},{16,17,18,19,20,21,22,23},{24..., dimensions={0} | all-to-all | bytes 458752 | tf_op jit(solution)/shard_map/all_to_all | solution.py:484
  174.7 0.7 finish.1
  (31 shorter events, 0.2 us)
Async XLA Ops:
  6.5 102.5 %copy-start.9 = (s32[64]{0:T(128)S(1)}, s32[64]{0:T(128)}, u32[]{:S(2)}) copy-start(s32[64]{0:T(128)} %param.22) | copy-start | bytes 772
  6.5 114.9 %copy-start.4 = (s32[2,32]{1,0:T(2,128)S(1)}, s32[2,32]{1,0:T(2,128)}, u32[]{:S(2)}) copy-start(s32[2,32]{1,0:T(2,128)} %refs_1_.2) | copy-start | bytes 772
  6.5 114.9 %copy-start.5 = (bf16[2,64]{1,0:T(2,128)(2,1)S(1)}, bf16[2,64]{1,0:T(2,128)(2,1)}, u32[]{:S(2)}) copy-start(bf16[2,64]{1,0:T(2,128)(2,1)} %refs_4_.1) | copy-start | bytes 772
  6.5 114.9 %copy-start.3 = (bf16[2,512]{1,0:T(2,128)(2,1)S(1)}, bf16[2,512]{1,0:T(2,128)(2,1)}, u32[]{:S(2)}) copy-start(bf16[2,512]{1,0:T(2,128)(2,1)} %refs_3_.1) | copy-start | bytes 6148
  6.5 114.9 %copy-start = (bf16[64,64,128]{2,1,0:T(8,128)(2,1)S(1)}, bf16[64,64,128]{2,1,0:T(8,128)(2,1)}, u32[]{:S(2)}) copy-start(bf16[64,64,128]{2,1,0:T(8,128)(2,1)} %refs_6_.1) | copy-start | bytes 3145732
  6.5 151.1 %all-gather.3.cloned.1.call-start = ((), (), s32[]{:S(2)}) async-start(), calls=%async_computation.4 | async-start | bytes 8257536 | tf_op jit(solution)/shard_map/all_gather | solution.py:470
  35.6 13.8 %collective-permute-start.2 = (bf16[192,768]{1,0:T(8,128)(2,1)S(1)}, bf16[192,768]{1,0:T(8,128)(2,1)S(1)}, u32[]{:S(2)}, u32[]{:S(2)}) collective-permute-start(bf16[192,768]{1,0:T(8,128)(2,1)S(1)} %get-tuple-element.59.refs_1_), channel_id=1, source_target_pairs={{0,32},{32,0},{64,96},{96,64},{128,160},{160,128},{192,224},{224,1... | collective-permute-start | bytes 884744 | tf_op jit(solution)/shard_map/ppermute | solution.py:397
  35.7 13.7 %collective-permute-start.1 = (bf16[192,768]{1,0:T(8,128)(2,1)S(1)}, bf16[192,768]{1,0:T(8,128)(2,1)S(1)}, u32[]{:S(2)}, u32[]{:S(2)}) collective-permute-start(bf16[192,768]{1,0:T(8,128)(2,1)S(1)} %get-tuple-element.59.refs_1_), channel_id=1, source_target_pairs={{0,192},{32,96},{64,0},{96,160},{128,64},{160,224},{192,128},{224,... | collective-permute-start | bytes 884744 | tf_op jit(solution)/shard_map/ppermute | solution.py:397
  38.5 10.9 %collective-permute-start = (bf16[192,768]{1,0:T(8,128)(2,1)S(1)}, bf16[192,768]{1,0:T(8,128)(2,1)S(1)}, u32[]{:S(2)}, u32[]{:S(2)}) collective-permute-start(bf16[192,768]{1,0:T(8,128)(2,1)S(1)} %get-tuple-element.59.refs_1_), channel_id=1, source_target_pairs={{0,64},{32,224},{64,128},{96,32},{128,192},{160,96},{192,0},{224,1... | collective-permute-start | bytes 884744 | tf_op jit(solution)/shard_map/ppermute | solution.py:397
  38.5 8.7 %collective-permute-start.3 = (bf16[64,1792]{1,0:T(8,128)(2,1)}, bf16[64,1792]{1,0:T(8,128)(2,1)S(1)}, u32[]{:S(2)}, u32[]{:S(2)}) collective-permute-start(bf16[64,1792]{1,0:T(8,128)(2,1)} %get-tuple-element.41), channel_id=1, source_target_pairs={{0,8},{1,9},{2,10},{3,11},{4,12},{5,13},{6,14},{7,15},{8,16},{9,17... | collective-permute-start | bytes 688136 | tf_op jit(solution)/shard_map/ppermute | solution.py:402
  40.1 9.3 %collective-permute-start.4 = (bf16[64,1792]{1,0:T(8,128)(2,1)}, bf16[64,1792]{1,0:T(8,128)(2,1)S(1)}, u32[]{:S(2)}, u32[]{:S(2)}) collective-permute-start(bf16[64,1792]{1,0:T(8,128)(2,1)} %get-tuple-element.42), channel_id=1, source_target_pairs={{0,16},{1,17},{2,18},{3,19},{4,20},{5,21},{6,22},{7,23},{8,24},{9,... | collective-permute-start | bytes 688136 | tf_op jit(solution)/shard_map/ppermute | solution.py:402
  47.2 2.2 %copy-start.6 = (bf16[64,1792]{1,0:T(8,128)(2,1)}, bf16[64,1792]{1,0:T(8,128)(2,1)S(1)}, u32[]{:S(2)}) copy-start(bf16[64,1792]{1,0:T(8,128)(2,1)S(1)} %collective-permute-done.3.refs_1_) | copy-start | bytes 688132
  49.4 0.7 copy-start.7
  50.1 12.1 %collective-permute-start.8 = (bf16[192,768]{1,0:T(8,128)(2,1)S(1)}, bf16[192,768]{1,0:T(8,128)(2,1)S(1)}, u32[]{:S(2)}, u32[]{:S(2)}) collective-permute-start(bf16[192,768]{1,0:T(8,128)(2,1)S(1)} %collective-permute-done.1.refs_3_), channel_id=1, source_target_pairs={{0,32},{32,0},{64,96},{96,64},{128,160},{160,128},{192,224},{224,1... | collective-permute-start | bytes 884744 | tf_op jit(solution)/shard_map/ppermute | solution.py:397
  50.1 12.1 %collective-permute-start.7 = (bf16[192,768]{1,0:T(8,128)(2,1)S(1)}, bf16[192,768]{1,0:T(8,128)(2,1)S(1)}, u32[]{:S(2)}, u32[]{:S(2)}) collective-permute-start(bf16[192,768]{1,0:T(8,128)(2,1)S(1)} %collective-permute-done.refs_2_), channel_id=1, source_target_pairs={{0,32},{32,0},{64,96},{96,64},{128,160},{160,128},{192,224},{224,1... | collective-permute-start | bytes 884744 | tf_op jit(solution)/shard_map/ppermute | solution.py:397
  50.6 11.6 %collective-permute-start.5 = (bf16[192,768]{1,0:T(8,128)(2,1)S(1)}, bf16[192,768]{1,0:T(8,128)(2,1)S(1)}, u32[]{:S(2)}, u32[]{:S(2)}) collective-permute-start(bf16[192,768]{1,0:T(8,128)(2,1)S(1)} %collective-permute-done.refs_2_), channel_id=1, source_target_pairs={{0,64},{32,224},{64,128},{96,32},{128,192},{160,96},{192,0},{224,1... | collective-permute-start | bytes 884744 | tf_op jit(solution)/shard_map/ppermute | solution.py:397
  50.9 11.3 %collective-permute-start.6 = (bf16[64,1792]{1,0:T(8,128)(2,1)}, bf16[64,1792]{1,0:T(8,128)(2,1)S(1)}, u32[]{:S(2)}, u32[]{:S(2)}) collective-permute-start(bf16[64,1792]{1,0:T(8,128)(2,1)} %get-tuple-element.49), channel_id=1, source_target_pairs={{0,24},{1,25},{2,26},{3,27},{4,28},{5,29},{6,30},{7,31},{8,0},{9,1... | collective-permute-start | bytes 688136 | tf_op jit(solution)/shard_map/ppermute | solution.py:402
  62.2 1.7 copy-start.8
  62.2 1.7 collective-permute-start.9
  63.9 0.7 copy-start.1
  93.6 1.0 copy-start.2
  97.7 23.8 %all-to-all-start = ((bf16[32,8,640]{2,1,0:T(8,128)(2,1)}), bf16[32,8,640]{2,1,0:T(8,128)(2,1)S(1)}, u32[]{:S(2)}, u32[]{:S(2)}) async-start(bf16[32,8,640]{2,1,0:T(8,128)(2,1)} %bitcast.10), calls=%async_computation | async-start | bytes 655360 | tf_op jit(solution)/shard_map/all_to_all | solution.py:473
Sparse Core Ops, SparseCore 0:
  93.7 48.7 all-gather.2

commit v7 on v5

--- a/solution.py
+++ b/solution.py
@@ -34,17 +34,17 @@
 
 
 def prepare_kernel(y_ref, nope_hbm, rope_hbm, weights_hbm, both_ref, *refs):
-    cut_refs, sem = refs[:Y], refs[Y]
+    cut_refs, sem = refs[: Y - 1], refs[Y - 1]
     width = nope_hbm.shape[1]
     columns = cut_refs[0].shape[1]
     copies = [
         pltpu.make_async_copy(nope_hbm, both_ref.at[:, :width], sem.at[0]),
         pltpu.make_async_copy(rope_hbm, both_ref.at[:, width:], sem.at[1]),
     ]
-    for k in range(Y):
+    for k in range(1, Y):
         start = pl.multiple_of(lax.rem(y_ref[0] + k, Y) * columns, 128)
         source = weights_hbm.at[:, pl.ds(start, columns)]
-        copies.append(pltpu.make_async_copy(source, cut_refs[k], sem.at[2 + k]))
+        copies.append(pltpu.make_async_copy(source, cut_refs[k - 1], sem.at[1 + k]))
     for copy in copies:
         copy.start()
     for copy in copies:
@@ -57,10 +57,10 @@
     return pl.pallas_call(
         prepare_kernel,
         out_shape=(jax.ShapeDtypeStruct((depth, w_qnope.shape[1] + w_qrope.shape[1]), BF16),)
-        + (cut,) * Y,
+        + (cut,) * (Y - 1),
         in_specs=[SCALARS] + [IN_HBM] * 3,
-        out_specs=(WHOLE,) * (1 + Y),
-        scratch_shapes=[pltpu.SemaphoreType.DMA((2 + Y,))],
+        out_specs=(WHOLE,) * Y,
+        scratch_shapes=[pltpu.SemaphoreType.DMA((1 + Y,))],
         compiler_params=params(8),
         name="prepare",
     )(y, *[in_hbm(a) for a in (w_qnope, w_qrope, weights)])
@@ -97,28 +97,35 @@
     )(place, in_hbm(latent), in_hbm(w_uk))
 
 
-def stack_kernel(y_ref, *refs):
-    pieces, (out_ref, sem) = refs[:Y], refs[Y:]
+def stack_kernel(y_ref, weights_hbm, *refs):
+    pieces, (out_ref, own_ref, sem) = refs[: Y - 1], refs[Y - 1 :]
+    y = y_ref[0]
+    columns = own_ref.shape[1]
+    span = pl.ds(pl.multiple_of(y * columns, 128), columns)
+    own = pltpu.make_async_copy(weights_hbm.at[:, span], own_ref, sem.at[0])
+    own.start()
     copies = []
-    for k in range(Y):
-        target = out_ref.at[lax.rem(y_ref[0] + (Y - k), Y)]
-        copies.append(pltpu.make_async_copy(pieces[k], target, sem.at[k]))
-    for copy in copies:
-        copy.start()
+    for k in range(1, Y):
+        target = out_ref.at[lax.rem(y + (Y - k), Y)]
+        copies.append(pltpu.make_async_copy(pieces[k - 1], target, sem.at[k]))
+        copies[-1].start()
+    own.wait()
+    copies.append(pltpu.make_async_copy(own_ref, out_ref.at[y], sem.at[Y]))
+    copies[-1].start()
     for copy in copies:
         copy.wait()
 
 
-def stack(y, pieces):
+def stack(y, weights, pieces):
     return pl.pallas_call(
         stack_kernel,
         out_shape=jax.ShapeDtypeStruct((Y,) + pieces[0].shape, BF16),
-        in_specs=[SCALARS] + [pl.BlockSpec(memory_space=pl.ANY)] * Y,
+        in_specs=[SCALARS, IN_HBM] + [pl.BlockSpec(memory_space=pl.ANY)] * (Y - 1),
         out_specs=IN_HBM,
-        scratch_shapes=[pltpu.SemaphoreType.DMA((Y,))],
+        scratch_shapes=[pltpu.VMEM(pieces[0].shape, BF16), pltpu.SemaphoreType.DMA((Y + 1,))],
         compiler_params=params(8),
         name="stack",
-    )(y, *pieces)
+    )(y, in_hbm(weights), *pieces)
 
 
 def one_hot(rows, columns, place, keep=None):
@@ -186,8 +193,8 @@
 
 
 def attend_kernel(
-    heads,     length_ref, table_ref, query_ref, new_ref, new_rope_ref, latent_hbm, rope_ref, out_ref,
-    scores_ref, held_ref, high_ref, absorbed_ref, rotary_ref, row_ref, slot_ref, sem,
+    heads,     length_ref, table_ref, query_ref, new_ref, new_rope_ref, latent_hbm, rope_hbm, out_ref,
+    scores_ref, held_ref, rope_ref, high_ref, absorbed_ref, rotary_ref, row_ref, slot_ref, sem,
 ):
     own, slots = table_ref.shape
     pool, page, width = held_ref.shape
@@ -200,6 +207,8 @@
     for c in range(CHUNKS):
         span = pl.ds(c * share, share)
         copies.append(pltpu.make_async_copy(latent_hbm.at[span], held_ref.at[span], sem.at[c]))
+    rope_copy = pltpu.make_async_copy(rope_hbm, rope_ref, sem.at[CHUNKS])
+    rope_copy.start()
     for copy in copies:
         copy.start()
     for r in range(own):
@@ -224,6 +233,7 @@
         score_new += jnp.sum(q_rot.astype(F32) * new_rope, axis=1, keepdims=True)
         new_scores.append(score_new * factor)
     high_ref[...] = jnp.full(high_ref.shape, -jnp.inf, F32)
+    rope_copy.wait()
     for c in range(CHUNKS):
         copies[c].wait()
         for g in range(c * share, (c + 1) * share):
@@ -277,21 +287,22 @@
     return pl.pallas_call(
         kernel,
         out_shape=jax.ShapeDtypeStruct((rows, width), BF16),
-        in_specs=[SCALARS, SCALARS] + [WHOLE] * 3 + [IN_HBM, WHOLE],
+        in_specs=[SCALARS, SCALARS] + [WHOLE] * 3 + [IN_HBM, IN_HBM],
         out_specs=WHOLE,
         scratch_shapes=[
             pltpu.VMEM((own, slots, all_heads, page), F32),
             pltpu.VMEM(cache_latent.shape, BF16),
+            pltpu.VMEM(cache_rope.shape, BF16),
             pltpu.VMEM((own, all_heads, page), F32),
             pltpu.VMEM((own, all_heads, width), BF16),
             pltpu.VMEM((own, all_heads, rope_dim), BF16),
             pltpu.SMEM((pool,), jnp.int32),
             pltpu.SMEM((pool,), jnp.int32),
-            pltpu.SemaphoreType.DMA((CHUNKS,)),
+            pltpu.SemaphoreType.DMA((CHUNKS + 1,)),
         ],
         compiler_params=params(24),
         name="attend",
-    )(lengths, table, query, new_latent, new_rope, in_hbm(cache_latent), cache_rope)
+    )(lengths, table, query, new_latent, new_rope, in_hbm(cache_latent), in_hbm(cache_rope))
 
 
 def values_kernel(parts, attn_ref, uv_hbm, out_ref, uv_ref, sem):
@@ -457,21 +468,21 @@
     flat = w_out.reshape(depth, width_all)
     both, *cuts = prepare(y_scalar, w_qnope, w_qrope, flat)
     ahead, behind, beside = shift_dp(both, 1, 0), shift_dp(both, -1, 0), shift_dp(both, 0, 1)
-    cuts[2] = shift_y(cuts[2], 2)
+    cuts[1] = shift_y(cuts[1], 2)
     latent, uk = arrange(piece_places(), q_latent, w_uk)
     ahead, behind, beside, cuts, cos, sin, latent, uk = lax.optimization_barrier(
         (ahead, behind, beside, cuts, cos, sin, latent, uk)
     )
     far = shift_dp(ahead, 1, 0)
     ahead_beside, behind_beside = shift_dp(ahead, 0, 1), shift_dp(behind, 0, 1)
-    cuts[1], cuts[3] = shift_y(cuts[1], 1), shift_y(cuts[3], 3)
+    cuts[0], cuts[2] = shift_y(cuts[0], 1), shift_y(cuts[2], 3)
     far, cuts, ahead_beside, behind_beside = lax.optimization_barrier(
         (far, cuts, ahead_beside, behind_beside)
     )
     pieces = [both, ahead, behind, far, beside]
     pieces += [ahead_beside, behind_beside, shift_dp(far, 0, 1)]
     cuts, pieces = lax.optimization_barrier((cuts, pieces))
-    panel = lax.all_gather(stack(y_scalar, cuts), "dp", axis=0)
+    panel = lax.all_gather(stack(y_scalar, flat, cuts), "dp", axis=0)
     query = project(latent, pieces, uk, cos, sin)
     query = query.reshape(sources, own * heads, query.shape[1])
     query = lax.all_to_all(query, "head", 0, 0, tiled=True).reshape(rows * heads, -1)

time: 128 us -> 122 us (0.953)
  local copies, waits for them, and re-layouts: 8.5 us -> 0.2 us
    unnamed x34 -> x10, local copies, waits for them, and re-layouts: 8.32 us -> 0.02 us
  transfers between devices with their start and end apart: 12 -> 12, of which waited for: 5 -> 5; matrix products, arithmetic and copies ran while one was open for 1% -> 1% of each run, Pallas kernels for 11% -> 12%
where the time goes in v7:
time: 122 us
  blocking collectives  39.5 us (32%)
  waiting for transfers between devices  26.1 us (21%)
  Pallas kernels  21.8 us (18%)
  starting transfers between devices  19.7 us (16%)
  between operations  13.6 us (11%)
    all_to_all x1, blocking collectives, body(): lax.all_to_all(attn, 'head', 0, 0, tiled=True).reshape(rows * heads, -1)  16.8 us
    all_to_all x1, blocking collectives, body(): lax.all_to_all(term, 'head', 0, 0, tiled=True, axis_index_groups=Z_GROUPS)  13.5 us
    all_to_all x1, waiting for transfers between devices, body(): lax.all_to_all(query, 'head', 0, 0, tiled=True).reshape(rows * heads, -1)  12.4 us
    ppermute x3, waiting for transfers between devices, shift_y(): return lax.ppermute(x, 'head', pairs)  12.1 us
    all_to_all x1, starting transfers between devices, body(): lax.all_to_all(query, 'head', 0, 0, tiled=True).reshape(rows * heads, -1)  11.5 us
    all_to_all x1, blocking collectives, body(): lax.all_to_all(values, 'head', 0, 0, tiled=True, axis_index_groups=Y_GROUPS)  9.18 us
    pallas_call x1, Pallas kernels, attend(): pl.pallas_call(kernel, out_shape=jax.ShapeDtypeStruct((rows, width), BF16...  9.11 us
    ppermute x3, starting transfers between devices, shift_y(): return lax.ppermute(x, 'head', pairs)  4.32 us
  transfers between devices with their start and end apart: 12, of which 5 were waited for; matrix products, arithmetic and copies ran while one was open for 1% of the time, Pallas kernels for 12%

profile of v7, /device:TPU:8, one launch (start us, length us, event | category | flops | bytes accessed | tf_op | source)
XLA Modules:
  0.0 121.8 jit_solution(4427322796617043417)
XLA Ops:
  6.5 0.0 all-gather.3.cloned.1.call-start
  6.6 1.3 %prepare.1 = (bf16[192,768]{1,0:T(8,128)(2,1)S(1)}, bf16[64,1792]{1,0:T(8,128)(2,1)S(1)}, bf16[64,1792]{1,0:T(8,128)(2,1)S(1)}, bf16[64,1792]{1,0:T(8,128)(2,1)S(1)}) custom-call(s32[1]{0:T(128)} %bitcast.y_ref, bf16[192,512]{1,0:T(8,128)(2,1)} %nope_hbm.1, bf16[192,256]{1,0:T(8,128)(2,1)} %rope_hbm.1, bf16[64,7168]{1,0:T(8,128)(2,1)} %bitcast.19), custom_call_target="tpu_custom_call" | custom-call | tf_op jit(solution)/shard_map/prepare/pallas_call | solution.py:57
  7.9 0.1 collective-permute-start.2
  8.0 2.8 %collective-permute-start.1 = (bf16[192,768]{1,0:T(8,128)(2,1)S(1)}, bf16[192,768]{1,0:T(8,128)(2,1)S(1)}, u32[]{:S(2)}, u32[]{:S(2)}) collective-permute-start(bf16[192,768]{1,0:T(8,128)(2,1)S(1)} %get-tuple-element.57.refs_1_), channel_id=1, source_target_pairs={{0,192},{32,96},{64,0},{96,160},{128,64},{160,224},{192,128},{224,... | collective-permute-start | bytes 884744 | tf_op jit(solution)/shard_map/ppermute | solution.py:412
  10.9 2.3 %collective-permute-start.3 = (bf16[64,1792]{1,0:T(8,128)(2,1)S(1)}, bf16[64,1792]{1,0:T(8,128)(2,1)S(1)}, u32[]{:S(2)}, u32[]{:S(2)}) collective-permute-start(bf16[64,1792]{1,0:T(8,128)(2,1)S(1)} %get-tuple-element.40), channel_id=1, source_target_pairs={{0,16},{1,17},{2,18},{3,19},{4,20},{5,21},{6,22},{7,23},{8,24},{9,... | collective-permute-start | bytes 688136 | tf_op jit(solution)/shard_map/ppermute | solution.py:417
  13.2 0.1 stack.36
  13.3 0.1 select_reduce_fusion.place_ref
  13.4 0.7 convert_element_type.3
  14.1 1.7 %arrange.1 = (bf16[8,64,192]{2,1,0:T(8,128)(2,1)S(1)}, bf16[4,128,512]{2,1,0:T(8,128)(2,1)S(1)}) custom-call(s32[8]{0:T(128)S(1)} %select_reduce_fusion.place_ref, bf16[64,1536]{1,0:T(8,128)(2,1)} %latent_hbm.1, bf16[4,128,512]{2,1,0:T(8,128)(2,1)} %uk_hbm.1), custom_call_target="tpu_custom_call" | custom-call | tf_op jit(solution)/shard_map/arrange/pallas_call | solution.py:86
  15.8 0.2 multiply_sine_fusion
  16.0 4.3 %collective-permute-done.3.refs_1_ = bf16[64,1792]{1,0:T(8,128)(2,1)S(1)} collective-permute-done((bf16[64,1792]{1,0:T(8,128)(2,1)S(1)}, bf16[64,1792]{1,0:T(8,128)(2,1)S(1)}, u32[]{:S(2)}, u32[]{:S(2)}) %collective-permute-start.3) | collective-permute-done | bytes 229408 | tf_op jit(solution)/shard_map/ppermute | solution.py:417
  20.2 0.1 collective-permute-start.8
  20.3 0.5 collective-permute-start.7
  20.8 0.3 collective-permute-start.4
  21.1 1.6 %collective-permute-start.5 = (bf16[64,1792]{1,0:T(8,128)(2,1)}, bf16[64,1792]{1,0:T(8,128)(2,1)S(1)}, u32[]{:S(2)}, u32[]{:S(2)}) collective-permute-start(bf16[64,1792]{1,0:T(8,128)(2,1)} %copy-done.3), channel_id=1, source_target_pairs={{0,8},{1,9},{2,10},{3,11},{4,12},{5,13},{6,14},{7,15},{8,16},{9,17... | collective-permute-start | bytes 688136 | tf_op jit(solution)/shard_map/ppermute | solution.py:417
  22.7 0.4 collective-permute-start.6
  23.1 6.5 %collective-permute-done.5.refs_0_ = bf16[64,1792]{1,0:T(8,128)(2,1)S(1)} collective-permute-done((bf16[64,1792]{1,0:T(8,128)(2,1)}, bf16[64,1792]{1,0:T(8,128)(2,1)S(1)}, u32[]{:S(2)}, u32[]{:S(2)}) %collective-permute-start.5) | collective-permute-done | bytes 229408 | tf_op jit(solution)/shard_map/ppermute | solution.py:417
  29.7 1.3 %collective-permute-done.6.refs_2_ = bf16[64,1792]{1,0:T(8,128)(2,1)S(1)} collective-permute-done((bf16[64,1792]{1,0:T(8,128)(2,1)S(1)}, bf16[64,1792]{1,0:T(8,128)(2,1)S(1)}, u32[]{:S(2)}, u32[]{:S(2)}) %collective-permute-start.6) | collective-permute-done | bytes 229408 | tf_op jit(solution)/shard_map/ppermute | solution.py:417
  31.0 0.1 collective-permute-start.9
  31.1 1.6 %collective-permute-done.9.refs_8_ = bf16[192,768]{1,0:T(8,128)(2,1)S(1)} collective-permute-done((bf16[192,768]{1,0:T(8,128)(2,1)S(1)}, bf16[192,768]{1,0:T(8,128)(2,1)S(1)}, u32[]{:S(2)}, u32[]{:S(2)}) %collective-permute-start.9) | collective-permute-done | bytes 294944 | tf_op jit(solution)/shard_map/ppermute | solution.py:412
  32.7 1.9 %stack.37 = bf16[4,64,1792]{2,1,0:T(8,128)(2,1)} custom-call(s32[1]{0:T(128)} %bitcast.y_ref, bf16[64,7168]{1,0:T(8,128)(2,1)} %bitcast.20, bf16[64,1792]{1,0:T(8,128)(2,1)S(1)} %collective-permute-done.5.refs_0_, bf16[64,1792]{1,0:T(8,128)(2,1)S(1)} %collective-permute-done.3.refs_1_, bf16[64,1792]{1,0:T(8,128)(2,1)S(1)} %collective-permute-done.6.refs_2_), custom_call_target="tpu_custom_call" | custom-call | tf_op jit(solution)/shard_map/stack/pallas_call | solution.py:120
  34.6 2.1 %project.1 = bf16[256,640]{1,0:T(8,128)(2,1)} custom-call(bf16[8,64,192]{2,1,0:T(8,128)(2,1)S(1)} %get-tuple-element.44.refs_0_, bf16[192,768]{1,0:T(8,128)(2,1)S(1)} %get-tuple-element.57.refs_1_, bf16[192,768]{1,0:T(8,128)(2,1)S(1)} %collective-permute-done.refs_2_, bf16[192,768]{1,0:T(8,128)(2,1)S(1)} %collective-permute-done.1.refs_3_, ...), custom_call_target="tpu_custom_call" | custom-call | tf_op jit(solution)/shard_map/project/pallas_call | solution.py:185
  36.8 11.5 %all-to-all-start = ((bf16[32,8,640]{2,1,0:T(8,128)(2,1)}), bf16[32,8,640]{2,1,0:T(8,128)(2,1)S(1)}, u32[]{:S(2)}, u32[]{:S(2)}) async-start(bf16[32,8,640]{2,1,0:T(8,128)(2,1)} %bitcast.10), calls=%async_computation | async-start | bytes 655360 | tf_op jit(solution)/shard_map/all_to_all | solution.py:488
  48.3 0.1 dynamic_slice.3.refs_0_
  48.3 12.4 %all-to-all-done = bf16[32,8,640]{2,1,0:T(8,128)(2,1)S(1)} async-done(((bf16[32,8,640]{2,1,0:T(8,128)(2,1)}), bf16[32,8,640]{2,1,0:T(8,128)(2,1)S(1)}, u32[]{:S(2)}, u32[]{:S(2)}) %all-to-all-start) | async-done | bytes 327712 | tf_op jit(solution)/shard_map/all_to_all | solution.py:488
  60.7 9.1 %attend.1 = bf16[256,512]{1,0:T(8,128)(2,1)S(1)} custom-call(s32[2]{0:T(128)S(1)} %dynamic_slice.3.refs_0_, s32[2,32]{1,0:T(2,128)S(1)} %copy-done.1, bf16[256,640]{1,0:T(8,128)(2,1)S(1)} %bitcast.15, bf16[2,512]{1,0:T(2,128)(2,1)S(1)} %copy-done, bf16[2,64]{1,0:T(2,128)(2,1)S(1)} %copy-done.2, bf16[64,128,512]{2,1,0:T(8,128)(2,1)} %refs_5_.1, ...), custom_call_target="tpu_custom_call" | custom-call | tf_op jit(solution)/shard_map/attend/pallas_call | solution.py:287
  69.8 16.8 %all_to_all.20 = bf16[32,8,512]{2,1,0:T(8,128)(2,1)S(1)} all-to-all(bf16[32,8,512]{2,1,0:T(8,128)(2,1)S(1)} %bitcast.16), channel_id=1, replica_groups=mesh['dp'=8,'head'=32] {'head'}, dimensions={0} | all-to-all | bytes 524288 | tf_op jit(solution)/shard_map/all_to_all | solution.py:494
  86.6 1.4 %values.1 = bf16[64,512]{1,0:T(8,128)(2,1)S(1)} custom-call(bf16[256,512]{1,0:T(8,128)(2,1)S(1)} %bitcast.17, bf16[4,512,128]{2,1,0:T(8,128)(2,1)} %refs_1_.3), custom_call_target="tpu_custom_call" | custom-call | tf_op jit(solution)/shard_map/values/pallas_call | solution.py:337
  88.1 9.2 %all_to_all.21.values_ref = bf16[4,64,512]{2,1,0:T(8,128)(2,1)S(1)} all-to-all(bf16[4,64,512]{2,1,0:T(8,128)(2,1)S(1)} %broadcast_in_dim.16), channel_id=1, replica_groups={{0,8,16,24},{1,9,17,25},{2,10,18,26},{3,11,19,27},{4,12,20,28},{5,13,21..., dimensions={0} | all-to-all | bytes 524288 | tf_op jit(solution)/shard_map/all_to_all | solution.py:497
  97.3 3.6 %mix.1 = bf16[8,64,224]{2,1,0:T(8,128)(2,1)S(1)} custom-call(bf16[4,64,512]{2,1,0:T(8,128)(2,1)S(1)} %all_to_all.21.values_ref, bf16[8,4,64,1792]{3,2,1,0:T(8,128)(2,1)} %bitcast.18), custom_call_target="tpu_custom_call" | custom-call | tf_op jit(solution)/shard_map/mix/pallas_call | solution.py:373
  100.9 13.5 %all_to_all.22.terms_ref = bf16[8,64,224]{2,1,0:T(8,128)(2,1)S(1)} all-to-all(bf16[8,64,224]{2,1,0:T(8,128)(2,1)S(1)} %mix.1), channel_id=1, replica_groups={{0,1,2,3,4,5,6,7},{8,9,10,11,12,13,14,15},{16,17,18,19,20,21,22,23},{24..., dimensions={0} | all-to-all | bytes 458752 | tf_op jit(solution)/shard_map/all_to_all | solution.py:499
  114.3 0.7 finish.1
  (21 shorter events, 0.1 us)
Async XLA Ops:
  6.5 41.7 %copy-start.4 = (s32[64]{0:T(128)S(1)}, s32[64]{0:T(128)}, u32[]{:S(2)}) copy-start(s32[64]{0:T(128)} %param.22) | copy-start | bytes 772
  6.5 54.2 %copy-start.1 = (s32[2,32]{1,0:T(2,128)S(1)}, s32[2,32]{1,0:T(2,128)}, u32[]{:S(2)}) copy-start(s32[2,32]{1,0:T(2,128)} %refs_1_.2) | copy-start | bytes 772
  6.5 54.2 %copy-start.2 = (bf16[2,64]{1,0:T(2,128)(2,1)S(1)}, bf16[2,64]{1,0:T(2,128)(2,1)}, u32[]{:S(2)}) copy-start(bf16[2,64]{1,0:T(2,128)(2,1)} %refs_4_.1) | copy-start | bytes 772
  6.5 54.2 %copy-start = (bf16[2,512]{1,0:T(2,128)(2,1)S(1)}, bf16[2,512]{1,0:T(2,128)(2,1)}, u32[]{:S(2)}) copy-start(bf16[2,512]{1,0:T(2,128)(2,1)} %refs_3_.1) | copy-start | bytes 6148
  6.5 90.7 %all-gather.3.cloned.1.call-start = ((), (), s32[]{:S(2)}) async-start(), calls=%async_computation.4 | async-start | bytes 8257536 | tf_op jit(solution)/shard_map/all_gather | solution.py:485
  7.9 3.0 %copy-start.3 = (bf16[64,1792]{1,0:T(8,128)(2,1)}, bf16[64,1792]{1,0:T(8,128)(2,1)S(1)}, u32[]{:S(2)}) copy-start(bf16[64,1792]{1,0:T(8,128)(2,1)S(1)} %get-tuple-element.46) | copy-start | bytes 688132
  7.9 12.3 %collective-permute-start.2 = (bf16[192,768]{1,0:T(8,128)(2,1)S(1)}, bf16[192,768]{1,0:T(8,128)(2,1)S(1)}, u32[]{:S(2)}, u32[]{:S(2)}) collective-permute-start(bf16[192,768]{1,0:T(8,128)(2,1)S(1)} %get-tuple-element.57.refs_1_), channel_id=1, source_target_pairs={{0,32},{32,0},{64,96},{96,64},{128,160},{160,128},{192,224},{224,1... | collective-permute-start | bytes 884744 | tf_op jit(solution)/shard_map/ppermute | solution.py:412
  8.0 12.2 %collective-permute-start.1 = (bf16[192,768]{1,0:T(8,128)(2,1)S(1)}, bf16[192,768]{1,0:T(8,128)(2,1)S(1)}, u32[]{:S(2)}, u32[]{:S(2)}) collective-permute-start(bf16[192,768]{1,0:T(8,128)(2,1)S(1)} %get-tuple-element.57.refs_1_), channel_id=1, source_target_pairs={{0,192},{32,96},{64,0},{96,160},{128,64},{160,224},{192,128},{224,... | collective-permute-start | bytes 884744 | tf_op jit(solution)/shard_map/ppermute | solution.py:412
  10.9 9.4 %collective-permute-start = (bf16[192,768]{1,0:T(8,128)(2,1)S(1)}, bf16[192,768]{1,0:T(8,128)(2,1)S(1)}, u32[]{:S(2)}, u32[]{:S(2)}) collective-permute-start(bf16[192,768]{1,0:T(8,128)(2,1)S(1)} %get-tuple-element.57.refs_1_), channel_id=1, source_target_pairs={{0,64},{32,224},{64,128},{96,32},{128,192},{160,96},{192,0},{224,1... | collective-permute-start | bytes 884744 | tf_op jit(solution)/shard_map/ppermute | solution.py:412
  10.9 9.3 %collective-permute-start.3 = (bf16[64,1792]{1,0:T(8,128)(2,1)S(1)}, bf16[64,1792]{1,0:T(8,128)(2,1)S(1)}, u32[]{:S(2)}, u32[]{:S(2)}) collective-permute-start(bf16[64,1792]{1,0:T(8,128)(2,1)S(1)} %get-tuple-element.40), channel_id=1, source_target_pairs={{0,16},{1,17},{2,18},{3,19},{4,20},{5,21},{6,22},{7,23},{8,24},{9,... | collective-permute-start | bytes 688136 | tf_op jit(solution)/shard_map/ppermute | solution.py:417
  20.2 10.8 %collective-permute-start.8 = (bf16[192,768]{1,0:T(8,128)(2,1)S(1)}, bf16[192,768]{1,0:T(8,128)(2,1)S(1)}, u32[]{:S(2)}, u32[]{:S(2)}) collective-permute-start(bf16[192,768]{1,0:T(8,128)(2,1)S(1)} %collective-permute-done.1.refs_3_), channel_id=1, source_target_pairs={{0,32},{32,0},{64,96},{96,64},{128,160},{160,128},{192,224},{224,1... | collective-permute-start | bytes 884744 | tf_op jit(solution)/shard_map/ppermute | solution.py:412
  20.3 10.7 %collective-permute-start.7 = (bf16[192,768]{1,0:T(8,128)(2,1)S(1)}, bf16[192,768]{1,0:T(8,128)(2,1)S(1)}, u32[]{:S(2)}, u32[]{:S(2)}) collective-permute-start(bf16[192,768]{1,0:T(8,128)(2,1)S(1)} %collective-permute-done.refs_2_), channel_id=1, source_target_pairs={{0,32},{32,0},{64,96},{96,64},{128,160},{160,128},{192,224},{224,1... | collective-permute-start | bytes 884744 | tf_op jit(solution)/shard_map/ppermute | solution.py:412
  20.8 10.2 %collective-permute-start.4 = (bf16[192,768]{1,0:T(8,128)(2,1)S(1)}, bf16[192,768]{1,0:T(8,128)(2,1)S(1)}, u32[]{:S(2)}, u32[]{:S(2)}) collective-permute-start(bf16[192,768]{1,0:T(8,128)(2,1)S(1)} %collective-permute-done.refs_2_), channel_id=1, source_target_pairs={{0,64},{32,224},{64,128},{96,32},{128,192},{160,96},{192,0},{224,1... | collective-permute-start | bytes 884744 | tf_op jit(solution)/shard_map/ppermute | solution.py:412
  21.1 8.6 %collective-permute-start.5 = (bf16[64,1792]{1,0:T(8,128)(2,1)}, bf16[64,1792]{1,0:T(8,128)(2,1)S(1)}, u32[]{:S(2)}, u32[]{:S(2)}) collective-permute-start(bf16[64,1792]{1,0:T(8,128)(2,1)} %copy-done.3), channel_id=1, source_target_pairs={{0,8},{1,9},{2,10},{3,11},{4,12},{5,13},{6,14},{7,15},{8,16},{9,17... | collective-permute-start | bytes 688136 | tf_op jit(solution)/shard_map/ppermute | solution.py:417
  22.7 8.3 %collective-permute-start.6 = (bf16[64,1792]{1,0:T(8,128)(2,1)S(1)}, bf16[64,1792]{1,0:T(8,128)(2,1)S(1)}, u32[]{:S(2)}, u32[]{:S(2)}) collective-permute-start(bf16[64,1792]{1,0:T(8,128)(2,1)S(1)} %get-tuple-element.48), channel_id=1, source_target_pairs={{0,24},{1,25},{2,26},{3,27},{4,28},{5,29},{6,30},{7,31},{8,0},{9,1... | collective-permute-start | bytes 688136 | tf_op jit(solution)/shard_map/ppermute | solution.py:417
  31.0 1.7 %collective-permute-start.9 = (bf16[192,768]{1,0:T(8,128)(2,1)S(1)}, bf16[192,768]{1,0:T(8,128)(2,1)S(1)}, u32[]{:S(2)}, u32[]{:S(2)}) collective-permute-start(bf16[192,768]{1,0:T(8,128)(2,1)S(1)} %collective-permute-done.4.refs_4_), channel_id=1, source_target_pairs={{0,32},{32,0},{64,96},{96,64},{128,160},{160,128},{192,224},{224,1... | collective-permute-start | bytes 884744 | tf_op jit(solution)/shard_map/ppermute | solution.py:412
  36.8 23.9 %all-to-all-start = ((bf16[32,8,640]{2,1,0:T(8,128)(2,1)}), bf16[32,8,640]{2,1,0:T(8,128)(2,1)S(1)}, u32[]{:S(2)}, u32[]{:S(2)}) async-start(bf16[32,8,640]{2,1,0:T(8,128)(2,1)} %bitcast.10), calls=%async_computation | async-start | bytes 655360 | tf_op jit(solution)/shard_map/all_to_all | solution.py:488
Sparse Core Ops, SparseCore 0:
  34.8 48.2 all-gather.2

commit v8 on v7

--- a/solution.py
+++ b/solution.py
@@ -348,14 +348,17 @@
 def mix_kernel(values_ref, weights_ref, out_ref, held_ref, sem):
     steps, sources, per, columns = weights_ref.shape
     depth = sources * per
+    spans = [pl.ds(d, 2) for d in range(0, steps, 2)]
     copies = [
-        pltpu.make_async_copy(weights_ref.at[d], held_ref.at[d], sem.at[d]) for d in range(steps)
+        pltpu.make_async_copy(weights_ref.at[span], held_ref.at[span], sem.at[k])
+        for k, span in enumerate(spans)
     ]
     for copy in copies:
         copy.start()
     total = None
     for d in range(steps):
-        copies[d].wait()
+        if d % 2 == 0:
+            copies[d // 2].wait()
         block = held_ref[d].reshape(depth, columns)
         part = jnp.concatenate(
             [values_ref[y, :, d * per : (d + 1) * per] for y in range(sources)], axis=1
@@ -377,7 +380,7 @@
         out_specs=WHOLE,
         scratch_shapes=[
             pltpu.VMEM(weights.shape, BF16),
-            pltpu.SemaphoreType.DMA((steps,)),
+            pltpu.SemaphoreType.DMA((steps // 2,)),
         ],
         compiler_params=params(20),
         name="mix",
@@ -469,9 +472,10 @@
     both, *cuts = prepare(y_scalar, w_qnope, w_qrope, flat)
     ahead, behind, beside = shift_dp(both, 1, 0), shift_dp(both, -1, 0), shift_dp(both, 0, 1)
     cuts[1] = shift_y(cuts[1], 2)
+    own_lengths = lax.dynamic_slice_in_dim(lengths, head * own, own)
     latent, uk = arrange(piece_places(), q_latent, w_uk)
-    ahead, behind, beside, cuts, cos, sin, latent, uk = lax.optimization_barrier(
-        (ahead, behind, beside, cuts, cos, sin, latent, uk)
+    ahead, behind, beside, cuts, cos, sin, latent, uk, own_lengths = lax.optimization_barrier(
+        (ahead, behind, beside, cuts, cos, sin, latent, uk, own_lengths)
     )
     far = shift_dp(ahead, 1, 0)
     ahead_beside, behind_beside = shift_dp(ahead, 0, 1), shift_dp(behind, 0, 1)
@@ -486,7 +490,6 @@
     query = project(latent, pieces, uk, cos, sin)
     query = query.reshape(sources, own * heads, query.shape[1])
     query = lax.all_to_all(query, "head", 0, 0, tiled=True).reshape(rows * heads, -1)
-    own_lengths = lax.dynamic_slice_in_dim(lengths, head * own, own)
     attn = attend(
         own_lengths, page_table, query, heads, new_latent, new_rope, cache_latent, cache_rope
     )

time: 122 us -> 121 us (level)
  blocking collectives: 39.5 us -> 63.2 us
  waiting for transfers between devices: 26.1 us -> 13 us
  starting transfers between devices: 19.7 us -> 8.22 us
    all_to_all x0 -> x1, blocking collectives: none -> 23.8 us  [body(): lax.all_to_all(query, 'head', 0, 0, tiled=True).reshape(rows * heads, -1)]
    all_to_all x1 -> x0, waiting for transfers between devices: 12.4 us -> none  [body(): lax.all_to_all(query, 'head', 0, 0, tiled=True).reshape(rows * heads, -1)]
    all_to_all x1 -> x0, starting transfers between devices: 11.5 us -> none  [body(): lax.all_to_all(query, 'head', 0, 0, tiled=True).reshape(rows * heads, -1)]
  transfers between devices with their start and end apart: 12 -> 11, of which waited for: 5 -> 4; matrix products, arithmetic and copies ran while one was open for 1% -> 2% of each run, Pallas kernels for 12% -> 11%
where the time goes in v8:
time: 121 us
  blocking collectives  63.2 us (52%)
  Pallas kernels  21.2 us (18%)
  between operations  13.5 us (11%)
  waiting for transfers between devices  13 us (11%)
  starting transfers between devices  8.22 us (7%)
    all_to_all x1, blocking collectives, body(): lax.all_to_all(query, 'head', 0, 0, tiled=True).reshape(rows * heads, -1)  23.8 us
    all_to_all x1, blocking collectives, body(): lax.all_to_all(attn, 'head', 0, 0, tiled=True).reshape(rows * heads, -1)  16.8 us
    all_to_all x1, blocking collectives, body(): lax.all_to_all(term, 'head', 0, 0, tiled=True, axis_index_groups=Z_GROUPS)  13.5 us
    ppermute x3, waiting for transfers between devices, shift_y(): return lax.ppermute(x, 'head', pairs)  11.4 us
    all_to_all x1, blocking collectives, body(): lax.all_to_all(values, 'head', 0, 0, tiled=True, axis_index_groups=Y_GROUPS)  9.17 us
    pallas_call x1, Pallas kernels, attend(): pl.pallas_call(kernel, out_shape=jax.ShapeDtypeStruct((rows, width), BF16...  9.04 us
    ppermute x3, starting transfers between devices, shift_y(): return lax.ppermute(x, 'head', pairs)  4.32 us
    ppermute x7, starting transfers between devices, shift_dp(): return lax.ppermute(x, 'dp', pairs)  3.89 us
  transfers between devices with their start and end apart: 11, of which 4 were waited for; matrix products, arithmetic and copies ran while one was open for 2% of the time, Pallas kernels for 11%

profile of v8, /device:TPU:8, one launch (start us, length us, event | category | flops | bytes accessed | tf_op | source)
XLA Modules:
  0.0 121.0 jit_solution(4680951222671099253)
XLA Ops:
  6.5 1.3 %prepare.1 = (bf16[192,768]{1,0:T(8,128)(2,1)S(1)}, bf16[64,1792]{1,0:T(8,128)(2,1)S(1)}, bf16[64,1792]{1,0:T(8,128)(2,1)S(1)}, bf16[64,1792]{1,0:T(8,128)(2,1)S(1)}) custom-call(s32[1]{0:T(128)} %bitcast.y_ref, bf16[192,512]{1,0:T(8,128)(2,1)} %nope_hbm.1, bf16[192,256]{1,0:T(8,128)(2,1)} %rope_hbm.1, bf16[64,7168]{1,0:T(8,128)(2,1)} %bitcast.20), custom_call_target="tpu_custom_call" | custom-call | tf_op jit(solution)/shard_map/prepare/pallas_call | solution.py:57
  7.9 0.1 collective-permute-start.2
  8.0 2.8 %collective-permute-start.1 = (bf16[192,768]{1,0:T(8,128)(2,1)S(1)}, bf16[192,768]{1,0:T(8,128)(2,1)S(1)}, u32[]{:S(2)}, u32[]{:S(2)}) collective-permute-start(bf16[192,768]{1,0:T(8,128)(2,1)S(1)} %get-tuple-element.59.refs_1_), channel_id=1, source_target_pairs={{0,192},{32,96},{64,0},{96,160},{128,64},{160,224},{192,128},{224,... | collective-permute-start | bytes 884744 | tf_op jit(solution)/shard_map/ppermute | solution.py:415
  10.8 0.0 collective-permute-start
  10.8 2.3 %collective-permute-start.3 = (bf16[64,1792]{1,0:T(8,128)(2,1)S(1)}, bf16[64,1792]{1,0:T(8,128)(2,1)S(1)}, u32[]{:S(2)}, u32[]{:S(2)}) collective-permute-start(bf16[64,1792]{1,0:T(8,128)(2,1)S(1)} %get-tuple-element.41), channel_id=1, source_target_pairs={{0,16},{1,17},{2,18},{3,19},{4,20},{5,21},{6,22},{7,23},{8,24},{9,... | collective-permute-start | bytes 688136 | tf_op jit(solution)/shard_map/ppermute | solution.py:420
  13.1 0.1 stack.36
  13.2 0.1 select_reduce_fusion.place_ref
  13.4 0.7 convert_element_type.3
  14.0 0.7 dynamic_slice.3.refs_0_
  14.8 1.7 %arrange.1 = (bf16[8,64,192]{2,1,0:T(8,128)(2,1)S(1)}, bf16[4,128,512]{2,1,0:T(8,128)(2,1)S(1)}) custom-call(s32[8]{0:T(128)S(1)} %select_reduce_fusion.place_ref, bf16[64,1536]{1,0:T(8,128)(2,1)} %latent_hbm.1, bf16[4,128,512]{2,1,0:T(8,128)(2,1)} %uk_hbm.1), custom_call_target="tpu_custom_call" | custom-call | tf_op jit(solution)/shard_map/arrange/pallas_call | solution.py:86
  16.5 0.2 multiply_sine_fusion
  16.7 3.5 %collective-permute-done.3.refs_1_ = bf16[64,1792]{1,0:T(8,128)(2,1)S(1)} collective-permute-done((bf16[64,1792]{1,0:T(8,128)(2,1)S(1)}, bf16[64,1792]{1,0:T(8,128)(2,1)S(1)}, u32[]{:S(2)}, u32[]{:S(2)}) %collective-permute-start.3) | collective-permute-done | bytes 229408 | tf_op jit(solution)/shard_map/ppermute | solution.py:420
  20.2 0.1 collective-permute-start.8
  20.3 0.5 collective-permute-start.7
  20.8 0.3 collective-permute-start.4
  21.1 1.6 %collective-permute-start.5 = (bf16[64,1792]{1,0:T(8,128)(2,1)}, bf16[64,1792]{1,0:T(8,128)(2,1)S(1)}, u32[]{:S(2)}, u32[]{:S(2)}) collective-permute-start(bf16[64,1792]{1,0:T(8,128)(2,1)} %copy-done.3), channel_id=1, source_target_pairs={{0,8},{1,9},{2,10},{3,11},{4,12},{5,13},{6,14},{7,15},{8,16},{9,17... | collective-permute-start | bytes 688136 | tf_op jit(solution)/shard_map/ppermute | solution.py:420
  22.7 0.4 collective-permute-start.6
  23.1 6.5 %collective-permute-done.5.refs_0_ = bf16[64,1792]{1,0:T(8,128)(2,1)S(1)} collective-permute-done((bf16[64,1792]{1,0:T(8,128)(2,1)}, bf16[64,1792]{1,0:T(8,128)(2,1)S(1)}, u32[]{:S(2)}, u32[]{:S(2)}) %collective-permute-start.5) | collective-permute-done | bytes 229408 | tf_op jit(solution)/shard_map/ppermute | solution.py:420
  29.7 1.3 %collective-permute-done.6.refs_2_ = bf16[64,1792]{1,0:T(8,128)(2,1)S(1)} collective-permute-done((bf16[64,1792]{1,0:T(8,128)(2,1)S(1)}, bf16[64,1792]{1,0:T(8,128)(2,1)S(1)}, u32[]{:S(2)}, u32[]{:S(2)}) %collective-permute-start.6) | collective-permute-done | bytes 229408 | tf_op jit(solution)/shard_map/ppermute | solution.py:420
  31.0 0.1 collective-permute-start.9
  31.1 1.6 %collective-permute-done.9.refs_8_ = bf16[192,768]{1,0:T(8,128)(2,1)S(1)} collective-permute-done((bf16[192,768]{1,0:T(8,128)(2,1)S(1)}, bf16[192,768]{1,0:T(8,128)(2,1)S(1)}, u32[]{:S(2)}, u32[]{:S(2)}) %collective-permute-start.9) | collective-permute-done | bytes 294944 | tf_op jit(solution)/shard_map/ppermute | solution.py:415
  32.7 1.9 %stack.37 = bf16[4,64,1792]{2,1,0:T(8,128)(2,1)} custom-call(s32[1]{0:T(128)} %bitcast.y_ref, bf16[64,7168]{1,0:T(8,128)(2,1)} %bitcast.21, bf16[64,1792]{1,0:T(8,128)(2,1)S(1)} %collective-permute-done.5.refs_0_, bf16[64,1792]{1,0:T(8,128)(2,1)S(1)} %collective-permute-done.3.refs_1_, bf16[64,1792]{1,0:T(8,128)(2,1)S(1)} %collective-permute-done.6.refs_2_), custom_call_target="tpu_custom_call" | custom-call | tf_op jit(solution)/shard_map/stack/pallas_call | solution.py:120
  34.6 0.0 all-gather.3.cloned.1.call-update
  34.6 1.4 %project.1 = bf16[256,640]{1,0:T(8,128)(2,1)S(1)} custom-call(bf16[8,64,192]{2,1,0:T(8,128)(2,1)S(1)} %get-tuple-element.46.refs_0_, bf16[192,768]{1,0:T(8,128)(2,1)S(1)} %get-tuple-element.59.refs_1_, bf16[192,768]{1,0:T(8,128)(2,1)S(1)} %collective-permute-done.refs_2_, bf16[192,768]{1,0:T(8,128)(2,1)S(1)} %collective-permute-done.1.refs_3_, ...), custom_call_target="tpu_custom_call" | custom-call | tf_op jit(solution)/shard_map/project/pallas_call | solution.py:185
  36.0 23.8 %all_to_all.20 = bf16[32,8,640]{2,1,0:T(8,128)(2,1)S(1)} all-to-all(bf16[32,8,640]{2,1,0:T(8,128)(2,1)S(1)} %bitcast.16), channel_id=1, replica_groups=mesh['dp'=8,'head'=32] {'head'}, dimensions={0} | all-to-all | bytes 655360 | tf_op jit(solution)/shard_map/all_to_all | solution.py:492
  59.8 9.0 %attend.1 = bf16[256,512]{1,0:T(8,128)(2,1)S(1)} custom-call(s32[2]{0:T(128)S(1)} %dynamic_slice.3.refs_0_, s32[2,32]{1,0:T(2,128)S(1)} %copy-done.1, bf16[256,640]{1,0:T(8,128)(2,1)S(1)} %bitcast.15, bf16[2,512]{1,0:T(2,128)(2,1)S(1)} %copy-done, bf16[2,64]{1,0:T(2,128)(2,1)S(1)} %copy-done.2, bf16[64,128,512]{2,1,0:T(8,128)(2,1)} %refs_5_.1, ...), custom_call_target="tpu_custom_call" | custom-call | tf_op jit(solution)/shard_map/attend/pallas_call | solution.py:287
  68.8 16.8 %all_to_all.21 = bf16[32,8,512]{2,1,0:T(8,128)(2,1)S(1)} all-to-all(bf16[32,8,512]{2,1,0:T(8,128)(2,1)S(1)} %bitcast.17), channel_id=1, replica_groups=mesh['dp'=8,'head'=32] {'head'}, dimensions={0} | all-to-all | bytes 524288 | tf_op jit(solution)/shard_map/all_to_all | solution.py:497
  85.6 1.4 %values.1 = bf16[64,512]{1,0:T(8,128)(2,1)S(1)} custom-call(bf16[256,512]{1,0:T(8,128)(2,1)S(1)} %bitcast.18, bf16[4,512,128]{2,1,0:T(8,128)(2,1)} %refs_1_.3), custom_call_target="tpu_custom_call" | custom-call | tf_op jit(solution)/shard_map/values/pallas_call | solution.py:337
  87.0 9.2 %all_to_all.22.values_ref = bf16[4,64,512]{2,1,0:T(8,128)(2,1)S(1)} all-to-all(bf16[4,64,512]{2,1,0:T(8,128)(2,1)S(1)} %broadcast_in_dim.16), channel_id=1, replica_groups={{0,8,16,24},{1,9,17,25},{2,10,18,26},{3,11,19,27},{4,12,20,28},{5,13,21..., dimensions={0} | all-to-all | bytes 524288 | tf_op jit(solution)/shard_map/all_to_all | solution.py:500
  96.2 3.8 %mix.1 = bf16[8,64,224]{2,1,0:T(8,128)(2,1)S(1)} custom-call(bf16[4,64,512]{2,1,0:T(8,128)(2,1)S(1)} %all_to_all.22.values_ref, bf16[8,4,64,1792]{3,2,1,0:T(8,128)(2,1)} %bitcast.19), custom_call_target="tpu_custom_call" | custom-call | tf_op jit(solution)/shard_map/mix/pallas_call | solution.py:376
  100.0 13.5 %all_to_all.23.terms_ref = bf16[8,64,224]{2,1,0:T(8,128)(2,1)S(1)} all-to-all(bf16[8,64,224]{2,1,0:T(8,128)(2,1)S(1)} %mix.1), channel_id=1, replica_groups={{0,1,2,3,4,5,6,7},{8,9,10,11,12,13,14,15},{16,17,18,19,20,21,22,23},{24..., dimensions={0} | all-to-all | bytes 458752 | tf_op jit(solution)/shard_map/all_to_all | solution.py:502
  113.5 0.7 finish.1
  (18 shorter events, 0.1 us)
Async XLA Ops:
  6.5 53.2 %copy-start.1 = (s32[2,32]{1,0:T(2,128)S(1)}, s32[2,32]{1,0:T(2,128)}, u32[]{:S(2)}) copy-start(s32[2,32]{1,0:T(2,128)} %refs_1_.2) | copy-start | bytes 772
  6.5 53.2 %copy-start.2 = (bf16[2,64]{1,0:T(2,128)(2,1)S(1)}, bf16[2,64]{1,0:T(2,128)(2,1)}, u32[]{:S(2)}) copy-start(bf16[2,64]{1,0:T(2,128)(2,1)} %refs_4_.1) | copy-start | bytes 772
  6.5 53.2 %copy-start = (bf16[2,512]{1,0:T(2,128)(2,1)S(1)}, bf16[2,512]{1,0:T(2,128)(2,1)}, u32[]{:S(2)}) copy-start(bf16[2,512]{1,0:T(2,128)(2,1)} %refs_3_.1) | copy-start | bytes 6148
  6.5 89.7 %all-gather.3.cloned.1.call-start = ((), (), s32[]{:S(2)}) async-start(), calls=%async_computation.4 | async-start | bytes 8257536 | tf_op jit(solution)/shard_map/all_gather | solution.py:489
  7.9 3.0 %copy-start.3 = (bf16[64,1792]{1,0:T(8,128)(2,1)}, bf16[64,1792]{1,0:T(8,128)(2,1)S(1)}, u32[]{:S(2)}) copy-start(bf16[64,1792]{1,0:T(8,128)(2,1)S(1)} %get-tuple-element.48) | copy-start | bytes 688132
  7.9 12.3 %collective-permute-start.2 = (bf16[192,768]{1,0:T(8,128)(2,1)S(1)}, bf16[192,768]{1,0:T(8,128)(2,1)S(1)}, u32[]{:S(2)}, u32[]{:S(2)}) collective-permute-start(bf16[192,768]{1,0:T(8,128)(2,1)S(1)} %get-tuple-element.59.refs_1_), channel_id=1, source_target_pairs={{0,32},{32,0},{64,96},{96,64},{128,160},{160,128},{192,224},{224,1... | collective-permute-start | bytes 884744 | tf_op jit(solution)/shard_map/ppermute | solution.py:415
  8.0 12.2 %collective-permute-start.1 = (bf16[192,768]{1,0:T(8,128)(2,1)S(1)}, bf16[192,768]{1,0:T(8,128)(2,1)S(1)}, u32[]{:S(2)}, u32[]{:S(2)}) collective-permute-start(bf16[192,768]{1,0:T(8,128)(2,1)S(1)} %get-tuple-element.59.refs_1_), channel_id=1, source_target_pairs={{0,192},{32,96},{64,0},{96,160},{128,64},{160,224},{192,128},{224,... | collective-permute-start | bytes 884744 | tf_op jit(solution)/shard_map/ppermute | solution.py:415
  10.8 9.4 %collective-permute-start = (bf16[192,768]{1,0:T(8,128)(2,1)S(1)}, bf16[192,768]{1,0:T(8,128)(2,1)S(1)}, u32[]{:S(2)}, u32[]{:S(2)}) collective-permute-start(bf16[192,768]{1,0:T(8,128)(2,1)S(1)} %get-tuple-element.59.refs_1_), channel_id=1, source_target_pairs={{0,64},{32,224},{64,128},{96,32},{128,192},{160,96},{192,0},{224,1... | collective-permute-start | bytes 884744 | tf_op jit(solution)/shard_map/ppermute | solution.py:415
  10.8 9.3 %collective-permute-start.3 = (bf16[64,1792]{1,0:T(8,128)(2,1)S(1)}, bf16[64,1792]{1,0:T(8,128)(2,1)S(1)}, u32[]{:S(2)}, u32[]{:S(2)}) collective-permute-start(bf16[64,1792]{1,0:T(8,128)(2,1)S(1)} %get-tuple-element.41), channel_id=1, source_target_pairs={{0,16},{1,17},{2,18},{3,19},{4,20},{5,21},{6,22},{7,23},{8,24},{9,... | collective-permute-start | bytes 688136 | tf_op jit(solution)/shard_map/ppermute | solution.py:420
  20.2 10.8 %collective-permute-start.8 = (bf16[192,768]{1,0:T(8,128)(2,1)S(1)}, bf16[192,768]{1,0:T(8,128)(2,1)S(1)}, u32[]{:S(2)}, u32[]{:S(2)}) collective-permute-start(bf16[192,768]{1,0:T(8,128)(2,1)S(1)} %collective-permute-done.1.refs_3_), channel_id=1, source_target_pairs={{0,32},{32,0},{64,96},{96,64},{128,160},{160,128},{192,224},{224,1... | collective-permute-start | bytes 884744 | tf_op jit(solution)/shard_map/ppermute | solution.py:415
  20.3 10.7 %collective-permute-start.7 = (bf16[192,768]{1,0:T(8,128)(2,1)S(1)}, bf16[192,768]{1,0:T(8,128)(2,1)S(1)}, u32[]{:S(2)}, u32[]{:S(2)}) collective-permute-start(bf16[192,768]{1,0:T(8,128)(2,1)S(1)} %collective-permute-done.refs_2_), channel_id=1, source_target_pairs={{0,32},{32,0},{64,96},{96,64},{128,160},{160,128},{192,224},{224,1... | collective-permute-start | bytes 884744 | tf_op jit(solution)/shard_map/ppermute | solution.py:415
  20.8 10.2 %collective-permute-start.4 = (bf16[192,768]{1,0:T(8,128)(2,1)S(1)}, bf16[192,768]{1,0:T(8,128)(2,1)S(1)}, u32[]{:S(2)}, u32[]{:S(2)}) collective-permute-start(bf16[192,768]{1,0:T(8,128)(2,1)S(1)} %collective-permute-done.refs_2_), channel_id=1, source_target_pairs={{0,64},{32,224},{64,128},{96,32},{128,192},{160,96},{192,0},{224,1... | collective-permute-start | bytes 884744 | tf_op jit(solution)/shard_map/ppermute | solution.py:415
  21.1 8.6 %collective-permute-start.5 = (bf16[64,1792]{1,0:T(8,128)(2,1)}, bf16[64,1792]{1,0:T(8,128)(2,1)S(1)}, u32[]{:S(2)}, u32[]{:S(2)}) collective-permute-start(bf16[64,1792]{1,0:T(8,128)(2,1)} %copy-done.3), channel_id=1, source_target_pairs={{0,8},{1,9},{2,10},{3,11},{4,12},{5,13},{6,14},{7,15},{8,16},{9,17... | collective-permute-start | bytes 688136 | tf_op jit(solution)/shard_map/ppermute | solution.py:420
  22.7 8.3 %collective-permute-start.6 = (bf16[64,1792]{1,0:T(8,128)(2,1)S(1)}, bf16[64,1792]{1,0:T(8,128)(2,1)S(1)}, u32[]{:S(2)}, u32[]{:S(2)}) collective-permute-start(bf16[64,1792]{1,0:T(8,128)(2,1)S(1)} %get-tuple-element.50), channel_id=1, source_target_pairs={{0,24},{1,25},{2,26},{3,27},{4,28},{5,29},{6,30},{7,31},{8,0},{9,1... | collective-permute-start | bytes 688136 | tf_op jit(solution)/shard_map/ppermute | solution.py:420
  31.0 1.7 %collective-permute-start.9 = (bf16[192,768]{1,0:T(8,128)(2,1)S(1)}, bf16[192,768]{1,0:T(8,128)(2,1)S(1)}, u32[]{:S(2)}, u32[]{:S(2)}) collective-permute-start(bf16[192,768]{1,0:T(8,128)(2,1)S(1)} %collective-permute-done.4.refs_4_), channel_id=1, source_target_pairs={{0,32},{32,0},{64,96},{96,64},{128,160},{160,128},{192,224},{224,1... | collective-permute-start | bytes 884744 | tf_op jit(solution)/shard_map/ppermute | solution.py:415
Sparse Core Ops, SparseCore 0:
  34.7 48.2 all-gather.2
